TPU v7x, 32 devices: a whole 2x2x4 slice. The times are simulated.
32 devices in a mesh: shard: 4 (over x, core), rep: 8 (over z, y).
Axes of the slice: x: 2, y: 2, z: 4, core: 2. Of those that a mesh axis runs over, the one named last changes fastest.
Arguments:
- tokens: bfloat16 [8, 1024, 1024], P('rep', 'shard'), may hold values from -6 to 6
- segments: int32 [8, 1024], P('rep', 'shard'), may hold values from 0 to 2, as said below
- grad_out: bfloat16 [8, 1024, 1024], P('rep', 'shard'), may hold values from -6 to 6
- attention_gain: bfloat16 [1024], P('shard'), may hold values from 0.25 to 1.75
- query_weight: bfloat16 [1024, 2048], P('shard'), may hold values from -0.1875 to 0.1875
- key_matrix: bfloat16 [1024, 1024], P('shard'), may hold values from -0.1875 to 0.1875
- value_matrix: bfloat16 [1024, 1024], P('shard'), may hold values from -0.1875 to 0.1875
- query_gain: bfloat16 [128], P('shard'), may hold values from 0.25 to 1.75
- key_gain: bfloat16 [128], P('shard'), may hold values from 0.25 to 1.75
- output_weight: bfloat16 [2048, 1024], P(None, 'shard'), may hold values from -1.5 to 1.5
- mlp_gain: bfloat16 [1024], P('shard'), may hold values from 0.25 to 1.75
- gate_weight: bfloat16 [1024, 3072], P('shard'), may hold values from -0.1875 to 0.1875
- up_weight: bfloat16 [1024, 3072], P('shard'), may hold values from -0.1875 to 0.1875
- down_weight: bfloat16 [3072, 1024], P('shard'), may hold values from -0.109375 to 0.109375
Outputs:
- layer_out: bfloat16 [8, 1024, 1024], P('rep', 'shard')
- grad_tokens: float32 [8, 1024, 1024], P('rep', 'shard')
- grad_attention_gain: float32 [1024], P('shard')
- grad_query_weight: float32 [1024, 2048], P('shard')
- grad_key_weight: float32 [1024, 1024], P('shard')
- grad_value_weight: float32 [1024, 1024], P('shard')
- grad_query_gain: float32 [128], P('shard')
- grad_key_gain: float32 [128], P('shard')
- grad_output_weight: float32 [2048, 1024], P(None, 'shard')
- grad_mlp_gain: float32 [1024], P('shard')
- grad_gate_weight: float32 [1024, 3072], P('shard')
- grad_up_weight: float32 [1024, 3072], P('shard')
- grad_down_weight: float32 [3072, 1024], P('shard')
Inputs may be any that keep to these rules, and one draw needn't show every extreme that they name: `segments`: in each sequence the ids are 0, 1 and 2 in this order, never falling, each present; document 1 begins within the first 256 tokens of the sequence and ends within its last 256 tokens.
All inputs are finite; a program needn't handle non-finite values.
Results may differ from a plain program's by a relative error of at most 0.019.
Values may be sent and summed in bfloat16 or wider, within the bound.
No kernel may reach another device: no remote copies, remote signals or barrier semaphores. Data moves between devices by JAX's collectives and lax.ppermute only.
A program may use at most 192 MiB of HBM per device.

v0:
```python
import jax
import jax.numpy as jnp
from jax import lax
from jax.sharding import PartitionSpec as P

eps_norm = 1e-06
theta_base = 1000000.0
masked_score = -1e30


def inverse_root(value_rows):
    return lax.rsqrt(jnp.mean(value_rows * value_rows, axis=-1, keepdims=True) + eps_norm)


def turned(value_rows):
    half = value_rows.shape[-1] // 2
    return jnp.concatenate([-value_rows[..., half:], value_rows[..., :half]], axis=-1)


def rotate(value_rows, cosine, sine):
    return value_rows * cosine + turned(value_rows) * sine


def norm_back(grad, value_rows, scale):
    return scale * grad - value_rows * scale * scale * scale * jnp.mean(
        grad * value_rows, axis=-1, keepdims=True
    )


def tables(position, head_dim):
    freqs = theta_base ** (-(jnp.arange(head_dim // 2, dtype=jnp.float32) * 2.0) / head_dim)
    angles = position.astype(jnp.float32)[..., None] * freqs
    angles = jnp.concatenate([angles, angles], axis=-1)
    return (jnp.cos(angles), jnp.sin(angles))


def product(left, right):
    return jnp.dot(left, right, preferred_element_type=jnp.float32)


def per_device(
    tokens,
    segments,
    grad_out,
    attention_gain,
    query_weight,
    key_matrix,
    value_matrix,
    query_gain,
    key_gain,
    output_weight,
    mlp_gain,
    gate_weight,
    up_weight,
    down_weight,
):
    rows = tokens.shape[1]
    shards = lax.axis_size("shard")
    mine = lax.axis_index("shard")
    head_dim = query_gain.shape[0] * shards
    key_heads = key_matrix.shape[1] // head_dim
    query_heads = query_weight.shape[1] // head_dim
    head_group = query_heads // key_heads
    scale = head_dim ** (-0.5)
    inputs = tokens[0].astype(jnp.float32)
    cotangent = grad_out[0]
    own_segments = segments[0]
    all_segments = lax.all_gather(own_segments, "shard", axis=0, tiled=True)
    opening = jnp.sum((all_segments[None, :] < own_segments[:, None]).astype(jnp.int32), axis=1)
    places = mine * rows + jnp.arange(rows, dtype=jnp.int32)
    cosine, sine = tables(places - opening, head_dim)
    cosine = cosine[:, None, :]
    sine = sine[:, None, :]
    (
        full_input_gain,
        full_query,
        full_key,
        full_value,
        full_query_gain,
        full_key_gain,
        full_output,
    ) = (
        lax.all_gather(attention_gain, "shard", axis=0, tiled=True),
        lax.all_gather(query_weight, "shard", axis=0, tiled=True),
        lax.all_gather(key_matrix, "shard", axis=0, tiled=True),
        lax.all_gather(value_matrix, "shard", axis=0, tiled=True),
        lax.all_gather(query_gain, "shard", axis=0, tiled=True),
        lax.all_gather(key_gain, "shard", axis=0, tiled=True),
        lax.all_gather(output_weight, "shard", axis=1, tiled=True),
    )
    input_gain_f = full_input_gain.astype(jnp.float32)
    query_gain_f = full_query_gain.astype(jnp.float32)
    key_gain_f = full_key_gain.astype(jnp.float32)
    input_scale = inverse_root(inputs)
    first_normalized = (inputs * input_scale * input_gain_f).astype(jnp.bfloat16)
    query_lin = product(first_normalized, full_query).reshape(rows, query_heads, head_dim)
    key_linear = product(first_normalized, full_key).reshape(rows, key_heads, head_dim)
    value_low = product(first_normalized, full_value).astype(jnp.bfloat16)
    query_scale = inverse_root(query_lin)
    key_scale = inverse_root(key_linear)
    query_rotary = rotate(query_lin * query_scale * query_gain_f, cosine, sine).astype(jnp.bfloat16)
    key_rot = rotate(key_linear * key_scale * key_gain_f, cosine, sine).astype(jnp.bfloat16)
    all_keys, all_values = (
        lax.all_gather(key_rot.reshape(rows, key_heads * head_dim), "shard", axis=0, tiled=True),
        lax.all_gather(value_low, "shard", axis=0, tiled=True),
    )
    grouped_query = query_rotary.reshape(rows, key_heads, head_group, head_dim)

    def block_scores(index):
        begin = index * rows
        key_block = lax.dynamic_slice_in_dim(all_keys, begin, rows, 0).reshape(
            rows, key_heads, head_dim
        )
        value_block = lax.dynamic_slice_in_dim(all_values, begin, rows, 0).reshape(
            rows, key_heads, head_dim
        )
        block_segments = lax.dynamic_slice_in_dim(all_segments, begin, rows, 0)
        key_places = begin + jnp.arange(rows, dtype=jnp.int32)
        allowed = (own_segments[:, None] == block_segments[None, :]) & (
            places[:, None] >= key_places[None, :]
        )
        raw = jnp.einsum(
            "rgpd,sgd->gprs", grouped_query, key_block, preferred_element_type=jnp.float32
        )
        scores = jnp.where(allowed, raw * scale, masked_score)
        return (scores, key_block, value_block)

    def peak_step(index, carry):
        peak, total = carry
        scores = block_scores(index)[0]
        fresh = jnp.maximum(peak, jnp.max(scores, axis=-1))
        total = total * jnp.exp(peak - fresh) + jnp.sum(jnp.exp(scores - fresh[..., None]), axis=-1)
        return (fresh, total)

    start_peak = jnp.full((key_heads, head_group, rows), masked_score, jnp.float32)
    start_total = jnp.zeros((key_heads, head_group, rows), jnp.float32)
    peak, total = lax.fori_loop(0, mine + 1, peak_step, (start_peak, start_total))
    log_total = peak + jnp.log(total)

    def value_step(index, carry):
        scores, key_block, value_block = block_scores(index)
        probs_low = jnp.exp(scores - log_total[..., None]).astype(jnp.bfloat16)
        return carry + jnp.einsum(
            "gprs,sgd->rgpd", probs_low, value_block, preferred_element_type=jnp.float32
        )

    attended = lax.fori_loop(
        0, mine + 1, value_step, jnp.zeros((rows, key_heads, head_group, head_dim), jnp.float32)
    )
    attended_low = attended.reshape(rows, query_heads * head_dim).astype(jnp.bfloat16)
    residual_one = inputs + product(attended_low, full_output)
    full_mlp_gain, full_gate, full_up, full_down = (
        lax.all_gather(mlp_gain, "shard", axis=0, tiled=True),
        lax.all_gather(gate_weight, "shard", axis=0, tiled=True),
        lax.all_gather(up_weight, "shard", axis=0, tiled=True),
        lax.all_gather(down_weight, "shard", axis=0, tiled=True),
    )
    mlp_gain_f = full_mlp_gain.astype(jnp.float32)
    residual_scale = inverse_root(residual_one)
    normed_two = (residual_one * residual_scale * mlp_gain_f).astype(jnp.bfloat16)
    gate = product(normed_two, full_gate)
    upper = product(normed_two, full_up)
    sigma = jax.nn.sigmoid(gate)
    hidden_low = (gate * sigma * upper).astype(jnp.bfloat16)
    layer_out = (residual_one + product(hidden_low, full_down)).astype(jnp.bfloat16)
    hidden_grad = product(cotangent, full_down.T)
    gate_grad = (hidden_grad * upper * sigma * (1.0 + gate * (1.0 - sigma))).astype(jnp.bfloat16)
    up_grad = (hidden_grad * gate * sigma).astype(jnp.bfloat16)
    normed_grad_two = product(gate_grad, full_gate.T) + product(up_grad, full_up.T)
    grad_mlp_gain = jnp.sum(normed_grad_two * residual_one * residual_scale, axis=0)
    residual_grad = cotangent.astype(jnp.float32) + norm_back(
        normed_grad_two * mlp_gain_f, residual_one, residual_scale
    )
    branch_grad = residual_grad.astype(jnp.bfloat16)
    out_grad = (
        product(branch_grad, full_output.T)
        .astype(jnp.bfloat16)
        .reshape(rows, key_heads, head_group, head_dim)
    )
    delta = jnp.transpose(jnp.sum(out_grad.astype(jnp.float32) * attended, axis=-1), (1, 2, 0))

    def query_step(index, query_grad):
        scores, key_block, value_block = block_scores(index)
        probs = jnp.exp(scores - log_total[..., None])
        prob_grad = jnp.einsum(
            "rgpd,sgd->gprs", out_grad, value_block, preferred_element_type=jnp.float32
        )
        score_grad = (probs * (prob_grad - delta[..., None]) * scale).astype(jnp.bfloat16)
        return query_grad + jnp.einsum(
            "gprs,sgd->rgpd", score_grad, key_block, preferred_element_type=jnp.float32
        )

    query_grad = lax.fori_loop(
        0, mine + 1, query_step, jnp.zeros((rows, key_heads, head_group, head_dim), jnp.float32)
    )
    every_query, every_out = (
        lax.all_gather(
            query_rotary.reshape(rows, query_heads * head_dim), "shard", axis=0, tiled=True
        ),
        lax.all_gather(out_grad.reshape(rows, query_heads * head_dim), "shard", axis=0, tiled=True),
    )
    every_log, every_delta = (
        lax.all_gather(log_total, "shard", axis=2, tiled=True),
        lax.all_gather(delta, "shard", axis=2, tiled=True),
    )
    own_values = value_low.reshape(rows, key_heads, head_dim)

    def key_step(index, carry):
        key_total, value_total = carry
        begin = index * rows
        query_block = lax.dynamic_slice_in_dim(every_query, begin, rows, 0).reshape(
            rows, key_heads, head_group, head_dim
        )
        out_block = lax.dynamic_slice_in_dim(every_out, begin, rows, 0).reshape(
            rows, key_heads, head_group, head_dim
        )
        log_block = lax.dynamic_slice_in_dim(every_log, begin, rows, 2)
        delta_block = lax.dynamic_slice_in_dim(every_delta, begin, rows, 2)
        query_segments = lax.dynamic_slice_in_dim(all_segments, begin, rows, 0)
        query_places = begin + jnp.arange(rows, dtype=jnp.int32)
        allowed = (query_segments[:, None] == own_segments[None, :]) & (
            query_places[:, None] >= places[None, :]
        )
        raw = jnp.einsum("rgpd,sgd->gprs", query_block, key_rot, preferred_element_type=jnp.float32)
        scores = jnp.where(allowed, raw * scale, masked_score)
        probs = jnp.exp(scores - log_block[..., None])
        prob_grad = jnp.einsum(
            "rgpd,sgd->gprs", out_block, own_values, preferred_element_type=jnp.float32
        )
        score_grad = (probs * (prob_grad - delta_block[..., None]) * scale).astype(jnp.bfloat16)
        key_total = key_total + jnp.einsum(
            "gprs,rgpd->sgd", score_grad, query_block, preferred_element_type=jnp.float32
        )
        value_total = value_total + jnp.einsum(
            "gprs,rgpd->sgd",
            probs.astype(jnp.bfloat16),
            out_block,
            preferred_element_type=jnp.float32,
        )
        return (key_total, value_total)

    start_keys = (
        jnp.zeros((rows, key_heads, head_dim), jnp.float32),
        jnp.zeros((rows, key_heads, head_dim), jnp.float32),
    )
    key_total, value_total = lax.fori_loop(mine, shards, key_step, start_keys)
    own_key_grad = key_total.reshape(rows, key_heads * head_dim)
    own_value_grad = value_total.reshape(rows, key_heads * head_dim)
    query_normed_grad = rotate(query_grad.reshape(rows, query_heads, head_dim), cosine, -sine)
    key_normed_grad = rotate(own_key_grad.reshape(rows, key_heads, head_dim), cosine, -sine)
    grad_query_gain = jnp.sum(query_normed_grad * query_lin * query_scale, axis=(0, 1))
    grad_key_gain = jnp.sum(key_normed_grad * key_linear * key_scale, axis=(0, 1))
    query_lin_grad = (
        norm_back(query_normed_grad * query_gain_f, query_lin, query_scale)
        .reshape(rows, query_heads * head_dim)
        .astype(jnp.bfloat16)
    )
    key_lin_grad = (
        norm_back(key_normed_grad * key_gain_f, key_linear, key_scale)
        .reshape(rows, key_heads * head_dim)
        .astype(jnp.bfloat16)
    )
    value_lin_grad = own_value_grad.astype(jnp.bfloat16)
    normed_grad_one = (
        product(query_lin_grad, full_query.T)
        + product(key_lin_grad, full_key.T)
        + product(value_lin_grad, full_value.T)
    )
    grad_attention_gain = jnp.sum(normed_grad_one * inputs * input_scale, axis=0)
    grad_tokens = residual_grad + norm_back(normed_grad_one * input_gain_f, inputs, input_scale)
    columns_two, columns_hidden = (
        lax.all_to_all(normed_two, "shard", split_axis=1, concat_axis=0, tiled=True),
        lax.all_to_all(hidden_low, "shard", split_axis=1, concat_axis=0, tiled=True),
    )
    every_gate, every_up, every_cotangent = (
        lax.all_gather(gate_grad, "shard", axis=0, tiled=True),
        lax.all_gather(up_grad, "shard", axis=0, tiled=True),
        lax.all_gather(cotangent, "shard", axis=0, tiled=True),
    )
    share_gate = product(columns_two.T, every_gate)
    share_up = product(columns_two.T, every_up)
    share_down = product(columns_hidden.T, every_cotangent)
    columns_one, columns_branch = (
        lax.all_to_all(first_normalized, "shard", split_axis=1, concat_axis=0, tiled=True),
        lax.all_to_all(branch_grad, "shard", split_axis=1, concat_axis=0, tiled=True),
    )
    every_query_grad, every_attended, every_key_grad, every_value_grad = (
        lax.all_gather(query_lin_grad, "shard", axis=0, tiled=True),
        lax.all_gather(attended_low, "shard", axis=0, tiled=True),
        lax.all_gather(key_lin_grad, "shard", axis=0, tiled=True),
        lax.all_gather(value_lin_grad, "shard", axis=0, tiled=True),
    )
    share_query = product(columns_one.T, every_query_grad)
    share_key = product(columns_one.T, every_key_grad)
    share_value = product(columns_one.T, every_value_grad)
    share_output = product(every_attended.T, columns_branch)
    share_input_gain, share_query_gain, share_key_gain, share_mlp_gain = (
        lax.psum_scatter(grad_attention_gain, "shard", scatter_dimension=0, tiled=True),
        lax.psum_scatter(grad_query_gain, "shard", scatter_dimension=0, tiled=True),
        lax.psum_scatter(grad_key_gain, "shard", scatter_dimension=0, tiled=True),
        lax.psum_scatter(grad_mlp_gain, "shard", scatter_dimension=0, tiled=True),
    )
    summed = (
        lax.psum(share_input_gain.astype(jnp.bfloat16), "rep").astype(jnp.float32),
        lax.psum(share_query.astype(jnp.bfloat16), "rep").astype(jnp.float32),
        lax.psum(share_key.astype(jnp.bfloat16), "rep").astype(jnp.float32),
        lax.psum(share_value.astype(jnp.bfloat16), "rep").astype(jnp.float32),
        lax.psum(share_query_gain.astype(jnp.bfloat16), "rep").astype(jnp.float32),
        lax.psum(share_key_gain.astype(jnp.bfloat16), "rep").astype(jnp.float32),
        lax.psum(share_output.astype(jnp.bfloat16), "rep").astype(jnp.float32),
        lax.psum(share_mlp_gain.astype(jnp.bfloat16), "rep").astype(jnp.float32),
        lax.psum(share_gate.astype(jnp.bfloat16), "rep").astype(jnp.float32),
        lax.psum(share_up.astype(jnp.bfloat16), "rep").astype(jnp.float32),
        lax.psum(share_down.astype(jnp.bfloat16), "rep").astype(jnp.float32),
    )
    return (
        layer_out[None],
        grad_tokens[None],
        summed[0],
        summed[1],
        summed[2],
        summed[3],
        summed[4],
        summed[5],
        summed[6],
        summed[7],
        summed[8],
        summed[9],
        summed[10],
    )


def solution(mesh):
    return jax.shard_map(
        per_device,
        mesh=mesh,
        in_specs=(
            P("rep", "shard", None),
            P("rep", "shard"),
            P("rep", "shard", None),
            P("shard"),
            P("shard", None),
            P("shard", None),
            P("shard", None),
            P("shard"),
            P("shard"),
            P(None, "shard"),
            P("shard"),
            P("shard", None),
            P("shard", None),
            P("shard", None),
        ),
        out_specs=(
            P("rep", "shard", None),
            P("rep", "shard", None),
            P("shard"),
            P("shard", None),
            P("shard", None),
            P("shard", None),
            P("shard"),
            P("shard"),
            P(None, "shard"),
            P("shard"),
            P("shard", None),
            P("shard", None),
            P("shard", None),
        ),
        check_vma=False,
    )
```

profile of v0, /device:TPU:0, one launch (start us, length us, event | category | flops | bytes accessed | tf_op | source)
XLA Modules:
  0.0 945.5 jit_solution(18126087254378977514)
XLA Ops:
  9.5 6.0 all-gather.2
  17.3 8.0 all-reduce.9
  41.0 18.4 %all-gather.23.cloned.1.call-done = bf16[1024,1024]{1,0:T(8,128)(2,1)} async-done(((bf16[256,1024]{1,0:T(8,128)(2,1)}), bf16[1024,1024]{1,0:T(8,128)(2,1)}) %all-gather.23.cloned.1.call-update) | async-done | bytes 2097168 | tf_op jit(solution)/shard_map/all_gather | solution.py:86
  70.5 24.9 %all-gather.31.cloned.1.call-done = bf16[1024,2048]{1,0:T(8,128)(2,1)} async-done(((bf16[256,2048]{1,0:T(8,128)(2,1)}), bf16[1024,2048]{1,0:T(8,128)(2,1)}) %all-gather.31.cloned.1.call-update) | async-done | bytes 4194320 | tf_op jit(solution)/shard_map/all_gather | solution.py:84
  95.5 6.4 copy.145
  108.4 11.4 %all-gather.29.cloned.1.call-done = bf16[1024,1024]{0,1:T(8,128)(2,1)} async-done(((bf16[256,1024]{0,1:T(8,128)(2,1)}), bf16[1024,1024]{0,1:T(8,128)(2,1)}) %all-gather.29.cloned.1.call-update) | async-done | bytes 2097168 | tf_op jit(solution)/shard_map/all_gather | solution.py:104
  123.0 10.4 %all-gather.43.cloned.1.call-start = ((), (), s32[]{:S(2)}) async-start(), calls=%async_computation.14 | async-start | bytes 5242880 | tf_op jit(solution)/shard_map/all_gather | solution.py:200
  133.4 10.9 %all-gather.25.cloned.1.call-done = bf16[1024,1024]{1,0:T(8,128)(2,1)} async-done(((bf16[256,1024]{1,0:T(8,128)(2,1)}), bf16[1024,1024]{1,0:T(8,128)(2,1)}) %all-gather.25.cloned.1.call-update) | async-done | bytes 2097168 | tf_op jit(solution)/shard_map/all_gather | solution.py:105
  155.2 25.6 %all-gather.33.cloned.1.call-done = bf16[2048,1024]{1,0:T(8,128)(2,1)} async-done(((bf16[2048,256]{1,0:T(8,128)(2,1)}), bf16[2048,1024]{1,0:T(8,128)(2,1)}) %all-gather.33.cloned.1.call-update) | async-done | bytes 4194320 | tf_op jit(solution)/shard_map/all_gather | solution.py:89
  186.7 42.1 %all-gather.35.cloned.1.call-done = bf16[1024,3072]{1,0:T(8,128)(2,1)} async-done(((bf16[256,3072]{1,0:T(8,128)(2,1)}), bf16[1024,3072]{1,0:T(8,128)(2,1)}) %all-gather.35.cloned.1.call-update) | async-done | bytes 6291472 | tf_op jit(solution)/shard_map/all_gather | solution.py:154
  228.8 6.4 fusion.97
  235.2 41.5 %all-gather.37.cloned.1.call-done = bf16[1024,3072]{1,0:T(8,128)(2,1)} async-done(((bf16[256,3072]{1,0:T(8,128)(2,1)}), bf16[1024,3072]{1,0:T(8,128)(2,1)}) %all-gather.37.cloned.1.call-update) | async-done | bytes 6291472 | tf_op jit(solution)/shard_map/all_gather | solution.py:155
  276.8 6.4 fusion.98
  283.2 41.6 %all-gather.39.cloned.1.call-done = bf16[3072,1024]{1,0:T(8,128)(2,1)} async-done(((bf16[768,1024]{1,0:T(8,128)(2,1)}), bf16[3072,1024]{1,0:T(8,128)(2,1)}) %all-gather.39.cloned.1.call-update) | async-done | bytes 6291472 | tf_op jit(solution)/shard_map/all_gather | solution.py:156
  324.7 9.9 %multiply_convert_fusion = (bf16[256,3072]{1,0:T(8,128)(2,1)}, bf16[256,3072]{1,0:T(8,128)(2,1)}, bf16[256,3072]{1,0:T(8,128)(2,1)}) fusion(f32[256,3072]{1,0:T(8,128)} %fusion.97, f32[256,3072]{1,0:T(8,128)} %fusion.98, bf16[3072,1024]{1,0:T(8,128)(2,1)} %all-gather.39.cloned.1.call-done, bf16[1,256,1024]{2,1,0:T(8,128)(2,1)} %param.24), kind=kOutput, calls=%fused_computation.73 | convolution fusion | flops 1623195648 | bytes 17825792 | tf_op jit(solution)/shard_map/dot_general | solution.py:38
  334.7 6.3 fusion.99
  341.0 6.0 multiply_reduce_fusion.4
  372.4 6.0 all_gather.92
  380.4 10.8 %while.50 = (s32[]{:T(128)}, f32[256,8,2,128]{0,3,2,1:T(8,128)}, s32[]{:T(128)}, bf16[1024,1024]{0,1:T(8,128)(2,1)}, s32[1,256]{1,0:T(1,128)S(1)}, /*index=5*/s3...) while((s32[]{:T(128)}, f32[256,8,2,128]{0,3,2,1:T(8,128)}, ...), condition=%wide.region_14.15_spmd.clone, body=%wide.region_13.14_spmd.clone.sunk | while | flops 813367808 | bytes 18522324 | solution.py:193
  384.7 6.5 bitcast_add_fusion.5
  400.3 74.4 %while.51 = (s32[]{:T(128)}, f32[256,8,128]{0,2,1:T(8,128)}, f32[256,8,128]{0,2,1:T(8,128)}, bf16[1024,2048]{0,1:T(8,128)(2,1)}, s32[1024]{0:T(1024)S(1)}, /*ind...) while((s32[]{:T(128)}, f32[256,8,128]{0,2,1:T(8,128)}, ...), condition=%wide.region_17.18_spmd.clone, body=%wide.region_16.17_spmd.clone.sunk | while | flops 1085997568 | bytes 37052696 | solution.py:246
  446.4 5.9 fusion.195
  464.9 5.9 fusion.195
  489.5 21.7 %all-to-all-done.3 = bf16[256,4,768]{2,0,1:T(8,128)(2,1)} async-done(((bf16[256,4,768]{2,0,1:T(8,128)(2,1)}), bf16[256,4,768]{2,0,1:T(8,128)(2,1)}, u32[]{:S(2)}, u32[]{:S(2)}) %all-to-all-start.3) | async-done | bytes 1572896 | tf_op jit(solution)/shard_map/all_to_all | solution.py:273
  519.8 9.7 %all-to-all-done.1 = bf16[256,4,256]{2,0,1:T(8,128)(2,1)S(1)} async-done(((bf16[256,4,256]{2,0,1:T(8,128)(2,1)}), bf16[256,4,256]{2,0,1:T(8,128)(2,1)S(1)}, u32[]{:S(2)}, u32[]{:S(2)}) %all-to-all-start.1) | async-done | bytes 524320 | tf_op jit(solution)/shard_map/all_to_all | solution.py:285
  553.4 6.7 all-to-all-done.2
  560.1 27.2 %all-gather.55.cloned.1.call-done = bf16[1024,3072]{1,0:T(8,128)(2,1)} async-done(((bf16[256,3072]{1,0:T(8,128)(2,1)}), bf16[1024,3072]{1,0:T(8,128)(2,1)}) %all-gather.55.cloned.1.call-update) | async-done | bytes 6291472 | tf_op jit(solution)/shard_map/all_gather | solution.py:277
  593.1 42.1 %all-gather.53.cloned.1.call-done = bf16[1024,3072]{1,0:T(8,128)(2,1)} async-done(((bf16[256,3072]{1,0:T(8,128)(2,1)}), bf16[1024,3072]{1,0:T(8,128)(2,1)}) %all-gather.53.cloned.1.call-update) | async-done | bytes 6291472 | tf_op jit(solution)/shard_map/all_gather | solution.py:276
  640.9 18.5 %all-gather.49.cloned.1.call-done = bf16[1024,1024]{0,1:T(8,128)(2,1)} async-done(((bf16[256,1024]{0,1:T(8,128)(2,1)}), bf16[1024,1024]{0,1:T(8,128)(2,1)}) %all-gather.49.cloned.1.call-update) | async-done | bytes 2097168 | tf_op jit(solution)/shard_map/all_gather | solution.py:291
  676.1 11.2 %all-reduce.6 = (bf16[1024]{0:T(1024)(128)(2,1)S(1)}, bf16[128]{0:T(256)(128)(2,1)S(1)}, bf16[128]{0:T(256)(128)(2,1)S(1)}, bf16[1024]{0:T(1024)(128)(2,1)S(1)}) all-reduce(f32[1024]{0:T(1024)S(1)} %get-tuple-element.612, f32[128]{0:T(128)S(1)} %copy-done.45, ...), channel_id=4, replica_groups=mesh['shard'=4,'rep'=8] {'shard'}, use_global_device_ids=true, to_apply=%region_21.22.clone | all-reduce | flops 2304 | bytes 13824
  687.6 22.8 %all-reduce.7 = (bf16[256]{0:T(256)(128)(2,1)S(1)}, bf16[32]{0:T(256)(128)(2,1)S(1)}, bf16[32]{0:T(256)(128)(2,1)S(1)}, bf16[256]{0:T(256)(128)(2,1)S(1)}) all-reduce(bf16[256]{0:T(256)(128)(2,1)S(1)} %dynamic-slice.15, bf16[32]{0:T(256)(128)(2,1)S(1)} %dynamic-slice.17, ...), channel_id=1, replica_groups=mesh['shard'=4,'rep'=8] {'rep'}, use_global_device_ids=true, to_apply=%region_22.23 | all-reduce | flops 576 | bytes 2304 | tf_op jit(solution)/shard_map/psum | solution.py:304
  715.4 210.5 %all-reduce.12.cloned.1.call-done = (bf16[256,2048]{1,0:T(8,128)(2,1)}, bf16[256,1024]{1,0:T(8,128)(2,1)}, bf16[256,1024]{1,0:T(8,128)(2,1)}, bf16[2048,256]{1,0...) async-done(((bf16[256,2048]{1,0:T(8,128)(2,1)}, bf16[256,1024]{1,0:T(8,128)(2,1)}, bf16[256,1024]{1,0:T(8,128)(2,1)}, ...) | async-done | bytes 7864336 | tf_op jit(solution)/shard_map/psum | solution.py:305
  (333 shorter events, 259.6 us)
Async XLA Ops:
  7.2 18.2 %copy-start.34 = (s32[1,256]{1,0:T(1,128)S(1)}, s32[1,256]{1,0:T(1,128)}, u32[]{:S(2)}) copy-start(s32[1,256]{1,0:T(1,128)} %param.23) | copy-start | bytes 3076
  7.2 24.1 %copy-start.10 = (bf16[1,256,1024]{2,1,0:T(8,128)(2,1)S(1)}, bf16[1,256,1024]{2,1,0:T(8,128)(2,1)}, u32[]{:S(2)}) copy-start(bf16[1,256,1024]{2,1,0:T(8,128)(2,1)} %param.22) | copy-start | bytes 1572868
  7.2 27.9 %all-gather.27.cloned.1.call-start = ((), (), s32[]{:S(2)}) async-start(), calls=%async_computation.6 | async-start | bytes 2621440 | tf_op jit(solution)/shard_map/all_gather | solution.py:85
  8.0 51.4 %all-gather.23.cloned.1.call-start = ((), (), s32[]{:S(2)}) async-start(), calls=%async_computation.4 | async-start | bytes 2621440 | tf_op jit(solution)/shard_map/all_gather | solution.py:86
  8.7 86.7 %all-gather.31.cloned.1.call-start = ((), (), s32[]{:S(2)}) async-start(), calls=%async_computation.8 | async-start | bytes 5242880 | tf_op jit(solution)/shard_map/all_gather | solution.py:84
  9.5 110.3 %all-gather.29.cloned.1.call-start = ((), (), s32[]{:S(2)}) async-start(), calls=%async_computation.7 | async-start | bytes 2621440 | tf_op jit(solution)/shard_map/all_gather | solution.py:104
  15.5 19.6 %copy-start.37 = (bf16[4,1,256]{2,1,0:T(2,128)(2,1)}, bf16[4,1,256]{2,1,0:T(2,128)(2,1)S(1)}, u32[]{:S(2)}) copy-start(bf16[4,1,256]{2,1,0:T(2,128)(2,1)S(1)} %all-gather.2) | copy-start | bytes 6148
  15.5 86.3 %copy-start.39 = (f32[4,1,256]{2,1,0:T(1,128)}, f32[4,1,256]{2,1,0:T(1,128)S(1)}, u32[]{:S(2)}) copy-start(f32[4,1,256]{2,1,0:T(1,128)S(1)} %convert_element_type.247) | copy-start | bytes 12292
  25.4 13.8 %copy-start.43 = (f32[128]{0:T(128)}, f32[128]{0:T(128)S(1)}, u32[]{:S(2)}) copy-start(f32[128]{0:T(128)S(1)} %convert_element_type.196) | copy-start | bytes 1540
  31.5 70.3 %copy-start.41 = (f32[256]{0:T(256)}, f32[256]{0:T(256)S(1)}, u32[]{:S(2)}) copy-start(f32[256]{0:T(256)S(1)} %add_rsqrt_fusion.3) | copy-start | bytes 3076
  40.9 103.4 %all-gather.25.cloned.1.call-start = ((), (), s32[]{:S(2)}) async-start(), calls=%async_computation.5 | async-start | bytes 2621440 | tf_op jit(solution)/shard_map/all_gather | solution.py:105
  62.5 118.3 %all-gather.33.cloned.1.call-start = ((), (), s32[]{:S(2)}) async-start(), calls=%async_computation.9 | async-start | bytes 5242880 | tf_op jit(solution)/shard_map/all_gather | solution.py:89
  63.1 165.7 %all-gather.35.cloned.1.call-start = ((), (), s32[]{:S(2)}) async-start(), calls=%async_computation.10 | async-start | bytes 7864320 | tf_op jit(solution)/shard_map/all_gather | solution.py:154
  63.9 212.9 %all-gather.37.cloned.1.call-start = ((), (), s32[]{:S(2)}) async-start(), calls=%async_computation.11 | async-start | bytes 7864320 | tf_op jit(solution)/shard_map/all_gather | solution.py:155
  64.6 260.1 %all-gather.39.cloned.1.call-start = ((), (), s32[]{:S(2)}) async-start(), calls=%async_computation.12 | async-start | bytes 7864320 | tf_op jit(solution)/shard_map/all_gather | solution.py:156
  65.4 332.1 %all-gather.41.cloned.1.call-start = ((), (), s32[]{:S(2)}) async-start(), calls=%async_computation.13 | async-start | bytes 5242880 | tf_op jit(solution)/shard_map/all_gather | solution.py:197
  107.7 12.1 %copy-start.9 = (bf16[256,16,128]{0,2,1:T(8,128)(2,1)}, bf16[256,16,128]{0,2,1:T(8,128)(2,1)S(1)}, u32[]{:S(2)}) copy-start(bf16[256,16,128]{0,2,1:T(8,128)(2,1)S(1)} %fusion.51) | copy-start | bytes 3145732
  123.0 275.2 %all-gather.43.cloned.1.call-start = ((), (), s32[]{:S(2)}) async-start(), calls=%async_computation.14 | async-start | bytes 5242880 | tf_op jit(solution)/shard_map/all_gather | solution.py:200
  351.3 163.5 %all-gather.57.cloned.1.call-start = ((), (), s32[]{:S(2)}) async-start(), calls=%async_computation.21 | async-start | bytes 2621440 | tf_op jit(solution)/shard_map/all_gather | solution.py:278
  351.9 181.1 %all-gather.51.cloned.1.call-start = ((), (), s32[]{:S(2)}) async-start(), calls=%async_computation.18 | async-start | bytes 5242880 | tf_op jit(solution)/shard_map/all_gather | solution.py:289
  361.6 184.0 %all-gather.45.cloned.1.call-start = ((), (), s32[]{:S(2)}) async-start(), calls=%async_computation.15 | async-start | bytes 5242880 | tf_op jit(solution)/shard_map/all_gather | solution.py:288
  397.4 152.8 %all-gather.47.cloned.1.call-start = ((), (), s32[]{:S(2)}) async-start(), calls=%async_computation.16 | async-start | bytes 2621440 | tf_op jit(solution)/shard_map/all_gather | solution.py:290
  400.3 75.9 %copy-start.36 = (f32[256,8]{0,1:T(8,128)S(1)}, f32[256,8]{0,1:T(8,128)}, u32[]{:S(2)}) copy-start(f32[256,8]{0,1:T(8,128)} %copy-done.35) | copy-start | bytes 24580
  478.2 109.1 %all-gather.55.cloned.1.call-start = ((), (), s32[]{:S(2)}) async-start(), calls=%async_computation.20 | async-start | bytes 7864320 | tf_op jit(solution)/shard_map/all_gather | solution.py:277
  478.8 156.3 %all-gather.53.cloned.1.call-start = ((), (), s32[]{:S(2)}) async-start(), calls=%async_computation.19 | async-start | bytes 7864320 | tf_op jit(solution)/shard_map/all_gather | solution.py:276
  480.9 30.4 %all-to-all-start.3 = ((bf16[256,4,768]{2,0,1:T(8,128)(2,1)}), bf16[256,4,768]{2,0,1:T(8,128)(2,1)}, u32[]{:S(2)}, u32[]{:S(2)}) async-start(bf16[256,4,768]{2,0,1:T(8,128)(2,1)} %bitcast.295), calls=%async_computation.3 | async-start | bytes 3145728 | tf_op jit(solution)/shard_map/all_to_all | solution.py:273
  485.3 174.1 %all-gather.49.cloned.1.call-start = ((), (), s32[]{:S(2)}) async-start(), calls=%async_computation.17 | async-start | bytes 2621440 | tf_op jit(solution)/shard_map/all_gather | solution.py:291
  511.3 18.2 %all-to-all-start.1 = ((bf16[256,4,256]{2,0,1:T(8,128)(2,1)}), bf16[256,4,256]{2,0,1:T(8,128)(2,1)S(1)}, u32[]{:S(2)}, u32[]{:S(2)}) async-start(bf16[256,4,256]{2,0,1:T(8,128)(2,1)} %bitcast.297), calls=%async_computation.1 | async-start | bytes 1048576 | tf_op jit(solution)/shard_map/all_to_all | solution.py:285
  529.5 12.3 %all-to-all-start = ((bf16[256,4,256]{2,0,1:T(8,128)(2,1)}), bf16[256,4,256]{2,0,1:T(8,128)(2,1)S(1)}, u32[]{:S(2)}, u32[]{:S(2)}) async-start(bf16[256,4,256]{2,0,1:T(8,128)(2,1)} %fusion.78), calls=%async_computation | async-start | bytes 1048576 | tf_op jit(solution)/shard_map/all_to_all | solution.py:284
  541.8 18.3 %all-to-all-start.2 = ((bf16[256,4,256]{2,0,1:T(8,128)(2,1)}), bf16[256,4,256]{2,0,1:T(8,128)(2,1)S(1)}, u32[]{:S(2)}, u32[]{:S(2)}) async-start(bf16[256,4,256]{2,0,1:T(8,128)(2,1)} %bitcast.296), calls=%async_computation.2 | async-start | bytes 1048576 | tf_op jit(solution)/shard_map/all_to_all | solution.py:272
  545.3 380.5 %all-reduce.12.cloned.1.call-start = ((), (), s32[]{:S(2)}) async-start(), calls=%async_computation.22 | async-start | bytes 15728640 | tf_op jit(solution)/shard_map/psum | solution.py:305
  675.0 37.5 %copy-start.15 = (bf16[1,256,1024]{2,1,0:T(8,128)(2,1)S(1)}, bf16[1,256,1024]{2,1,0:T(8,128)(2,1)}, u32[]{:S(2)}) copy-start(bf16[1,256,1024]{2,1,0:T(8,128)(2,1)} %param.24) | copy-start | bytes 1572868
  (49 other events, 157.4 us)
Sparse Core Ops, SparseCore 0:
  9.6 25.4 all-gather.26
  36.7 22.6 all-gather.22
  60.9 34.4 all-gather.30
  96.9 22.8 all-gather.28
  121.7 22.5 all-gather.24
  145.7 35.0 all-gather.32
  182.4 46.3 all-gather.34
  230.3 46.3 all-gather.36
  278.3 46.3 all-gather.38
  326.1 35.0 all-gather.40
  363.3 34.8 all-gather.42
  399.6 22.5 all-gather.56
  424.4 35.0 all-gather.50
  461.4 40.8 all-gather.44
  504.3 28.9 all-gather.46
  535.3 51.9 all-gather.54
  588.7 46.3 all-gather.52
  636.5 22.8 all-gather.48
  666.0 259.8 all-reduce.11
where the time goes:
time: 955 us; the launch traced here: 945 us
  waiting for transfers between devices  568 us (59%)
  matrix products  156 us (16%)
  local copies, waits for them, and re-layouts  69.8 us (7%)
  blocking collectives  69.8 us (7%)
  other arithmetic  37.5 us (4%)
  starting transfers between devices  26.2 us (3%)
  between operations  17 us (2%)
    psum x1, waiting for transfers between devices, per_device(): lax.psum(share_query.astype(jnp.bfloat16), 'rep').astype(jnp.float32)  210 us
    dot_general x21, matrix products, product(): return jnp.dot(left, right, preferred_element_type=jnp.float32)  92.4 us
    all_gather x1, waiting for transfers between devices, per_device(): lax.all_gather(gate_grad, 'shard', axis=0, tiled=True)  42.1 us
    all_gather x1, waiting for transfers between devices, per_device(): lax.all_gather(gate_weight, 'shard', axis=0, tiled=True)  42.1 us
    all_gather x1, waiting for transfers between devices, per_device(): lax.all_gather(down_weight, 'shard', axis=0, tiled=True)  41.6 us
    all_gather x1, waiting for transfers between devices, per_device(): lax.all_gather(up_weight, 'shard', axis=0, tiled=True)  41.5 us
    all_gather x1, waiting for transfers between devices, per_device(): lax.all_gather(up_grad, 'shard', axis=0, tiled=True)  27.2 us
    all_gather x1, waiting for transfers between devices, per_device(): lax.all_gather(output_weight, 'shard', axis=1, tiled=True)  25.6 us
  transfers between devices with their start and end apart: 23, of which 18 were waited for; matrix products, arithmetic and copies ran while one was open for 25% of the time, Pallas kernels for 0%

commit v1 on v0

v1 whole, which is shorter than its diff:
```python
import functools
import math

import jax
import jax.numpy as jnp
from jax import lax
from jax.experimental import pallas as pl
from jax.experimental.pallas import tpu as pltpu
from jax.sharding import PartitionSpec as P

eps_norm = 1e-06
theta_base = 1000000.0
f32 = jnp.float32
bf16 = jnp.bfloat16
vmem_bytes = 50 * 1024 * 1024


def dot(left, right):
    return lax.dot_general(left, right, (((1,), (0,)), ((), ())), preferred_element_type=f32)


def dot_nt(left, right):
    return lax.dot_general(left, right, (((1,), (1,)), ((), ())), preferred_element_type=f32)


def dot_tn(left, right):
    return lax.dot_general(left, right, (((0,), (0,)), ((), ())), preferred_element_type=f32)


def inverse_root(rows):
    return lax.rsqrt(jnp.mean(rows * rows, axis=-1, keepdims=True) + eps_norm)


def norm_back(grad, rows, scale):
    return scale * grad - rows * (scale * scale * scale) * jnp.mean(
        grad * rows, axis=-1, keepdims=True
    )


def params():
    return pltpu.CompilerParams(vmem_limit_bytes=vmem_bytes)


def cost(flops, moved, trans=0):
    return pl.CostEstimate(flops=int(flops), bytes_accessed=int(moved), transcendentals=int(trans))


def half_turn(rows):
    return pltpu.roll(rows, rows.shape[-1] // 2, axis=1)


def project_kernel(q_heads, k_heads, tok, gain, weight, cosine, sine, gains, normed, lin, rot, val):
    rows = tok[...].astype(f32)
    low = (rows * inverse_root(rows) * gain[...]).astype(bf16)
    normed[...] = low
    head = cosine.shape[1]
    full = dot(low, weight[...])
    cos_, sin_ = cosine[...], sine[...]
    for index in range(q_heads + k_heads):
        part = full[:, index * head : (index + 1) * head]
        lin[:, index * head : (index + 1) * head] = part
        which = 0 if index < q_heads else 1
        unit = part * inverse_root(part) * gains[which : which + 1, :]
        rot[:, index * head : (index + 1) * head] = (unit * cos_ + half_turn(unit) * sin_).astype(
            bf16
        )
    val[...] = full[:, (q_heads + k_heads) * head :].astype(bf16)


def project(tok, gain, weight, cosine, sine, gains, q_heads, k_heads, block):
    total, width = tok.shape
    head = cosine.shape[1]
    qk = (q_heads + k_heads) * head
    kv = k_heads * head
    row = lambda n: pl.BlockSpec((block, n), lambda i: (i, 0))
    fixed = lambda a, b: pl.BlockSpec((a, b), lambda i: (0, 0))
    return pl.pallas_call(
        functools.partial(project_kernel, q_heads, k_heads),
        grid=(total // block,),
        in_specs=[
            row(width),
            fixed(1, width),
            fixed(*weight.shape),
            row(head),
            row(head),
            fixed(2, head),
        ],
        out_specs=[row(width), row(qk), row(qk), row(kv)],
        out_shape=[
            jax.ShapeDtypeStruct((total, width), bf16),
            jax.ShapeDtypeStruct((total, qk), f32),
            jax.ShapeDtypeStruct((total, qk), bf16),
            jax.ShapeDtypeStruct((total, kv), bf16),
        ],
        compiler_params=params(),
        cost_estimate=cost(2 * total * weight.size, 2 * weight.size + total * width * 12),
    )(tok, gain, weight, cosine, sine, gains)


def allowed_pairs(j, k, start_q, start_k, block, seg_col, seg_row):
    own = seg_col[pl.ds(start_q, block), :]
    other = seg_row[:, pl.ds(start_k, block)]
    allowed = own == other
    if j == k:
        at_q = lax.broadcasted_iota(jnp.int32, (block, block), 0)
        at_k = lax.broadcasted_iota(jnp.int32, (block, block), 1)
        allowed = allowed & (at_q >= at_k)
    return allowed


def attend_kernel(blocks, group, factor, order, query, key, val, seg_col, seg_row, out, logs):
    total, head = key.shape
    block = total // blocks
    flip = order[0]
    start = [pl.multiple_of((jnp.int32(i) ^ flip) * block, block) for i in range(blocks)]
    ones = jnp.ones((block, head), bf16)
    for j in range(blocks):
        stacked = jnp.concatenate(
            [query[pl.ds(start[j], block), h * head : (h + 1) * head] for h in range(group)], axis=0
        )
        acc = jnp.zeros((group * block, 2 * head), f32)
        for k in range(j + 1):
            raw = dot_nt(stacked, key[pl.ds(start[k], block), :])
            allowed = allowed_pairs(j, k, start[j], start[k], block, seg_col, seg_row)
            allowed = jnp.concatenate([allowed] * group, axis=0)
            probs = jnp.where(allowed, jnp.exp2(raw * factor), 0.0).astype(bf16)
            both = jnp.concatenate([val[pl.ds(start[k], block), :], ones], axis=1)
            acc = acc + dot(probs, both)
        sums = acc[:, head:]
        result = acc[:, :head] / sums
        log_sums = jnp.log2(sums)
        for h in range(group):
            out[pl.ds(start[j], block), h * head : (h + 1) * head] = result[
                h * block : (h + 1) * block
            ]
            logs[pl.ds(start[j], block), h * head : (h + 1) * head] = log_sums[
                h * block : (h + 1) * block
            ]


def attend(order, rot, val, seg_col, seg_row, q_heads, k_heads, head, blocks):
    total = rot.shape[0]
    group = q_heads // k_heads
    factor = head**-0.5 * math.log2(math.e)
    wide = pl.BlockSpec((total, group * head), lambda g, o: (0, g))
    return pl.pallas_call(
        functools.partial(attend_kernel, blocks, group, factor),
        grid_spec=pltpu.PrefetchScalarGridSpec(
            num_scalar_prefetch=1,
            grid=(k_heads,),
            in_specs=[
                wide,
                pl.BlockSpec((total, head), lambda g, o: (0, q_heads + g)),
                pl.BlockSpec((total, head), lambda g, o: (0, g)),
                pl.BlockSpec((total, 1), lambda g, o: (0, 0)),
                pl.BlockSpec((1, total), lambda g, o: (0, 0)),
            ],
            out_specs=[wide, wide],
        ),
        out_shape=[jax.ShapeDtypeStruct((total, q_heads * head), f32)] * 2,
        compiler_params=params(),
        cost_estimate=cost(4 * total * total * q_heads * head, total * q_heads * head * 12),
    )(order, rot, rot, val, seg_col, seg_row)


def attend_back_kernel(
    blocks, group, factor, scale, order, query, key, val, out_grad, out, logs, seg_col, seg_row,
    query_grad, key_grad, val_grad,
):
    total, head = key.shape
    block = total // blocks
    flip = order[0]
    start = [pl.multiple_of((jnp.int32(i) ^ flip) * block, block) for i in range(blocks)]

    def heads_of(ref, at):
        return jnp.concatenate(
            [ref[pl.ds(at, block), h * head : (h + 1) * head] for h in range(group)], axis=0
        )

    deltas = []
    for j in range(blocks):
        product = heads_of(out_grad, start[j]).astype(f32) * heads_of(out, start[j])
        deltas.append(jnp.sum(product, axis=1, keepdims=True))
    sums = [None] * blocks
    for k in range(blocks):
        key_block = key[pl.ds(start[k], block), :]
        val_block = val[pl.ds(start[k], block), :]
        key_sum = jnp.zeros((block, head), f32)
        val_sum = jnp.zeros((block, head), f32)
        for j in range(k, blocks):
            stacked = heads_of(query, start[j])
            grads = heads_of(out_grad, start[j])
            logged = heads_of(logs, start[j])
            logged = jnp.concatenate([logged] * (block // head), axis=1)
            raw = dot_nt(stacked, key_block)
            allowed = allowed_pairs(j, k, start[j], start[k], block, seg_col, seg_row)
            allowed = jnp.concatenate([allowed] * group, axis=0)
            probs = jnp.where(allowed, jnp.exp2(raw * factor - logged), 0.0)
            prob_grad = dot_nt(grads, val_block)
            score_grad = (probs * (prob_grad - deltas[j]) * scale).astype(bf16)
            val_sum = val_sum + dot_tn(probs.astype(bf16), grads)
            key_sum = key_sum + dot_tn(score_grad, stacked)
            piece = dot(score_grad, key_block)
            sums[j] = piece if k == 0 else sums[j] + piece
        key_grad[pl.ds(start[k], block), :] = key_sum
        val_grad[pl.ds(start[k], block), :] = val_sum
        for h in range(group):
            query_grad[pl.ds(start[k], block), h * head : (h + 1) * head] = sums[k][
                h * block : (h + 1) * block
            ]


def attend_back(order, rot, val, out_grad, out, logs, seg_col, seg_row, q_heads, k_heads, head, blocks):
    total = rot.shape[0]
    group = q_heads // k_heads
    scale = head**-0.5
    wide = pl.BlockSpec((total, group * head), lambda g, o: (0, g))
    thin = pl.BlockSpec((total, head), lambda g, o: (0, g))
    return pl.pallas_call(
        functools.partial(attend_back_kernel, blocks, group, scale * math.log2(math.e), scale),
        grid_spec=pltpu.PrefetchScalarGridSpec(
            num_scalar_prefetch=1,
            grid=(k_heads,),
            in_specs=[
                wide,
                pl.BlockSpec((total, head), lambda g, o: (0, q_heads + g)),
                thin,
                wide,
                wide,
                wide,
                pl.BlockSpec((total, 1), lambda g, o: (0, 0)),
                pl.BlockSpec((1, total), lambda g, o: (0, 0)),
            ],
            out_specs=[wide, thin, thin],
        ),
        out_shape=[
            jax.ShapeDtypeStruct((total, q_heads * head), f32),
            jax.ShapeDtypeStruct((total, k_heads * head), f32),
            jax.ShapeDtypeStruct((total, k_heads * head), f32),
        ],
        compiler_params=params(),
        cost_estimate=cost(10 * total * total * q_heads * head, total * q_heads * head * 20),
    )(order, rot, rot, val, out_grad, out, logs, seg_col, seg_row)


def feed_kernel(norm, cot, weight, down, hidden, gate_up_grad, norm_grad, out):
    units = down.shape[0]
    low = norm[...]
    gate = dot(low, weight[:, :units])
    upper = dot(low, weight[:, units:])
    sigma = 1.0 / (1.0 + jnp.exp(-gate))
    silu = gate * sigma
    hid = (silu * upper).astype(bf16)
    hidden[...] = hid
    back = dot_nt(cot[...], down[...])
    gate_grad = (back * upper * sigma * (1.0 + gate * (1.0 - sigma))).astype(bf16)
    up_grad = (back * silu).astype(bf16)
    gate_up_grad[:, :units] = gate_grad
    gate_up_grad[:, units:] = up_grad
    norm_grad[...] = (
        dot_nt(gate_grad, weight[:, :units]) + dot_nt(up_grad, weight[:, units:])
    ).astype(bf16)
    out[...] = dot(hid, down[...]).astype(bf16)


def feed(norm, cot, weight, down, block):
    total, width = norm.shape
    units = down.shape[0]
    row = lambda n: pl.BlockSpec((block, n), lambda i: (i, 0))
    fixed = lambda a, b: pl.BlockSpec((a, b), lambda i: (0, 0))
    return pl.pallas_call(
        feed_kernel,
        grid=(total // block,),
        in_specs=[row(width), row(width), fixed(*weight.shape), fixed(*down.shape)],
        out_specs=[row(units), row(2 * units), row(width), row(width)],
        out_shape=[
            jax.ShapeDtypeStruct((total, units), bf16),
            jax.ShapeDtypeStruct((total, 2 * units), bf16),
            jax.ShapeDtypeStruct((total, width), bf16),
            jax.ShapeDtypeStruct((total, width), bf16),
        ],
        compiler_params=params(),
        cost_estimate=cost(12 * total * down.size, 6 * down.size + total * width * 16, total * units),
    )(norm, cot, weight, down)


def unproject_kernel(
    q_heads, k_heads, query_grad, key_grad, val_grad, lin, cosine, sine, gains, weight, tok,
    lin_grad, norm_grad, gain_sum, head_sum,
):
    head = cosine.shape[1]
    cos_, sin_ = cosine[...], sine[...]
    sums = [jnp.zeros((1, head), f32), jnp.zeros((1, head), f32)]
    for index in range(q_heads + k_heads):
        which = 0 if index < q_heads else 1
        ref, place = (query_grad, index) if which == 0 else (key_grad, index - q_heads)
        turned = ref[:, place * head : (place + 1) * head]
        grad = turned * cos_ - half_turn(turned) * sin_
        rows = lin[:, index * head : (index + 1) * head]
        scale = inverse_root(rows)
        sums[which] = sums[which] + jnp.sum(grad * rows * scale, axis=0, keepdims=True)
        lin_grad[:, index * head : (index + 1) * head] = norm_back(
            grad * gains[which : which + 1, :], rows, scale
        ).astype(bf16)
    lin_grad[:, (q_heads + k_heads) * head :] = val_grad[...].astype(bf16)
    normed_grad = dot_nt(lin_grad[...], weight[...])
    norm_grad[...] = normed_grad.astype(bf16)
    rows = tok[...].astype(f32)
    gain_part = jnp.sum(normed_grad * rows * inverse_root(rows), axis=0, keepdims=True)

    @pl.when(pl.program_id(0) == 0)
    def _():
        gain_sum[...] = jnp.zeros_like(gain_sum)
        head_sum[...] = jnp.zeros_like(head_sum)

    gain_sum[...] += gain_part
    head_sum[...] += jnp.concatenate(sums, axis=0)


def unproject(query_grad, key_grad, val_grad, lin, cosine, sine, gains, weight, tok, q_heads, k_heads, block):
    total, width = tok.shape
    head = cosine.shape[1]
    row = lambda n: pl.BlockSpec((block, n), lambda i: (i, 0))
    fixed = lambda a, b: pl.BlockSpec((a, b), lambda i: (0, 0))
    return pl.pallas_call(
        functools.partial(unproject_kernel, q_heads, k_heads),
        grid=(total // block,),
        in_specs=[
            row(q_heads * head),
            row(k_heads * head),
            row(k_heads * head),
            row((q_heads + k_heads) * head),
            row(head),
            row(head),
            fixed(2, head),
            fixed(*weight.shape),
            row(width),
        ],
        out_specs=[row(weight.shape[1]), row(width), fixed(1, width), fixed(2, head)],
        out_shape=[
            jax.ShapeDtypeStruct((total, weight.shape[1]), bf16),
            jax.ShapeDtypeStruct((total, width), bf16),
            jax.ShapeDtypeStruct((1, width), f32),
            jax.ShapeDtypeStruct((2, head), f32),
        ],
        compiler_params=params(),
        cost_estimate=cost(2 * total * weight.size, 2 * weight.size + total * width * 16),
    )(query_grad, key_grad, val_grad, lin, cosine, sine, gains, weight, tok)


def place_kernel(count, outs, moves, scalars, *refs):
    inputs, results = refs[:count], refs[count:]
    shard, pos = scalars[0], scalars[1]
    for source, index, rows, columns, target, spot in moves:
        piece = inputs[source][index + (slice(rows[0], rows[1]), slice(columns[0], columns[1]))]
        row, column = spot(shard, pos)
        results[target][
            pl.ds(pl.multiple_of(row, 16), rows[1] - rows[0]),
            pl.ds(pl.multiple_of(column, 128), columns[1] - columns[0]),
        ] = piece.astype(results[target].dtype)


def place(scalars, inputs, out_shapes, moves):
    moved = sum(item.size * 2 for item in inputs) + sum(
        math.prod(shape) * (4 if kind == f32 else 2) for shape, kind in out_shapes
    )
    whole = pl.BlockSpec(memory_space=pltpu.VMEM)
    return pl.pallas_call(
        functools.partial(place_kernel, len(inputs), len(out_shapes), moves),
        in_specs=[pl.BlockSpec(memory_space=pltpu.SMEM)] + [whole] * len(inputs),
        out_specs=[whole] * len(out_shapes),
        out_shape=[jax.ShapeDtypeStruct(shape, kind) for shape, kind in out_shapes],
        compiler_params=params(),
        cost_estimate=cost(0, moved),
    )(scalars, *inputs)


class Moves:
    def __init__(self):
        self.shards = lax.axis_size("shard")
        self.reps = lax.axis_size("rep")
        self.mine = lax.axis_index("shard")
        self.direct = self.shards == 4 and self.reps == 8
        self.flip = self.mine if self.direct else jnp.int32(0)
        rep = lax.axis_index("rep")
        self.pos = jnp.where(rep % 2 == 0, rep // 2, 7 - rep // 2)
        self.ring = [0, 2, 4, 6, 7, 5, 3, 1]
        self.scalars = jnp.stack([self.mine, self.pos]).astype(jnp.int32)

    def swap(self, item, mask):
        return lax.ppermute(item, "shard", [(i, i ^ mask) for i in range(4)])

    def up(self, item):
        ring = self.ring
        return lax.ppermute(item, "rep", [(ring[i], ring[(i + 1) % 8]) for i in range(8)])

    def down(self, item):
        ring = self.ring
        return lax.ppermute(item, "rep", [(ring[(i + 1) % 8], ring[i]) for i in range(8)])

    def gather(self, item):
        if not self.direct:
            return lax.all_gather(item, "shard", axis=0, tiled=True)
        far = self.swap(item, 2)
        near = self.swap(item, 1)
        cross = self.swap(far, 1)
        return jnp.concatenate([item, near, far, cross], axis=0)

    def scatter(self, item):
        if not self.direct:
            return lax.psum_scatter(item.astype(f32), "shard", scatter_dimension=0, tiled=True)
        rows = item.shape[0] // 4
        own, near, far, cross = (item[i * rows : (i + 1) * rows] for i in range(4))
        far = self.swap(far + self.swap(cross, 1), 2)
        near = self.swap(near, 1)
        return own.astype(f32) + near.astype(f32) + far.astype(f32)

    def ring_gather(self, item, axis):
        half = item.shape[axis] // 2
        first = lambda v: lax.slice_in_dim(v, 0, half, axis=axis)
        last = lambda v: lax.slice_in_dim(v, half, 2 * half, axis=axis)
        u1, d1 = self.up(item), self.down(item)
        u2, d2 = self.up(u1), self.down(d1)
        u3, d3 = self.up(u2), self.down(d2)
        u4, d4 = self.up(first(u3)), self.down(last(d3))
        return [
            (item, 0, None), (u1, -1, None), (d1, 1, None), (u2, -2, None), (d2, 2, None),
            (u3, -3, None), (d3, 3, None), (u4, 4, 0), (d4, 4, 1),
        ]

    def ring_scatter(self, item, axis):
        def local(offset):
            return lax.dynamic_index_in_dim(item, (self.pos + offset) % 8, axis, keepdims=False)

        first = lambda v: lax.slice_in_dim(v, 0, 1, axis=axis)
        last = lambda v: lax.slice_in_dim(v, 1, 2, axis=axis)
        u = self.up(first(local(4)))
        d = self.down(last(local(4)))
        a, b = local(3), local(5)
        u = self.up(jnp.concatenate([first(a) + u, last(a)], axis=axis))
        d = self.down(jnp.concatenate([first(b), last(b) + d], axis=axis))
        u, d = self.up(u + local(2)), self.down(d + local(6))
        u, d = self.up(u + local(1)), self.down(d + local(7))
        return (u.astype(f32) + d.astype(f32) + local(0).astype(f32)).astype(bf16)

    def exchange(self, block):
        return [
            block(0), self.swap(block(1), 1), self.swap(block(2), 2), self.swap(block(3), 3),
        ]


def fetch(moves, block, rows, spot, shape):
    eighth = rows // 8
    pos = moves.pos
    own = block(0, 0, rows)
    width = own.shape[1]
    near = moves.swap(block(1, 0, rows), 1)
    begin = pos * eighth
    piece = jnp.stack([block(2, begin, eighth), block(3, begin, eighth)])
    parts = moves.ring_gather(moves.swap(piece, 2), 1)
    far = jnp.concatenate([part[0] for part, _, _ in parts], axis=0)
    cross = moves.swap(jnp.concatenate([part[1] for part, _, _ in parts], axis=0), 1)
    todo = []

    def where(which, offset, half):
        def at(shard, pos_):
            line = 0
            if offset is not None:
                line = lax.rem(pos_ + (offset + 8), 8) * eighth + half * (eighth // 2)
            return spot(shard ^ which, line)

        return at

    for which in (0, 1):
        todo.append((which, (), (0, rows), (0, width), 0, where(which, None, 0)))
    for which in (2, 3):
        line = 0
        for part, offset, half in parts:
            size = part.shape[1]
            todo.append(
                (which, (), (line, line + size), (0, width), 0, where(which, offset, half or 0))
            )
            line += size
    return place(moves.scalars, [own, near, far, cross], [(shape, bf16)], todo)[0]


def per_device(
    tokens, segments, grad_out, attention_gain, query_weight, key_matrix, value_matrix, query_gain,
    key_gain, output_weight, mlp_gain, gate_weight, up_weight, down_weight,
):
    moves = Moves()
    shards, mine, direct = moves.shards, moves.mine, moves.direct
    rows, width = tokens.shape[1:]
    total = rows * shards
    slice_width = attention_gain.shape[0]
    head_slice = query_gain.shape[0]
    head = head_slice * shards
    k_heads = key_matrix.shape[1] // head // shards
    q_heads = query_weight.shape[1] // head // shards
    q_width, k_width = q_heads * head, k_heads * head
    units = down_weight.shape[0]
    own_tokens = tokens[0]
    cot = grad_out[0]

    small = jnp.concatenate(
        [attention_gain, mlp_gain, query_gain, key_gain, segments[0].astype(bf16)]
    )[None]
    small = moves.gather(small)
    if direct:
        whole = jnp.where(mine % 2 == 0, small, small[jnp.array([1, 0, 3, 2])])
        whole = jnp.where(mine // 2 == 0, whole, whole[jnp.array([2, 3, 0, 1])])
    else:
        whole = small
    cut = [slice_width, 2 * slice_width, 2 * slice_width + head_slice, 2 * slice_width + 2 * head_slice]
    input_gain = whole[:, : cut[0]].reshape(1, width).astype(f32)
    second_gain = whole[:, cut[0] : cut[1]].reshape(1, width).astype(f32)
    head_gains = jnp.stack(
        [whole[:, cut[1] : cut[2]].reshape(head), whole[:, cut[2] : cut[3]].reshape(head)]
    ).astype(f32)
    segs = small[:, cut[3] :].reshape(total).astype(f32)
    index = jnp.arange(shards, dtype=jnp.int32) ^ moves.flip
    places = (index[:, None] * rows + jnp.arange(rows, dtype=jnp.int32)[None]).reshape(total)
    firsts = jnp.sum((segs < 0.5).astype(jnp.int32))
    seconds = jnp.sum((segs < 1.5).astype(jnp.int32))
    opening = jnp.where(segs < 0.5, 0, jnp.where(segs < 1.5, firsts, seconds))
    freqs = theta_base ** (-(jnp.arange(head // 2, dtype=f32) * 2.0) / head)
    angles = (places - opening).astype(f32)[:, None] * freqs
    cosine, sine = jnp.cos(angles), jnp.sin(angles)
    cosine = jnp.concatenate([cosine, cosine], axis=1)
    sine = jnp.concatenate([-sine, sine], axis=1)
    seg_col, seg_row = segs[:, None], segs[None, :]
    order = moves.flip.astype(jnp.int32)[None]

    def columns(item, i, begin, count, size):
        return lax.dynamic_slice(item, (begin, (mine ^ i) * size), (count, size))

    if direct:
        qkv_weight = fetch(
            moves,
            lambda i, begin, n: jnp.concatenate(
                [
                    columns(query_weight, i, begin, n, q_width),
                    columns(key_matrix, i, begin, n, k_width),
                    columns(value_matrix, i, begin, n, k_width),
                ],
                axis=1,
            ),
            slice_width,
            lambda source, line: (source * slice_width + line, 0),
            (width, q_width + 2 * k_width),
        )
        out_weight = fetch(
            moves,
            lambda i, begin, n: lax.dynamic_slice(
                output_weight, ((mine ^ i) * q_width + begin, 0), (n, slice_width)
            ),
            q_width,
            lambda source, line: (line, source * slice_width),
            (q_width, width),
        )
        feed_weight = fetch(
            moves,
            lambda i, begin, n: jnp.concatenate(
                [
                    columns(gate_weight, i, begin, n, units),
                    columns(up_weight, i, begin, n, units),
                ],
                axis=1,
            ),
            slice_width,
            lambda source, line: (source * slice_width + line, 0),
            (width, 2 * units),
        )
    else:
        spread = lambda item: lax.all_to_all(item, "shard", split_axis=1, concat_axis=0, tiled=True)
        qkv_weight = jnp.concatenate(
            [spread(query_weight), spread(key_matrix), spread(value_matrix)], axis=1
        )
        out_weight = lax.all_to_all(output_weight, "shard", split_axis=0, concat_axis=1, tiled=True)
        feed_weight = jnp.concatenate([spread(gate_weight), spread(up_weight)], axis=1)

    all_tokens = moves.gather(own_tokens)
    normed_one, lin, rot, val = project(
        all_tokens, input_gain, qkv_weight, cosine, sine, head_gains, q_heads, k_heads, rows
    )
    attended, logs = attend(order, rot, val, seg_col, seg_row, q_heads, k_heads, head, shards)
    attended_low = attended.astype(bf16)
    inputs = own_tokens.astype(f32)
    residual_one = inputs + moves.scatter(dot(attended_low, out_weight).astype(bf16))
    residual_scale = inverse_root(residual_one)
    normed_two = moves.gather((residual_one * residual_scale * second_gain).astype(bf16))

    all_cot = moves.gather(cot)
    hidden, gate_up_grad, norm_grad, out_part = feed(normed_two, all_cot, feed_weight, down_weight, rows)
    share_down = dot_tn(hidden, all_cot).astype(bf16)
    share_feed = dot_tn(normed_two, gate_up_grad).astype(bf16)
    layer_out = (residual_one + moves.scatter(out_part)).astype(bf16)
    normed_grad_two = moves.scatter(norm_grad)
    mlp_gain_part = jnp.sum(normed_grad_two * residual_one * residual_scale, axis=0)
    residual_grad = cot.astype(f32) + norm_back(
        normed_grad_two * second_gain, residual_one, residual_scale
    )
    branch_grad = moves.gather(residual_grad.astype(bf16))

    out_grad = dot_nt(branch_grad, out_weight).astype(bf16)
    share_out = dot_tn(attended_low, branch_grad).astype(bf16)
    query_grad, key_grad, val_grad = attend_back(
        order, rot, val, out_grad, attended, logs, seg_col, seg_row, q_heads, k_heads, head, shards
    )
    lin_grad, norm_one_part, gain_part, head_part = unproject(
        query_grad, key_grad, val_grad, lin, cosine, sine, head_gains, qkv_weight, all_tokens,
        q_heads, k_heads, rows,
    )
    share_qkv = dot_tn(normed_one, lin_grad).astype(bf16)
    normed_grad_one = moves.scatter(norm_one_part)
    grad_tokens = residual_grad + norm_back(normed_grad_one * input_gain, inputs, inverse_root(inputs))

    gains = jnp.concatenate([gain_part[0], mlp_gain_part, head_part.reshape(2 * head)])[None]
    if direct:
        gains = gains + moves.swap(gains, 1)
        gains = gains + moves.swap(gains, 2)
        for mask in (1, 2, 4):
            gains = gains + lax.ppermute(gains, "rep", [(i, i ^ mask) for i in range(8)])
    else:
        gains = lax.psum(gains, ("shard", "rep"))
    gains = gains[0]

    def own_part(begin, size):
        return lax.dynamic_slice_in_dim(gains, begin + mine * size, size, 0)

    grad_attention_gain = own_part(0, slice_width)
    grad_mlp_gain = own_part(width, slice_width)
    grad_query_gain = own_part(2 * width, head_slice)
    grad_key_gain = own_part(2 * width + head, head_slice)

    if direct:
        ring_at = lambda pos_, offset: lax.rem(pos_ + (offset + 8), 8)

        def finish_columns(share, pieces):
            n = share.shape[1]
            sub = slice_width // 16
            chunk = moves.ring_scatter(share.reshape(4, 8, 2, sub, n), 1)
            got = moves.exchange(lambda i: lax.dynamic_index_in_dim(chunk, mine ^ i, 0, keepdims=False))
            parts = moves.ring_gather(jnp.stack(got), 1)
            todo = []
            for source, (part, offset, half) in enumerate(parts):
                for i in range(4):
                    for h in range(part.shape[1]):
                        begin = 0
                        for target, size in enumerate(pieces):

                            def at(shard, pos_, i=i, line=(half or 0) + h, offset=offset, size=size):
                                row = ring_at(pos_, offset) * (2 * sub) + line * sub
                                return row, (shard ^ i) * size

                            todo.append((source, (i, h), (0, sub), (begin, begin + size), target, at))
                            begin += size
            shapes = [((slice_width, size * shards), f32) for size in pieces]
            return place(moves.scalars, [part for part, _, _ in parts], shapes, todo)

        def finish_down(share):
            sub = units // 16
            chunk = moves.ring_scatter(share.reshape(8, 2, sub, width), 0)
            parts = moves.ring_gather(chunk, 0)
            todo = []
            for source, (part, offset, half) in enumerate(parts):
                for h in range(part.shape[0]):

                    def at(shard, pos_, line=(half or 0) + h, offset=offset):
                        return ring_at(pos_, offset) * (2 * sub) + line * sub, 0

                    todo.append((source, (h,), (0, sub), (0, width), 0, at))
            return place(
                moves.scalars, [part for part, _, _ in parts], [((units, width), f32)], todo
            )[0]

        def finish_out(share):
            sub = q_width // 16
            chunk = moves.ring_scatter(share.reshape(8, 2, sub, width), 0)
            got = moves.exchange(
                lambda i: lax.dynamic_slice_in_dim(chunk, (mine ^ i) * slice_width, slice_width, 2)
            )
            parts = moves.ring_gather(jnp.stack(got), 1)
            todo = []
            for source, (part, offset, half) in enumerate(parts):
                for i in range(4):
                    for h in range(part.shape[1]):

                        def at(shard, pos_, i=i, line=(half or 0) + h, offset=offset):
                            row = ring_at(pos_, offset) * (2 * sub) + line * sub
                            return (shard ^ i) * q_width + row, 0

                        todo.append((source, (i, h), (0, sub), (0, slice_width), 0, at))
            return place(
                moves.scalars,
                [part for part, _, _ in parts],
                [((q_width * shards, slice_width), f32)],
                todo,
            )[0]

        grad_down = finish_down(share_down)
        grad_gate, grad_up = finish_columns(share_feed, [units, units])
        grad_output = finish_out(share_out)
        grad_query, grad_key, grad_value = finish_columns(share_qkv, [q_width, k_width, k_width])
    else:

        def finish(share, begin, size):
            part = lax.all_to_all(
                share[:, begin : begin + size], "shard", split_axis=0, concat_axis=1, tiled=True
            )
            return lax.psum(part, "rep").astype(f32)

        grad_down = lax.psum(share_down, "rep").astype(f32)
        grad_gate = finish(share_feed, 0, units)
        grad_up = finish(share_feed, units, units)
        grad_output = lax.psum(
            lax.all_to_all(share_out, "shard", split_axis=1, concat_axis=0, tiled=True), "rep"
        ).astype(f32)
        grad_query = finish(share_qkv, 0, q_width)
        grad_key = finish(share_qkv, q_width, k_width)
        grad_value = finish(share_qkv, q_width + k_width, k_width)

    return (
        layer_out[None], grad_tokens[None], grad_attention_gain, grad_query, grad_key, grad_value,
        grad_query_gain, grad_key_gain, grad_output, grad_mlp_gain, grad_gate, grad_up, grad_down,
    )


def solution(mesh):
    rows_over = P("shard", None)
    return jax.shard_map(
        per_device,
        mesh=mesh,
        in_specs=(
            P("rep", "shard", None), P("rep", "shard"), P("rep", "shard", None), P("shard"), rows_over,
            rows_over, rows_over, P("shard"), P("shard"), P(None, "shard"), P("shard"), rows_over,
            rows_over, rows_over,
        ),
        out_specs=(
            P("rep", "shard", None), P("rep", "shard", None), P("shard"), rows_over, rows_over,
            rows_over, P("shard"), P("shard"), P(None, "shard"), P("shard"), rows_over, rows_over,
            rows_over,
        ),
        check_vma=False,
    )
```

time: 955 us -> 463 us (0.48)
  waiting for transfers between devices: 568 us -> 167 us
  matrix products: 156 us -> 19.1 us
  starting transfers between devices: 26.2 us -> 135 us
  Pallas kernels: 0 us -> 70.8 us
  blocking collectives: 69.8 us -> 0 us
  local copies, waits for them, and re-layouts: 69.8 us -> 33.3 us
  between operations: 17 us -> 2.11 us
    all_gather x18 -> x0, waiting for transfers between devices: 309 us -> none  [the longest x1 42.1 us: per_device(): lax.all_gather(gate_grad, 'shard', axis=0, tiled=True)]
    psum x1 -> x0, waiting for transfers between devices: 210 us -> none  [per_device(): lax.psum(share_query.astype(jnp.bfloat16), 'rep').astype(jnp.float32)]
    ppermute x0 -> x138, waiting for transfers between devices: none -> 167 us  [the longest x44 72.4 us: up(): lax.ppermute(item, 'rep', [(ring[i], ring[(i + 1) % 8]) for i in range(8)])]
    dot_general x37 -> x6, matrix products: 156 us -> 19.1 us  [the longest x4 14 us: dot_tn(): lax.dot_general(left, right, (((0,), (0,)), ((), ())), preferred_element_...]
    ppermute x0 -> x138, starting transfers between devices: none -> 135 us  [the longest x44 61.9 us: up(): lax.ppermute(item, 'rep', [(ring[i], ring[(i + 1) % 8]) for i in range(8)])]
    pallas_call x0 -> x12, Pallas kernels: none -> 70.8 us  [the longest x7 17.9 us: place(): pl.pallas_call(functools.partial(place_kernel, len(inputs), len(out_shape...]
    all_to_all x4 -> x0, waiting for transfers between devices: 42.4 us -> none  [the longest x1 21.7 us: per_device(): lax.all_to_all(hidden_low, 'shard', split_axis=1, concat_axis=0, tiled=True)]
    all_gather x5 -> x0, blocking collectives: 27.9 us -> none  [the longest x1 6.03 us: per_device(): lax.all_gather(delta, 'shard', axis=2, tiled=True)]
  transfers between devices with their start and end apart: 23 -> 138, of which waited for: 18 -> 57; matrix products, arithmetic and copies ran while one was open for 25% -> 14% of each run, Pallas kernels for 0% -> 11%
where the time goes in v1:
time: 463 us; the launch traced here: 456 us
  waiting for transfers between devices  167 us (36%)
  starting transfers between devices  135 us (29%)
  Pallas kernels  70.8 us (15%)
  local copies, waits for them, and re-layouts  33.3 us (7%)
  other arithmetic  29.4 us (6%)
  matrix products  19.1 us (4%)
    ppermute x44, waiting for transfers between devices, up(): lax.ppermute(item, 'rep', [(ring[i], ring[(i + 1) % 8]) for i in range(8)])  72.4 us
    ppermute x44, starting transfers between devices, up(): lax.ppermute(item, 'rep', [(ring[i], ring[(i + 1) % 8]) for i in range(8)])  61.9 us
    ppermute x47, waiting for transfers between devices, swap(): return lax.ppermute(item, 'shard', [(i, i ^ mask) for i in range(4)])  48.8 us
    ppermute x44, starting transfers between devices, down(): lax.ppermute(item, 'rep', [(ring[(i + 1) % 8], ring[i]) for i in range(8)])  44.6 us
    ppermute x44, waiting for transfers between devices, down(): lax.ppermute(item, 'rep', [(ring[(i + 1) % 8], ring[i]) for i in range(8)])  40 us
    ppermute x47, starting transfers between devices, swap(): return lax.ppermute(item, 'shard', [(i, i ^ mask) for i in range(4)])  25.1 us
    pallas_call x7, Pallas kernels, place(): pl.pallas_call(functools.partial(place_kernel, len(inputs), len(out_shape...  17.9 us
    unnamed x132, local copies, waits for them, and re-layouts  16.7 us
  transfers between devices with their start and end apart: 138, of which 57 were waited for; matrix products, arithmetic and copies ran while one was open for 14% of the time, Pallas kernels for 11%

profile of v1, /device:TPU:0, one launch (start us, length us, event | category | flops | bytes accessed | tf_op | source)
XLA Modules:
  0.0 455.7 jit_solution(12369717556777755301)
XLA Ops:
  4.2 3.0 collective-permute-start.4
  61.6 4.5 collective-permute-done.25
  71.8 3.2 collective-permute-done.10
  77.0 3.0 collective-permute-done.11
  82.7 3.1 collective-permute-done.40
  114.3 7.3 %shard_map.256 = (bf16[1024,1024]{1,0:T(8,128)(2,1)}, f32[1024,768]{1,0:T(8,128)}, bf16[1024,768]{1,0:T(8,128)(2,1)S(1)}, bf16[1024,256]{1,0:T(8,128)(2,1)S(1)}) custom-call(bf16[1024,1024]{1,0:T(8,128)(2,1)} %pad_maximum_fusion.tok, f32[1,1024]{1,0:T(1,128)S(1)} %bitcast.402, bf16[1024,1024]{1,0:T(8,128)(2,1)} %shard_map.255.weight, ...), custom_call_target="tpu_custom_call" | custom-call | flops 2147483648 | bytes 14680064 | tf_op jit(solution)/shard_map/pallas_call | solution.py:77
  121.6 5.4 %shard_map.257 = (f32[1024,512]{1,0:T(8,128)}, f32[1024,512]{1,0:T(8,128)}) custom-call(s32[1]{0:T(128)} %bitcast.1.order, bf16[1024,768]{1,0:T(8,128)(2,1)S(1)} %get-tuple-element.35.query.key, bf16[1024,768]{1,0:T(8,128)(2,1)S(1)} %get-tuple-element.35.query.key, bf16[1024,256]{1,0:T(8,128)(2,1)S(1)} %get-tuple-element.36.val, f32[1024,1]{1,0:T(8,128)S(1)} %bitcast.397, ...), custom_call_target="tpu_custom_call" | custom-call | flops 2147483648 | bytes 6291456 | tf_op jit(solution)/shard_map/pallas_call | solution.py:146
  138.5 9.1 %collective-permute-done.30 = bf16[256,1024]{1,0:T(8,128)(2,1)S(1)} collective-permute-done((bf16[256,1024]{1,0:T(8,128)(2,1)S(1)}, bf16[256,1024]{1,0:T(8,128)(2,1)S(1)}, u32[]{:S(2)}, u32[]{:S(2)}) %collective-permute-start.30) | collective-permute-done | bytes 524320 | tf_op jit(solution)/shard_map/ppermute | solution.py:391
  152.2 10.5 %collective-permute-done.32 = bf16[256,1024]{1,0:T(8,128)(2,1)} collective-permute-done((bf16[256,1024]{1,0:T(8,128)(2,1)}, bf16[256,1024]{1,0:T(8,128)(2,1)}, u32[]{:S(2)}, u32[]{:S(2)}) %collective-permute-start.32) | collective-permute-done | bytes 524320 | tf_op jit(solution)/shard_map/ppermute | solution.py:391
  163.9 3.1 pad_maximum_fusion.2.cot
  167.0 3.0 shard_map.259.weight
  170.1 3.1 pad_maximum_fusion.1.norm
  173.2 15.3 %shard_map.260 = (bf16[1024,768]{1,0:T(8,128)(2,1)S(1)}, bf16[1024,1536]{1,0:T(8,128)(2,1)}, bf16[1024,1024]{1,0:T(8,128)(2,1)}, bf16[1024,1024]{1,0:T(8,128)(2,1)}) custom-call(bf16[1024,1024]{1,0:T(8,128)(2,1)} %pad_maximum_fusion.1.norm, bf16[1024,1024]{1,0:T(8,128)(2,1)} %pad_maximum_fusion.2.cot, bf16[1024,1536]{1,0:T(8,128)(2,1)} %shard_map.259.weight, ...), custom_call_target="tpu_custom_call" | custom-call | flops 9663676416 | bytes 21495808 | tf_op jit(solution)/shard_map/pallas_call | solution.py:271
  188.5 3.3 convolution_convert_fusion.3
  194.5 5.3 %convolution_convert_fusion = bf16[1024,1536]{1,0:T(8,128)(2,1)S(1)} fusion(bf16[1024,1536]{1,0:T(8,128)(2,1)S(1)} %copy-done.50, bf16[256,1024]{1,0:T(8,128)(2,1)} %collective-permute-done.33, bf16[256,1024]{1,0:T(8,128)(2,1)} %collective-permute-done.32, bf16[256,1024]{1,0:T(8,128)(2,1)} %collective-permute-done.31, bf16[256,1024]{1,0:T(8,128)(2,1)} %multiply_convert_fusion), kind=kOutput, calls=%fused_computation.2 | convolution fusion | flops 3231186944 | bytes 8388608 | tf_op jit(solution)/shard_map/dot_general | solution.py:27
  204.4 3.3 collective-permute-done.107
  214.9 9.2 %collective-permute-done.124 = bf16[2,48,1024]{2,1,0:T(8,128)(2,1)S(1)} collective-permute-done((bf16[2,48,1024]{2,1,0:T(8,128)(2,1)S(1)}, bf16[2,48,1024]{2,1,0:T(8,128)(2,1)S(1)}, u32[]{:S(2)}, u32[]{:S(2)}) %collective-permute-start.124) | collective-permute-done | bytes 196640 | tf_op jit(solution)/shard_map/ppermute | solution.py:395
  228.9 7.6 %collective-permute-done.105 = bf16[4,2,16,1536]{3,2,1,0:T(8,128)(2,1)S(1)} collective-permute-done((bf16[4,2,16,1536]{3,2,1,0:T(8,128)(2,1)S(1)}, bf16[4,2,16,1536]{3,2,1,0:T(8,128)(2,1)S(1)}, u32[]{:S(2)}, u32[]{:S(2)}) %collective-permute-start.105) | collective-permute-done | bytes 393248 | tf_op jit(solution)/shard_map/ppermute | solution.py:395
  245.3 7.4 %collective-permute-done.50 = bf16[256,1024]{1,0:T(8,128)(2,1)S(1)} collective-permute-done((bf16[256,1024]{1,0:T(8,128)(2,1)S(1)}, bf16[256,1024]{1,0:T(8,128)(2,1)S(1)}, u32[]{:S(2)}, u32[]{:S(2)}) %collective-permute-start.50) | collective-permute-done | bytes 524320 | tf_op jit(solution)/shard_map/ppermute | solution.py:391
  256.8 10.5 %collective-permute-done.55 = bf16[256,1024]{1,0:T(8,128)(2,1)S(1)} collective-permute-done((bf16[256,1024]{1,0:T(8,128)(2,1)S(1)}, bf16[256,1024]{1,0:T(8,128)(2,1)S(1)}, u32[]{:S(2)}, u32[]{:S(2)}) %collective-permute-start.55) | collective-permute-done | bytes 524320 | tf_op jit(solution)/shard_map/ppermute | solution.py:391
  280.5 12.2 %shard_map.261 = (f32[1024,512]{1,0:T(8,128)}, f32[1024,256]{1,0:T(8,128)S(1)}, f32[1024,256]{1,0:T(8,128)S(1)}) custom-call(s32[1]{0:T(128)} %bitcast.1.order, bf16[1024,768]{1,0:T(8,128)(2,1)} %copy-done.27, bf16[1024,768]{1,0:T(8,128)(2,1)} %copy-done.27, bf16[1024,256]{1,0:T(8,128)(2,1)S(1)} %copy-done.29, ...), custom_call_target="tpu_custom_call" | custom-call | flops 5368709120 | bytes 10485760 | tf_op jit(solution)/shard_map/pallas_call | solution.py:219
  292.6 12.7 %shard_map.262 = (bf16[1024,1024]{1,0:T(8,128)(2,1)}, bf16[1024,1024]{1,0:T(8,128)(2,1)}, f32[1,1024]{1,0:T(1,128)S(1)}, f32[2,128]{1,0:T(2,128)S(1)}) custom-call(f32[1024,512]{1,0:T(8,128)} %get-tuple-element.41.query_grad, f32[1024,256]{1,0:T(8,128)S(1)} %get-tuple-element.42.key_grad, f32[1024,256]{1,0:T(8,128)S(1)} %get-tuple-element.43.val_grad, ...), custom_call_target="tpu_custom_call" | custom-call | flops 2147483648 | bytes 18874368 | tf_op jit(solution)/shard_map/pallas_call | solution.py:325
  305.5 4.0 convolution_convert_fusion.1
  320.5 6.1 %collective-permute-done.65 = bf16[4,1,16,1024]{3,2,1,0:T(8,128)(2,1)S(1)} collective-permute-done((bf16[4,1,16,1024]{3,2,1,0:T(8,128)(2,1)S(1)}, bf16[4,1,16,1024]{3,2,1,0:T(8,128)(2,1)S(1)}, u32[]{:S(2)}, u32[]{:S(2)}) %collective-permute-start.65) | collective-permute-done | bytes 131104 | tf_op jit(solution)/shard_map/ppermute | solution.py:395
  334.7 3.7 collective-permute-done.62
  341.0 4.9 %collective-permute-done.90 = bf16[2,32,1024]{2,1,0:T(8,128)(2,1)S(1)} collective-permute-done((bf16[2,32,1024]{2,1,0:T(8,128)(2,1)S(1)}, bf16[2,32,1024]{2,1,0:T(8,128)(2,1)S(1)}, u32[]{:S(2)}, u32[]{:S(2)}) %collective-permute-start.90) | collective-permute-done | bytes 131104 | tf_op jit(solution)/shard_map/ppermute | solution.py:399
  346.6 5.0 %collective-permute-done.133.refs_4_ = bf16[2,48,1024]{2,1,0:T(8,128)(2,1)S(1)} collective-permute-done((bf16[2,48,1024]{2,1,0:T(8,128)(2,1)S(1)}, bf16[2,48,1024]{2,1,0:T(8,128)(2,1)S(1)}, u32[]{:S(2)}, u32[]{:S(2)}) %collective-permute-start.133) | collective-permute-done | bytes 196640 | tf_op jit(solution)/shard_map/ppermute | solution.py:399
  360.1 7.7 %collective-permute-done.87 = bf16[2,32,1024]{2,1,0:T(8,128)(2,1)S(1)} collective-permute-done((bf16[2,32,1024]{2,1,0:T(8,128)(2,1)S(1)}, bf16[2,32,1024]{2,1,0:T(8,128)(2,1)S(1)}, u32[]{:S(2)}, u32[]{:S(2)}) %collective-permute-start.87) | collective-permute-done | bytes 131104 | tf_op jit(solution)/shard_map/ppermute | solution.py:395
  385.2 5.4 %collective-permute-done.95.refs_1_ = bf16[4,2,32,256]{3,2,1,0:T(8,128)(2,1)S(1)} collective-permute-done((bf16[4,2,32,256]{3,2,1,0:T(8,128)(2,1)S(1)}, bf16[4,2,32,256]{3,2,1,0:T(8,128)(2,1)S(1)}, u32[]{:S(2)}, u32[]{:S(2)}) %collective-permute-start.95) | collective-permute-done | bytes 131104 | tf_op jit(solution)/shard_map/ppermute | solution.py:395
  429.7 3.7 shard_map.265
  440.0 5.7 %collective-permute-done.80.refs_5_ = bf16[4,2,16,1024]{3,2,1,0:T(8,128)(2,1)S(1)} collective-permute-done((bf16[4,2,16,1024]{3,2,1,0:T(8,128)(2,1)S(1)}, bf16[4,2,16,1024]{3,2,1,0:T(8,128)(2,1)S(1)}, u32[]{:S(2)}, u32[]{:S(2)}) %collective-permute-start.80) | collective-permute-done | bytes 262176 | tf_op jit(solution)/shard_map/ppermute | solution.py:395
  452.1 3.4 shard_map.263
  (520 shorter events, 258.7 us)
Async XLA Ops:
  4.2 16.9 %collective-permute-start.4 = (bf16[1,832]{1,0:T(2,128)(2,1)S(1)}, bf16[1,832]{1,0:T(2,128)(2,1)S(1)}, u32[]{:S(2)}, u32[]{:S(2)}) collective-permute-start(bf16[1,832]{1,0:T(2,128)(2,1)S(1)} %broadcast_in_dim.44), channel_id=1, source_target_pairs={{0,16},{8,24},{16,0},{24,8},{1,17},{9,25},{17,1},{25,9},{2,18},{10... | collective-permute-start | bytes 5000 | tf_op jit(solution)/shard_map/ppermute | solution.py:391
  7.2 95.5 %collective-permute-start.1 = (bf16[256,1024]{1,0:T(8,128)(2,1)}, bf16[256,1024]{1,0:T(8,128)(2,1)}, u32[]{:S(2)}, u32[]{:S(2)}) collective-permute-start(bf16[256,1024]{1,0:T(8,128)(2,1)} %bitcast.405), channel_id=1, source_target_pairs={{0,16},{8,24},{16,0},{24,8},{1,17},{9,25},{17,1},{25,9},{2,18},{10... | collective-permute-start | bytes 1572872 | tf_op jit(solution)/shard_map/ppermute | solution.py:391
  7.4 98.8 %collective-permute-start = (bf16[256,1024]{1,0:T(8,128)(2,1)}, bf16[256,1024]{1,0:T(8,128)(2,1)}, u32[]{:S(2)}, u32[]{:S(2)}) collective-permute-start(bf16[256,1024]{1,0:T(8,128)(2,1)} %bitcast.406), channel_id=1, source_target_pairs={{0,8},{8,0},{16,24},{24,16},{1,9},{9,1},{17,25},{25,17},{2,10},{10... | collective-permute-start | bytes 1572872 | tf_op jit(solution)/shard_map/ppermute | solution.py:391
  9.4 41.1 %collective-permute-start.38 = (bf16[2,32,1536]{2,1,0:T(8,128)(2,1)}, bf16[2,32,1536]{2,1,0:T(8,128)(2,1)}, u32[]{:S(2)}, u32[]{:S(2)}) collective-permute-start(bf16[2,32,1536]{2,1,0:T(8,128)(2,1)} %pad_maximum_fusion.18), channel_id=1, source_target_pairs={{0,16},{8,24},{16,0},{24,8},{1,17},{9,25},{17,1},{25,9},{2,18},{10... | collective-permute-start | bytes 589832 | tf_op jit(solution)/shard_map/ppermute | solution.py:391
  30.3 67.3 %collective-permute-start.17 = (bf16[512,256]{1,0:T(8,128)(2,1)S(1)}, bf16[512,256]{1,0:T(8,128)(2,1)S(1)}, u32[]{:S(2)}, u32[]{:S(2)}) collective-permute-start(bf16[512,256]{1,0:T(8,128)(2,1)S(1)} %copy-done.43), channel_id=1, source_target_pairs={{0,8},{8,0},{16,24},{24,16},{1,9},{9,1},{17,25},{25,17},{2,10},{10... | collective-permute-start | bytes 786440 | tf_op jit(solution)/shard_map/ppermute | solution.py:391
  58.4 23.5 %collective-permute-start.39 = (bf16[2,32,1536]{2,1,0:T(8,128)(2,1)}, bf16[2,32,1536]{2,1,0:T(8,128)(2,1)S(1)}, u32[]{:S(2)}, u32[]{:S(2)}) collective-permute-start(bf16[2,32,1536]{2,1,0:T(8,128)(2,1)} %collective-permute-done.38), channel_id=1, source_target_pairs={{0,2},{2,4},{4,6},{6,7},{7,5},{5,3},{3,1},{1,0},{8,10},{10,12},{12... | collective-permute-start | bytes 589832 | tf_op jit(solution)/shard_map/ppermute | solution.py:395
  106.2 45.4 %collective-permute-start.35 = (bf16[256,1024]{1,0:T(8,128)(2,1)S(1)}, bf16[256,1024]{1,0:T(8,128)(2,1)}, u32[]{:S(2)}, u32[]{:S(2)}) collective-permute-start(bf16[256,1024]{1,0:T(8,128)(2,1)S(1)} %bitcast.417), channel_id=1, source_target_pairs={{0,16},{8,24},{16,0},{24,8},{1,17},{9,25},{17,1},{25,9},{2,18},{10... | collective-permute-start | bytes 1572872 | tf_op jit(solution)/shard_map/ppermute | solution.py:391
  107.1 45.1 %collective-permute-start.34 = (bf16[256,1024]{1,0:T(8,128)(2,1)S(1)}, bf16[256,1024]{1,0:T(8,128)(2,1)}, u32[]{:S(2)}, u32[]{:S(2)}) collective-permute-start(bf16[256,1024]{1,0:T(8,128)(2,1)S(1)} %bitcast.418), channel_id=1, source_target_pairs={{0,8},{8,0},{16,24},{24,16},{1,9},{9,1},{17,25},{25,17},{2,10},{10... | collective-permute-start | bytes 1572872 | tf_op jit(solution)/shard_map/ppermute | solution.py:391
  109.9 20.8 %collective-permute-start.43 = (bf16[2,32,1536]{2,1,0:T(8,128)(2,1)S(1)}, bf16[2,32,1536]{2,1,0:T(8,128)(2,1)S(1)}, u32[]{:S(2)}, u32[]{:S(2)}) collective-permute-start(bf16[2,32,1536]{2,1,0:T(8,128)(2,1)S(1)} %collective-permute-done.41), channel_id=1, source_target_pairs={{0,2},{2,4},{4,6},{6,7},{7,5},{5,3},{3,1},{1,0},{8,10},{10,12},{12... | collective-permute-start | bytes 589832 | tf_op jit(solution)/shard_map/ppermute | solution.py:395
  111.7 21.7 %collective-permute-start.44 = (bf16[2,32,1536]{2,1,0:T(8,128)(2,1)S(1)}, bf16[2,32,1536]{2,1,0:T(8,128)(2,1)S(1)}, u32[]{:S(2)}, u32[]{:S(2)}) collective-permute-start(bf16[2,32,1536]{2,1,0:T(8,128)(2,1)S(1)} %collective-permute-done.42), channel_id=1, source_target_pairs={{2,0},{4,2},{6,4},{7,6},{5,7},{3,5},{1,3},{0,1},{10,8},{12,10},{14... | collective-permute-start | bytes 589832 | tf_op jit(solution)/shard_map/ppermute | solution.py:399
  136.2 30.9 %collective-permute-start.37 = (bf16[256,1536]{1,0:T(8,128)(2,1)}, bf16[256,1536]{1,0:T(8,128)(2,1)S(1)}, u32[]{:S(2)}, u32[]{:S(2)}) collective-permute-start(bf16[256,1536]{1,0:T(8,128)(2,1)} %pad_maximum_fusion.5), channel_id=1, source_target_pairs={{0,8},{8,0},{16,24},{24,16},{1,9},{9,1},{17,25},{25,17},{2,10},{10... | collective-permute-start | bytes 2359304 | tf_op jit(solution)/shard_map/ppermute | solution.py:391
  152.2 17.9 %collective-permute-start.31 = (bf16[256,1024]{1,0:T(8,128)(2,1)}, bf16[256,1024]{1,0:T(8,128)(2,1)}, u32[]{:S(2)}, u32[]{:S(2)}) collective-permute-start(bf16[256,1024]{1,0:T(8,128)(2,1)} %multiply_convert_fusion), channel_id=1, source_target_pairs={{0,8},{8,0},{16,24},{24,16},{1,9},{9,1},{17,25},{25,17},{2,10},{10... | collective-permute-start | bytes 1572872 | tf_op jit(solution)/shard_map/ppermute | solution.py:391
  202.1 25.6 %collective-permute-start.49 = (bf16[256,1024]{1,0:T(8,128)(2,1)S(1)}, bf16[256,1024]{1,0:T(8,128)(2,1)S(1)}, u32[]{:S(2)}, u32[]{:S(2)}) collective-permute-start(bf16[256,1024]{1,0:T(8,128)(2,1)S(1)} %get-tuple-element.86), channel_id=1, source_target_pairs={{0,8},{8,0},{16,24},{24,16},{1,9},{9,1},{17,25},{25,17},{2,10},{10... | collective-permute-start | bytes 1572872 | tf_op jit(solution)/shard_map/ppermute | solution.py:391
  207.8 16.9 %collective-permute-start.108 = (bf16[4,2,16,1536]{3,2,1,0:T(8,128)(2,1)S(1)}, bf16[4,2,16,1536]{3,2,1,0:T(8,128)(2,1)S(1)}, u32[]{:S(2)}, u32[]{:S(2)}) collective-permute-start(bf16[4,2,16,1536]{3,2,1,0:T(8,128)(2,1)S(1)} %pad_maximum_fusion.11), channel_id=1, source_target_pairs={{2,0},{4,2},{6,4},{7,6},{5,7},{3,5},{1,3},{0,1},{10,8},{12,10},{14... | collective-permute-start | bytes 1179656 | tf_op jit(solution)/shard_map/ppermute | solution.py:399
  224.7 18.8 %collective-permute-start.48 = (bf16[256,1024]{1,0:T(8,128)(2,1)S(1)}, bf16[256,1024]{1,0:T(8,128)(2,1)S(1)}, u32[]{:S(2)}, u32[]{:S(2)}) collective-permute-start(bf16[256,1024]{1,0:T(8,128)(2,1)S(1)} %get-tuple-element.85), channel_id=1, source_target_pairs={{0,8},{8,0},{16,24},{24,16},{1,9},{9,1},{17,25},{25,17},{2,10},{10... | collective-permute-start | bytes 1572872 | tf_op jit(solution)/shard_map/ppermute | solution.py:391
  236.5 19.0 %collective-permute-start.125 = (bf16[2,48,1024]{2,1,0:T(8,128)(2,1)S(1)}, bf16[2,48,1024]{2,1,0:T(8,128)(2,1)S(1)}, u32[]{:S(2)}, u32[]{:S(2)}) collective-permute-start(bf16[2,48,1024]{2,1,0:T(8,128)(2,1)S(1)} %get-tuple-element.89), channel_id=1, source_target_pairs={{0,2},{2,4},{4,6},{6,7},{7,5},{5,3},{3,1},{1,0},{8,10},{10,12},{12... | collective-permute-start | bytes 589832 | tf_op jit(solution)/shard_map/ppermute | solution.py:395
  239.2 16.4 %collective-permute-start.129 = (bf16[2,48,1024]{2,1,0:T(8,128)(2,1)S(1)}, bf16[2,48,1024]{2,1,0:T(8,128)(2,1)S(1)}, u32[]{:S(2)}, u32[]{:S(2)}) collective-permute-start(bf16[2,48,1024]{2,1,0:T(8,128)(2,1)S(1)} %get-tuple-element.90), channel_id=1, source_target_pairs={{2,0},{4,2},{6,4},{7,6},{5,7},{3,5},{1,3},{0,1},{10,8},{12,10},{14... | collective-permute-start | bytes 589832 | tf_op jit(solution)/shard_map/ppermute | solution.py:399
  256.6 18.0 %collective-permute-start.54 = (bf16[256,1024]{1,0:T(8,128)(2,1)S(1)}, bf16[256,1024]{1,0:T(8,128)(2,1)S(1)}, u32[]{:S(2)}, u32[]{:S(2)}) collective-permute-start(bf16[256,1024]{1,0:T(8,128)(2,1)S(1)} %get-tuple-element.63), channel_id=1, source_target_pairs={{0,8},{8,0},{16,24},{24,16},{1,9},{9,1},{17,25},{25,17},{2,10},{10... | collective-permute-start | bytes 1572872 | tf_op jit(solution)/shard_map/ppermute | solution.py:391
  269.4 63.1 %collective-permute-start.131 = (bf16[2,48,1024]{2,1,0:T(8,128)(2,1)S(1)}, bf16[2,48,1024]{2,1,0:T(8,128)(2,1)S(1)}, u32[]{:S(2)}, u32[]{:S(2)}) collective-permute-start(bf16[2,48,1024]{2,1,0:T(8,128)(2,1)S(1)} %fusion.11.refs_0_), channel_id=1, source_target_pairs={{2,0},{4,2},{6,4},{7,6},{5,7},{3,5},{1,3},{0,1},{10,8},{12,10},{14... | collective-permute-start | bytes 589832 | tf_op jit(solution)/shard_map/ppermute | solution.py:399
  273.5 60.7 %collective-permute-start.132 = (bf16[2,48,1024]{2,1,0:T(8,128)(2,1)S(1)}, bf16[2,48,1024]{2,1,0:T(8,128)(2,1)S(1)}, u32[]{:S(2)}, u32[]{:S(2)}) collective-permute-start(bf16[2,48,1024]{2,1,0:T(8,128)(2,1)S(1)} %collective-permute-done.130.refs_1_), channel_id=1, source_target_pairs={{0,2},{2,4},{4,6},{6,7},{7,5},{5,3},{3,1},{1,0},{8,10},{10,12},{12... | collective-permute-start | bytes 589832 | tf_op jit(solution)/shard_map/ppermute | solution.py:395
  276.0 39.0 %collective-permute-start.84 = (bf16[1,32,1024]{2,1,0:T(8,128)(2,1)S(1)}, bf16[1,32,1024]{2,1,0:T(8,128)(2,1)S(1)}, u32[]{:S(2)}, u32[]{:S(2)}) collective-permute-start(bf16[1,32,1024]{2,1,0:T(8,128)(2,1)S(1)} %get-tuple-element.113), channel_id=1, source_target_pairs={{0,2},{2,4},{4,6},{6,7},{7,5},{5,3},{3,1},{1,0},{8,10},{10,12},{12... | collective-permute-start | bytes 196616 | tf_op jit(solution)/shard_map/ppermute | solution.py:395
  277.7 37.8 %collective-permute-start.88 = (bf16[1,32,1024]{2,1,0:T(8,128)(2,1)S(1)}, bf16[1,32,1024]{2,1,0:T(8,128)(2,1)S(1)}, u32[]{:S(2)}, u32[]{:S(2)}) collective-permute-start(bf16[1,32,1024]{2,1,0:T(8,128)(2,1)S(1)} %get-tuple-element.115), channel_id=1, source_target_pairs={{2,0},{4,2},{6,4},{7,6},{5,7},{3,5},{1,3},{0,1},{10,8},{12,10},{14... | collective-permute-start | bytes 196616 | tf_op jit(solution)/shard_map/ppermute | solution.py:399
  313.4 39.9 %collective-permute-start.114 = (bf16[4,2,16,1536]{3,2,1,0:T(8,128)(2,1)S(1)}, bf16[4,2,16,1536]{3,2,1,0:T(8,128)(2,1)S(1)}, u32[]{:S(2)}, u32[]{:S(2)}) collective-permute-start(bf16[4,2,16,1536]{3,2,1,0:T(8,128)(2,1)S(1)} %pad_maximum_fusion.12.refs_0_), channel_id=1, source_target_pairs={{0,2},{2,4},{4,6},{6,7},{7,5},{5,3},{3,1},{1,0},{8,10},{10,12},{12... | collective-permute-start | bytes 1179656 | tf_op jit(solution)/shard_map/ppermute | solution.py:395
  328.2 26.6 %collective-permute-start.115 = (bf16[4,2,16,1536]{3,2,1,0:T(8,128)(2,1)S(1)}, bf16[4,2,16,1536]{3,2,1,0:T(8,128)(2,1)S(1)}, u32[]{:S(2)}, u32[]{:S(2)}) collective-permute-start(bf16[4,2,16,1536]{3,2,1,0:T(8,128)(2,1)S(1)} %pad_maximum_fusion.12.refs_0_), channel_id=1, source_target_pairs={{2,0},{4,2},{6,4},{7,6},{5,7},{3,5},{1,3},{0,1},{10,8},{12,10},{14... | collective-permute-start | bytes 1179656 | tf_op jit(solution)/shard_map/ppermute | solution.py:399
  334.2 21.0 %collective-permute-start.70 = (bf16[4,2,16,1024]{3,2,1,0:T(8,128)(2,1)S(1)}, bf16[4,2,16,1024]{3,2,1,0:T(8,128)(2,1)S(1)}, u32[]{:S(2)}, u32[]{:S(2)}) collective-permute-start(bf16[4,2,16,1024]{3,2,1,0:T(8,128)(2,1)S(1)} %pad_maximum_fusion.16), channel_id=1, source_target_pairs={{2,0},{4,2},{6,4},{7,6},{5,7},{3,5},{1,3},{0,1},{10,8},{12,10},{14... | collective-permute-start | bytes 786440 | tf_op jit(solution)/shard_map/ppermute | solution.py:399
  353.3 19.1 %collective-permute-start.116 = (bf16[4,2,16,1536]{3,2,1,0:T(8,128)(2,1)S(1)}, bf16[4,2,16,1536]{3,2,1,0:T(8,128)(2,1)S(1)}, u32[]{:S(2)}, u32[]{:S(2)}) collective-permute-start(bf16[4,2,16,1536]{3,2,1,0:T(8,128)(2,1)S(1)} %collective-permute-done.114.refs_1_), channel_id=1, source_target_pairs={{0,2},{2,4},{4,6},{6,7},{7,5},{5,3},{3,1},{1,0},{8,10},{10,12},{12... | collective-permute-start | bytes 1179656 | tf_op jit(solution)/shard_map/ppermute | solution.py:395
  354.8 18.5 %collective-permute-start.117 = (bf16[4,2,16,1536]{3,2,1,0:T(8,128)(2,1)S(1)}, bf16[4,2,16,1536]{3,2,1,0:T(8,128)(2,1)S(1)}, u32[]{:S(2)}, u32[]{:S(2)}) collective-permute-start(bf16[4,2,16,1536]{3,2,1,0:T(8,128)(2,1)S(1)} %collective-permute-done.115.refs_2_), channel_id=1, source_target_pairs={{2,0},{4,2},{6,4},{7,6},{5,7},{3,5},{1,3},{0,1},{10,8},{12,10},{14... | collective-permute-start | bytes 1179656 | tf_op jit(solution)/shard_map/ppermute | solution.py:399
  382.9 17.9 %collective-permute-start.58 = (bf16[256,1024]{1,0:T(8,128)(2,1)S(1)}, bf16[256,1024]{1,0:T(8,128)(2,1)S(1)}, u32[]{:S(2)}, u32[]{:S(2)}) collective-permute-start(bf16[256,1024]{1,0:T(8,128)(2,1)S(1)} %get-tuple-element.82), channel_id=1, source_target_pairs={{0,8},{8,0},{16,24},{24,16},{1,9},{9,1},{17,25},{25,17},{2,10},{10... | collective-permute-start | bytes 1572872 | tf_op jit(solution)/shard_map/ppermute | solution.py:391
  403.6 32.5 %collective-permute-start.57 = (bf16[256,1024]{1,0:T(8,128)(2,1)}, bf16[256,1024]{1,0:T(8,128)(2,1)}, u32[]{:S(2)}, u32[]{:S(2)}) collective-permute-start(bf16[256,1024]{1,0:T(8,128)(2,1)} %get-tuple-element.81), channel_id=1, source_target_pairs={{0,8},{8,0},{16,24},{24,16},{1,9},{9,1},{17,25},{25,17},{2,10},{10... | collective-permute-start | bytes 1572872 | tf_op jit(solution)/shard_map/ppermute | solution.py:391
  405.4 30.7 %collective-permute-start.59 = (bf16[256,1024]{1,0:T(8,128)(2,1)}, bf16[256,1024]{1,0:T(8,128)(2,1)}, u32[]{:S(2)}, u32[]{:S(2)}) collective-permute-start(bf16[256,1024]{1,0:T(8,128)(2,1)} %slice_add_fusion.1), channel_id=1, source_target_pairs={{0,16},{8,24},{16,0},{24,8},{1,17},{9,25},{17,1},{25,9},{2,18},{10... | collective-permute-start | bytes 1572872 | tf_op jit(solution)/shard_map/ppermute | solution.py:391
  409.6 17.4 %collective-permute-start.76 = (bf16[4,2,16,1024]{3,2,1,0:T(8,128)(2,1)S(1)}, bf16[4,2,16,1024]{3,2,1,0:T(8,128)(2,1)}, u32[]{:S(2)}, u32[]{:S(2)}) collective-permute-start(bf16[4,2,16,1024]{3,2,1,0:T(8,128)(2,1)S(1)} %pad_maximum_fusion.17.refs_0_), channel_id=1, source_target_pairs={{0,2},{2,4},{4,6},{6,7},{7,5},{5,3},{3,1},{1,0},{8,10},{10,12},{12... | collective-permute-start | bytes 786440 | tf_op jit(solution)/shard_map/ppermute | solution.py:395
  411.1 17.2 %collective-permute-start.77 = (bf16[4,2,16,1024]{3,2,1,0:T(8,128)(2,1)S(1)}, bf16[4,2,16,1024]{3,2,1,0:T(8,128)(2,1)}, u32[]{:S(2)}, u32[]{:S(2)}) collective-permute-start(bf16[4,2,16,1024]{3,2,1,0:T(8,128)(2,1)S(1)} %pad_maximum_fusion.17.refs_0_), channel_id=1, source_target_pairs={{2,0},{4,2},{6,4},{7,6},{5,7},{3,5},{1,3},{0,1},{10,8},{12,10},{14... | collective-permute-start | bytes 786440 | tf_op jit(solution)/shard_map/ppermute | solution.py:399
  (157 other events, 1414.2 us)

commit v2 on v1

v2 whole, which is shorter than its diff:
```python
import functools
import math

import jax
import jax.numpy as jnp
from jax import lax
from jax.experimental import pallas as pl
from jax.experimental.pallas import tpu as pltpu
from jax.sharding import PartitionSpec as P

eps_norm = 1e-06
theta_base = 1000000.0
f32 = jnp.float32
bf16 = jnp.bfloat16
vmem_bytes = 50 * 1024 * 1024


def dot(left, right):
    return lax.dot_general(left, right, (((1,), (0,)), ((), ())), preferred_element_type=f32)


def dot_nt(left, right):
    return lax.dot_general(left, right, (((1,), (1,)), ((), ())), preferred_element_type=f32)


def dot_tn(left, right):
    return lax.dot_general(left, right, (((0,), (0,)), ((), ())), preferred_element_type=f32)


def inverse_root(rows):
    return lax.rsqrt(jnp.mean(rows * rows, axis=-1, keepdims=True) + eps_norm)


def norm_back(grad, rows, scale):
    return scale * grad - rows * (scale * scale * scale) * jnp.mean(
        grad * rows, axis=-1, keepdims=True
    )


def params():
    return pltpu.CompilerParams(vmem_limit_bytes=vmem_bytes)


def cost(flops, moved, trans=0):
    return pl.CostEstimate(flops=int(flops), bytes_accessed=int(moved), transcendentals=int(trans))


def half_turn(rows):
    return pltpu.roll(rows, rows.shape[-1] // 2, axis=1)


def pick(refs, held):
    for k, ref in enumerate(refs):

        @pl.when(pl.program_id(0) == k)
        def _(ref=ref):
            held[...] = ref[...]


def project_kernel(
    q_heads, k_heads, count, gain, weight, cosine, sine, gains, *refs
):
    tok, (normed, lin, rot, val, held) = refs[:count], refs[count:]
    pick(tok, held)
    rows = held[...].astype(f32)
    low = (rows * inverse_root(rows) * gain[...]).astype(bf16)
    normed[...] = low
    head = cosine.shape[1]
    full = dot(low, weight[...])
    cos_, sin_ = cosine[...], sine[...]
    for index in range(q_heads + k_heads):
        part = full[:, index * head : (index + 1) * head]
        lin[:, index * head : (index + 1) * head] = part
        which = 0 if index < q_heads else 1
        unit = part * inverse_root(part) * gains[which : which + 1, :]
        rot[:, index * head : (index + 1) * head] = (unit * cos_ + half_turn(unit) * sin_).astype(
            bf16
        )
    val[...] = full[:, (q_heads + k_heads) * head :].astype(bf16)


def row_block(rows, columns, first=0):
    return pl.BlockSpec((rows, columns), lambda i: (i + first, 0))


def fixed_block(rows, columns):
    return pl.BlockSpec((rows, columns), lambda i: (0, 0))


def project(tok, gain, weight, cosine, sine, gains, q_heads, k_heads):
    count = len(tok)
    block, width = tok[0].shape
    total = block * count
    head = cosine.shape[1]
    qk = (q_heads + k_heads) * head
    kv = k_heads * head
    return pl.pallas_call(
        functools.partial(project_kernel, q_heads, k_heads, count),
        grid=(count,),
        in_specs=[
            fixed_block(1, width),
            fixed_block(*weight.shape),
            row_block(block, head),
            row_block(block, head),
            fixed_block(2, head),
        ]
        + [fixed_block(block, width)] * count,
        out_specs=[row_block(block, n) for n in (width, qk, qk, kv)],
        out_shape=[
            jax.ShapeDtypeStruct((total, width), bf16),
            jax.ShapeDtypeStruct((total, qk), f32),
            jax.ShapeDtypeStruct((total, qk), bf16),
            jax.ShapeDtypeStruct((total, kv), bf16),
        ],
        scratch_shapes=[pltpu.VMEM((block, width), bf16)],
        compiler_params=params(),
        cost_estimate=cost(2 * total * weight.size, 2 * weight.size + total * width * 12),
    )(gain, weight, cosine, sine, gains, *tok)


def allowed_pairs(j, k, start_q, start_k, block, seg_col, seg_row):
    own = seg_col[pl.ds(start_q, block), :]
    other = seg_row[:, pl.ds(start_k, block)]
    allowed = own == other
    if j == k:
        at_q = lax.broadcasted_iota(jnp.int32, (block, block), 0)
        at_k = lax.broadcasted_iota(jnp.int32, (block, block), 1)
        allowed = allowed & (at_q >= at_k)
    return allowed


def attend_kernel(blocks, group, factor, order, query, key, val, seg_col, seg_row, out, low, logs):
    total, head = key.shape
    block = total // blocks
    flip = order[0]
    start = [pl.multiple_of((jnp.int32(i) ^ flip) * block, block) for i in range(blocks)]
    ones = jnp.ones((block, head), bf16)
    for j in range(blocks):
        stacked = jnp.concatenate(
            [query[pl.ds(start[j], block), h * head : (h + 1) * head] for h in range(group)], axis=0
        )
        acc = jnp.zeros((group * block, 2 * head), f32)
        for k in range(j + 1):
            raw = dot_nt(stacked, key[pl.ds(start[k], block), :])
            allowed = allowed_pairs(j, k, start[j], start[k], block, seg_col, seg_row)
            allowed = jnp.concatenate([allowed] * group, axis=0)
            probs = jnp.where(allowed, jnp.exp2(raw * factor), 0.0).astype(bf16)
            both = jnp.concatenate([val[pl.ds(start[k], block), :], ones], axis=1)
            acc = acc + dot(probs, both)
        sums = acc[:, head:]
        result = acc[:, :head] / sums
        log_sums = jnp.log2(sums)
        for h in range(group):
            out[pl.ds(start[j], block), h * head : (h + 1) * head] = result[
                h * block : (h + 1) * block
            ]
            low[pl.ds(start[j], block), h * head : (h + 1) * head] = result[
                h * block : (h + 1) * block
            ].astype(bf16)
            logs[pl.ds(start[j], block), h * head : (h + 1) * head] = log_sums[
                h * block : (h + 1) * block
            ]


def attend(order, rot, val, seg_col, seg_row, q_heads, k_heads, head, blocks):
    total = rot.shape[0]
    group = q_heads // k_heads
    factor = head**-0.5 * math.log2(math.e)
    wide = pl.BlockSpec((total, group * head), lambda g, o: (0, g))
    return pl.pallas_call(
        functools.partial(attend_kernel, blocks, group, factor),
        grid_spec=pltpu.PrefetchScalarGridSpec(
            num_scalar_prefetch=1,
            grid=(k_heads,),
            in_specs=[
                wide,
                pl.BlockSpec((total, head), lambda g, o: (0, q_heads + g)),
                pl.BlockSpec((total, head), lambda g, o: (0, g)),
                pl.BlockSpec((total, 1), lambda g, o: (0, 0)),
                pl.BlockSpec((1, total), lambda g, o: (0, 0)),
            ],
            out_specs=[wide, wide, wide],
        ),
        out_shape=[jax.ShapeDtypeStruct((total, q_heads * head), kind) for kind in (f32, bf16, f32)],
        compiler_params=params(),
        cost_estimate=cost(4 * total * total * q_heads * head, total * q_heads * head * 12),
    )(order, rot, rot, val, seg_col, seg_row)


def attend_back_kernel(
    blocks, group, factor, scale, order, query, key, val, out_grad, out, logs, seg_col, seg_row,
    query_grad, key_grad, val_grad,
):
    total, head = key.shape
    block = total // blocks
    flip = order[0]
    start = [pl.multiple_of((jnp.int32(i) ^ flip) * block, block) for i in range(blocks)]

    def heads_of(ref, at):
        return jnp.concatenate(
            [ref[pl.ds(at, block), h * head : (h + 1) * head] for h in range(group)], axis=0
        )

    deltas = []
    for j in range(blocks):
        product = heads_of(out_grad, start[j]).astype(f32) * heads_of(out, start[j])
        deltas.append(jnp.sum(product, axis=1, keepdims=True))
    sums = [None] * blocks
    for k in range(blocks):
        key_block = key[pl.ds(start[k], block), :]
        val_block = val[pl.ds(start[k], block), :]
        key_sum = jnp.zeros((block, head), f32)
        val_sum = jnp.zeros((block, head), f32)
        for j in range(k, blocks):
            stacked = heads_of(query, start[j])
            grads = heads_of(out_grad, start[j])
            logged = heads_of(logs, start[j])
            logged = jnp.concatenate([logged] * (block // head), axis=1)
            raw = dot_nt(stacked, key_block)
            allowed = allowed_pairs(j, k, start[j], start[k], block, seg_col, seg_row)
            allowed = jnp.concatenate([allowed] * group, axis=0)
            probs = jnp.where(allowed, jnp.exp2(raw * factor - logged), 0.0)
            prob_grad = dot_nt(grads, val_block)
            score_grad = (probs * (prob_grad - deltas[j]) * scale).astype(bf16)
            val_sum = val_sum + dot_tn(probs.astype(bf16), grads)
            key_sum = key_sum + dot_tn(score_grad, stacked)
            piece = dot(score_grad, key_block)
            sums[j] = piece if k == 0 else sums[j] + piece
        key_grad[pl.ds(start[k], block), :] = key_sum
        val_grad[pl.ds(start[k], block), :] = val_sum
        for h in range(group):
            query_grad[pl.ds(start[k], block), h * head : (h + 1) * head] = sums[k][
                h * block : (h + 1) * block
            ]


def attend_back(order, rot, val, out_grad, out, logs, seg_col, seg_row, q_heads, k_heads, head, blocks):
    total = rot.shape[0]
    group = q_heads // k_heads
    scale = head**-0.5
    wide = pl.BlockSpec((total, group * head), lambda g, o: (0, g))
    thin = pl.BlockSpec((total, head), lambda g, o: (0, g))
    return pl.pallas_call(
        functools.partial(attend_back_kernel, blocks, group, scale * math.log2(math.e), scale),
        grid_spec=pltpu.PrefetchScalarGridSpec(
            num_scalar_prefetch=1,
            grid=(k_heads,),
            in_specs=[
                wide,
                pl.BlockSpec((total, head), lambda g, o: (0, q_heads + g)),
                thin,
                wide,
                wide,
                wide,
                pl.BlockSpec((total, 1), lambda g, o: (0, 0)),
                pl.BlockSpec((1, total), lambda g, o: (0, 0)),
            ],
            out_specs=[wide, thin, thin],
        ),
        out_shape=[
            jax.ShapeDtypeStruct((total, q_heads * head), f32),
            jax.ShapeDtypeStruct((total, k_heads * head), f32),
            jax.ShapeDtypeStruct((total, k_heads * head), f32),
        ],
        compiler_params=params(),
        cost_estimate=cost(10 * total * total * q_heads * head, total * q_heads * head * 20),
    )(order, rot, rot, val, out_grad, out, logs, seg_col, seg_row)


def feed_kernel(count, kept, weight, down, *refs):
    norm, cot = refs[:count], refs[count : 2 * count]
    hidden, gate_out, up_out, norm_all, cot_all, norm_grad, out, low_held, cot_held = refs[
        2 * count + kept :
    ]
    pick(norm, low_held)
    pick(cot, cot_held)
    units = down.shape[0]
    low = low_held[...]
    norm_all[...] = low
    cot_all[...] = cot_held[...]
    gate = dot(low, weight[:, :units])
    upper = dot(low, weight[:, units:])
    sigma = 1.0 / (1.0 + jnp.exp(-gate))
    silu = gate * sigma
    hid = (silu * upper).astype(bf16)
    hidden[...] = hid
    back = dot_nt(cot_held[...], down[...])
    gate_grad = (back * upper * sigma * (1.0 + gate * (1.0 - sigma))).astype(bf16)
    up_grad = (back * silu).astype(bf16)
    gate_out[...] = gate_grad
    up_out[...] = up_grad
    norm_grad[...] = (
        dot_nt(gate_grad, weight[:, :units]) + dot_nt(up_grad, weight[:, units:])
    ).astype(bf16)
    out[...] = dot(hid, down[...]).astype(bf16)


def feed(norm, cot, weight, down, first, blocks, before):
    count = len(norm)
    block, width = norm[0].shape
    total = block * blocks
    units = down.shape[0]
    kept = [units, units, units, width, width]
    return pl.pallas_call(
        functools.partial(feed_kernel, count, len(before)),
        grid=(count,),
        in_specs=[fixed_block(*weight.shape), fixed_block(*down.shape)]
        + [fixed_block(block, width)] * (2 * count)
        + [pl.BlockSpec(memory_space=pl.ANY)] * len(before),
        out_specs=[row_block(block, n, first) for n in kept] + [row_block(block, width)] * 2,
        out_shape=[jax.ShapeDtypeStruct((total, n), bf16) for n in kept]
        + [jax.ShapeDtypeStruct((block * count, width), bf16)] * 2,
        scratch_shapes=[pltpu.VMEM((block, width), bf16)] * 2,
        input_output_aliases={2 + 2 * count + i: i for i in range(len(before))},
        compiler_params=params(),
        cost_estimate=cost(
            12 * block * count * down.size, 6 * down.size + block * count * width * 16,
            block * count * units,
        ),
    )(weight, down, *norm, *cot, *before)


def branch_kernel(count, weight, *refs):
    branch, (out_grad, branch_all, held) = refs[:count], refs[count:]
    pick(branch, held)
    low = held[...]
    branch_all[...] = low
    out_grad[...] = dot_nt(low, weight[...]).astype(bf16)


def branch_back(branch, weight):
    count = len(branch)
    block, width = branch[0].shape
    total = block * count
    return pl.pallas_call(
        functools.partial(branch_kernel, count),
        grid=(count,),
        in_specs=[fixed_block(*weight.shape)] + [fixed_block(block, width)] * count,
        out_specs=[row_block(block, weight.shape[0]), row_block(block, width)],
        out_shape=[
            jax.ShapeDtypeStruct((total, weight.shape[0]), bf16),
            jax.ShapeDtypeStruct((total, width), bf16),
        ],
        scratch_shapes=[pltpu.VMEM((block, width), bf16)],
        compiler_params=params(),
        cost_estimate=cost(2 * total * weight.size, 2 * weight.size + total * width * 6),
    )(weight, *branch)


def unproject_kernel(
    q_heads, k_heads, count, query_grad, key_grad, val_grad, lin, cosine, sine, gains, weight, *refs
):
    tok, (query_out, pair_out, norm_grad, gain_sum, head_sum, held) = refs[:count], refs[count:]
    pick(tok, held)
    head = cosine.shape[1]
    cos_, sin_ = cosine[...], sine[...]
    sums = [jnp.zeros((1, head), f32), jnp.zeros((1, head), f32)]
    for index in range(q_heads + k_heads):
        which = 0 if index < q_heads else 1
        ref, result, spot = (
            (query_grad, query_out, index) if which == 0 else (key_grad, pair_out, index - q_heads)
        )
        turned = ref[:, spot * head : (spot + 1) * head]
        grad = turned * cos_ - half_turn(turned) * sin_
        rows = lin[:, index * head : (index + 1) * head]
        scale = inverse_root(rows)
        sums[which] = sums[which] + jnp.sum(grad * rows * scale, axis=0, keepdims=True)
        result[:, spot * head : (spot + 1) * head] = norm_back(
            grad * gains[which : which + 1, :], rows, scale
        ).astype(bf16)
    pair_out[:, k_heads * head :] = val_grad[...].astype(bf16)
    normed_grad = dot_nt(query_out[...], weight[:, : q_heads * head]) + dot_nt(
        pair_out[...], weight[:, q_heads * head :]
    )
    norm_grad[...] = normed_grad.astype(bf16)
    rows = held[...].astype(f32)
    gain_part = jnp.sum(normed_grad * rows * inverse_root(rows), axis=0, keepdims=True)

    @pl.when(pl.program_id(0) == 0)
    def _():
        gain_sum[...] = jnp.zeros_like(gain_sum)
        head_sum[...] = jnp.zeros_like(head_sum)

    gain_sum[...] += gain_part
    head_sum[...] += jnp.concatenate(sums, axis=0)


def unproject(query_grad, key_grad, val_grad, lin, cosine, sine, gains, weight, tok, q_heads, k_heads):
    count = len(tok)
    block, width = tok[0].shape
    total = block * count
    head = cosine.shape[1]
    q_width, kv_width = q_heads * head, 2 * k_heads * head
    return pl.pallas_call(
        functools.partial(unproject_kernel, q_heads, k_heads, count),
        grid=(count,),
        in_specs=[
            row_block(block, q_width),
            row_block(block, k_heads * head),
            row_block(block, k_heads * head),
            row_block(block, (q_heads + k_heads) * head),
            row_block(block, head),
            row_block(block, head),
            fixed_block(2, head),
            fixed_block(*weight.shape),
        ]
        + [fixed_block(block, width)] * count,
        out_specs=[
            row_block(block, q_width), row_block(block, kv_width), row_block(block, width),
            fixed_block(1, width), fixed_block(2, head),
        ],
        out_shape=[
            jax.ShapeDtypeStruct((total, q_width), bf16),
            jax.ShapeDtypeStruct((total, kv_width), bf16),
            jax.ShapeDtypeStruct((total, width), bf16),
            jax.ShapeDtypeStruct((1, width), f32),
            jax.ShapeDtypeStruct((2, head), f32),
        ],
        scratch_shapes=[pltpu.VMEM((block, width), bf16)],
        compiler_params=params(),
        cost_estimate=cost(2 * total * weight.size, 2 * weight.size + total * width * 16),
    )(query_grad, key_grad, val_grad, lin, cosine, sine, gains, weight, *tok)


def place_kernel(count, outs, moves, scalars, *refs):
    inputs, results = refs[:count], refs[count:]
    values = [scalars[i] for i in range(scalars.shape[0])]
    for source, index, rows, columns, target, spot in moves:
        piece = inputs[source][index + (slice(rows[0], rows[1]), slice(columns[0], columns[1]))]
        row, column = spot(*values)
        results[target][
            pl.ds(pl.multiple_of(row, 16), rows[1] - rows[0]),
            pl.ds(pl.multiple_of(column, 128), columns[1] - columns[0]),
        ] = piece.astype(results[target].dtype)


def place(scalars, inputs, out_shapes, moves):
    moved = sum(item.size * 2 for item in inputs) + sum(
        math.prod(shape) * (4 if kind == f32 else 2) for shape, kind in out_shapes
    )
    whole = pl.BlockSpec(memory_space=pltpu.VMEM)
    return pl.pallas_call(
        functools.partial(place_kernel, len(inputs), len(out_shapes), moves),
        in_specs=[pl.BlockSpec(memory_space=pltpu.SMEM)] + [whole] * len(inputs),
        out_specs=[whole] * len(out_shapes),
        out_shape=[jax.ShapeDtypeStruct(shape, kind) for shape, kind in out_shapes],
        compiler_params=params(),
        cost_estimate=cost(0, moved),
    )(scalars, *inputs)


def cut_kernel(sizes, scalars, *refs):
    inputs, (own, near, piece) = refs[: len(sizes)], refs[len(sizes) :]
    mine, y = scalars[0], scalars[1]
    half = piece.shape[1]
    begin = 0
    for ref, size in zip(inputs, sizes):
        lanes = lambda i: pl.ds(pl.multiple_of((mine ^ i) * size, 128), size)
        rows = pl.ds(pl.multiple_of(y * half, 16), half)
        own[:, begin : begin + size] = ref[:, lanes(0)]
        near[:, begin : begin + size] = ref[:, lanes(1)]
        piece[0, :, begin : begin + size] = ref[rows, lanes(2)]
        piece[1, :, begin : begin + size] = ref[rows, lanes(3)]
        begin += size


def cut(scalars, inputs, sizes):
    rows = inputs[0].shape[0]
    wide = sum(sizes)
    whole = pl.BlockSpec(memory_space=pltpu.VMEM)
    shapes = [(rows, wide), (rows, wide), (2, rows // 2, wide)]
    return pl.pallas_call(
        functools.partial(cut_kernel, sizes),
        in_specs=[pl.BlockSpec(memory_space=pltpu.SMEM)] + [whole] * len(inputs),
        out_specs=[whole] * 3,
        out_shape=[jax.ShapeDtypeStruct(shape, bf16) for shape in shapes],
        compiler_params=params(),
        cost_estimate=cost(0, 4 * sum(item.size for item in inputs)),
    )(scalars, *inputs)


def ring_kernel(layout, plan, count, sets, chunks, *refs):
    local = [refs[i * count : (i + 1) * count] for i in range(sets)]
    arrived = refs[sets * count : len(refs) - len(plan)]
    results = refs[len(refs) - len(plan) :]
    for result, (which, halves, adds) in zip(results, plan):
        for source, block, lane, size, to_block, to_lane in layout:
            for at, half in enumerate(halves):
                value = local[which][source][block, 0, half, :, lane : lane + size].astype(f32)
                for index, held in adds:
                    if half in held:
                        value = value + arrived[index][
                            to_block, held.index(half), :, to_lane : to_lane + size
                        ].astype(f32)
                result[to_block, at, :, to_lane : to_lane + size] = value.astype(bf16)


def ring_step(shares, layout, blocks, chunks, plan, arrived):
    lines, lanes = shares[0].shape[3], blocks[1]
    specs = []
    for which in range(len(chunks)):
        for share in shares:
            shape = (share.shape[0], 1) + share.shape[2:]
            specs.append(
                pl.BlockSpec(shape, lambda i, c, which=which: (0, c[which], 0, 0, 0))
            )
    whole = lambda shape: pl.BlockSpec(shape, lambda i, c: (0,) * len(shape))
    shapes = [(blocks[0], len(halves), lines, lanes) for _, halves, _ in plan]
    return pl.pallas_call(
        functools.partial(ring_kernel, layout, plan, len(shares), len(chunks)),
        grid_spec=pltpu.PrefetchScalarGridSpec(
            num_scalar_prefetch=1,
            grid=(1,),
            in_specs=specs + [whole(item.shape) for item in arrived],
            out_specs=[whole(shape) for shape in shapes],
        ),
        out_shape=[jax.ShapeDtypeStruct(shape, bf16) for shape in shapes],
        compiler_params=params(),
        cost_estimate=cost(0, 6 * sum(math.prod(shape) for shape in shapes)),
    )(jnp.stack(chunks).astype(jnp.int32), *shares * len(chunks), *arrived)


def split_kernel(pieces, scalars, chunk, own, near, far):
    mine = scalars[0]
    for i, (result, spot) in enumerate([(own, 0), (near, 0), (far, 0), (near, 1)]):
        begin = 0
        for block, lane, size in pieces(mine ^ i):
            result[spot, :, :, begin : begin + size] = chunk[
                block, :, :, pl.ds(pl.multiple_of(lane, 128), size)
            ]
            begin += size


def split(scalars, chunk, pieces, wide):
    whole = pl.BlockSpec(memory_space=pltpu.VMEM)
    lines = chunk.shape[1:3]
    shapes = [(1, *lines, wide), (2, *lines, wide), (1, *lines, wide)]
    return pl.pallas_call(
        functools.partial(split_kernel, pieces),
        in_specs=[pl.BlockSpec(memory_space=pltpu.SMEM), whole],
        out_specs=[whole] * 3,
        out_shape=[jax.ShapeDtypeStruct(shape, bf16) for shape in shapes],
        compiler_params=params(),
        cost_estimate=cost(0, 4 * chunk.size),
    )(scalars, chunk)


def pack_kernel(layout, *refs):
    inputs, result = refs[:-1], refs[-1]
    for source, block, lane, size, to_block, to_lane in layout:
        result[to_block, :, :, to_lane : to_lane + size] = inputs[source][
            block, :, :, lane : lane + size
        ]


def pack(inputs, layout, shape):
    whole = pl.BlockSpec(memory_space=pltpu.VMEM)
    return pl.pallas_call(
        functools.partial(pack_kernel, layout),
        in_specs=[whole] * len(inputs),
        out_specs=whole,
        out_shape=jax.ShapeDtypeStruct(shape, bf16),
        compiler_params=params(),
        cost_estimate=cost(0, 4 * math.prod(shape)),
    )(*inputs)


class Moves:
    def __init__(self):
        self.shards = lax.axis_size("shard")
        self.reps = lax.axis_size("rep")
        self.mine = lax.axis_index("shard")
        self.direct = self.shards == 4 and self.reps == 8
        self.flip = self.mine if self.direct else jnp.int32(0)
        rep = lax.axis_index("rep")
        self.bits = {1: rep % 2, 2: (rep // 2) % 2, 4: rep // 4}
        self.pos = jnp.where(rep % 2 == 0, rep // 2, 7 - rep // 2)
        self.ring = [0, 2, 4, 6, 7, 5, 3, 1]
        self.scalars = jnp.stack([self.mine, self.bits[1], self.pos]).astype(jnp.int32)

    def up(self, item):
        ring = self.ring
        return lax.ppermute(item, "rep", [(ring[i], ring[(i + 1) % 8]) for i in range(8)])

    def down(self, item):
        ring = self.ring
        return lax.ppermute(item, "rep", [(ring[(i + 1) % 8], ring[i]) for i in range(8)])

    def swap(self, item, mask):
        return lax.ppermute(item, "shard", [(i, i ^ mask) for i in range(4)])

    def cross_rep(self, item, mask):
        return lax.ppermute(item, "rep", [(i, i ^ mask) for i in range(8)])

    def gather(self, item):
        if not self.direct:
            rows = item.shape[0]
            whole = lax.all_gather(item, "shard", axis=0, tiled=True)
            return [whole[i * rows : (i + 1) * rows] for i in range(self.shards)]
        far = self.swap(item, 2)
        near = self.swap(item, 1)
        cross = self.swap(far, 1)
        return [item, near, far, cross]

    def scatter(self, near_part, far_part):
        if not self.direct:
            item = jnp.concatenate([near_part, far_part], axis=0).astype(f32)
            return lax.psum_scatter(item, "shard", scatter_dimension=0, tiled=True)
        rows = near_part.shape[0] // 2
        far = self.swap(far_part[:rows] + self.swap(far_part[rows:], 1), 2)
        near = self.swap(near_part[rows:], 1)
        return near_part[:rows].astype(f32) + near.astype(f32) + far.astype(f32)

    def ring_scatter(self, shares, layout, blocks):
        step = functools.partial(ring_step, shares, layout, blocks)
        chunk = lambda offset: (self.pos + offset) % 8
        both = (0, 1)
        u, d = step([chunk(4)], [(0, (0,), []), (0, (1,), [])], [])
        u, d = self.up(u), self.down(d)
        plan = [(0, both, [(0, (0,))]), (1, both, [(1, (1,))])]
        u, d = step([chunk(3), chunk(5)], plan, [u, d])
        u, d = self.up(u), self.down(d)
        plan = [(0, both, [(0, both)]), (1, both, [(1, both)])]
        u, d = step([chunk(2), chunk(6)], plan, [u, d])
        u, d = self.up(u), self.down(d)
        u, d = step([chunk(1), chunk(7)], plan, [u, d])
        u, d = self.up(u), self.down(d)
        return step([chunk(0)], [(0, both, [(0, both), (1, both)])], [u, d])[0]

    def ring_gather(self, item):
        u1, d1 = self.up(item), self.down(item)
        u2, d2 = self.up(u1), self.down(d1)
        u3, d3 = self.up(u2), self.down(d2)
        u4, d4 = self.up(u3[:, :1]), self.down(d3[:, 1:])
        return [
            (item, 0, None), (u1, -1, None), (d1, 1, None), (u2, -2, None), (d2, 2, None),
            (u3, -3, None), (d3, 3, None), (u4, 4, 0), (d4, 4, 1),
        ]

    def exchange(self, chunk, pieces, wide):
        own, near, far = split(self.scalars, chunk, pieces, wide)
        near = self.swap(near, 1)
        far = self.swap(jnp.concatenate([far, near[1:]], axis=0), 2)
        return own, near, far


class Fetch:
    def __init__(self, moves, own, near, piece, spot, shape):
        self.moves, self.own, self.near, self.piece = moves, own, near, piece
        self.spot, self.shape = spot, shape

    def start(self, *before):
        self.here = self.moves.swap(after(self.piece, *before), 2)
        self.there = self.moves.cross_rep(self.here, 1)

    def finish(self):
        moves, here, there, spot = self.moves, self.here, self.there, self.spot
        rows, width = self.own.shape
        half = rows // 2
        near = moves.swap(self.near, 1)
        inputs = [self.own, near, here, moves.swap(here[1], 1), there, moves.swap(there[1], 1)]
        todo = [
            (0, (), (0, rows), (0, width), 0, lambda shard, *_: spot(shard, 0)),
            (1, (), (0, rows), (0, width), 0, lambda shard, *_: spot(shard ^ 1, 0)),
            (2, (0,), (0, half), (0, width), 0, lambda shard, y, *_: spot(shard ^ 2, y * half)),
            (3, (), (0, half), (0, width), 0, lambda shard, y, *_: spot(shard ^ 3, y * half)),
            (4, (0,), (0, half), (0, width), 0, lambda shard, y, *_: spot(shard ^ 2, (1 - y) * half)),
            (5, (), (0, half), (0, width), 0, lambda shard, y, *_: spot(shard ^ 3, (1 - y) * half)),
        ]
        return place(moves.scalars, inputs, [(self.shape, bf16)], todo)[0]


def after(item, *others):
    return lax.optimization_barrier((item, *others))[0]


def per_device(
    tokens, segments, grad_out, attention_gain, query_weight, key_matrix, value_matrix, query_gain,
    key_gain, output_weight, mlp_gain, gate_weight, up_weight, down_weight,
):
    moves = Moves()
    shards, mine, direct = moves.shards, moves.mine, moves.direct
    rows, width = tokens.shape[1:]
    total = rows * shards
    slice_width = attention_gain.shape[0]
    head_slice = query_gain.shape[0]
    head = head_slice * shards
    k_heads = key_matrix.shape[1] // head // shards
    q_heads = query_weight.shape[1] // head // shards
    q_width, k_width = q_heads * head, k_heads * head
    units = down_weight.shape[0]
    own_tokens = tokens[0]
    cot = grad_out[0]

    small = jnp.concatenate(
        [attention_gain, mlp_gain, query_gain, key_gain, segments[0].astype(bf16)]
    )[None]
    small = jnp.concatenate(moves.gather(small), axis=0)
    if direct:
        whole = jnp.where(mine % 2 == 0, small, small[jnp.array([1, 0, 3, 2])])
        whole = jnp.where(mine // 2 == 0, whole, whole[jnp.array([2, 3, 0, 1])])
    else:
        whole = small
    cuts = [slice_width, 2 * slice_width, 2 * slice_width + head_slice, 2 * slice_width + 2 * head_slice]
    input_gain = whole[:, : cuts[0]].reshape(1, width).astype(f32)
    second_gain = whole[:, cuts[0] : cuts[1]].reshape(1, width).astype(f32)
    head_gains = jnp.stack(
        [whole[:, cuts[1] : cuts[2]].reshape(head), whole[:, cuts[2] : cuts[3]].reshape(head)]
    ).astype(f32)
    segs = small[:, cuts[3] :].reshape(total).astype(f32)
    index = jnp.arange(shards, dtype=jnp.int32) ^ moves.flip
    places = (index[:, None] * rows + jnp.arange(rows, dtype=jnp.int32)[None]).reshape(total)
    firsts = jnp.sum((segs < 0.5).astype(jnp.int32))
    seconds = jnp.sum((segs < 1.5).astype(jnp.int32))
    opening = jnp.where(segs < 0.5, 0, jnp.where(segs < 1.5, firsts, seconds))
    freqs = theta_base ** (-(jnp.arange(head // 2, dtype=f32) * 2.0) / head)
    angles = (places - opening).astype(f32)[:, None] * freqs
    cosine, sine = jnp.cos(angles), jnp.sin(angles)
    cosine = jnp.concatenate([cosine, cosine], axis=1)
    sine = jnp.concatenate([-sine, sine], axis=1)
    seg_col, seg_row = segs[:, None], segs[None, :]
    order = moves.flip.astype(jnp.int32)[None]

    all_tokens = all_cot = None
    if direct:
        by_rows = lambda source, line: (source * slice_width + line, 0)
        qkv = Fetch(
            moves,
            *cut(moves.scalars, [query_weight, key_matrix, value_matrix], [q_width, k_width, k_width]),
            by_rows,
            (width, q_width + 2 * k_width),
        )
        outer = lambda i, begin, n: lax.dynamic_slice(
            output_weight, ((mine ^ i) * q_width + begin, 0), (n, slice_width)
        )
        half = q_width // 2
        output = Fetch(
            moves,
            outer(0, 0, q_width),
            outer(1, 0, q_width),
            jnp.stack([outer(2, moves.bits[1] * half, half), outer(3, moves.bits[1] * half, half)]),
            lambda source, line: (line, source * slice_width),
            (q_width, width),
        )
        both = Fetch(
            moves,
            *cut(moves.scalars, [gate_weight, up_weight], [units, units]),
            by_rows,
            (width, 2 * units),
        )
        qkv.start()
        all_tokens = moves.gather(after(own_tokens, qkv.here))
        output.start(all_tokens[2], qkv.there)
        qkv_weight = qkv.finish()
        both.start(output.here)
        out_weight = output.finish()
        all_cot = moves.gather(after(cot, both.here))
    else:
        spread = lambda item: lax.all_to_all(item, "shard", split_axis=1, concat_axis=0, tiled=True)
        qkv_weight = jnp.concatenate(
            [spread(query_weight), spread(key_matrix), spread(value_matrix)], axis=1
        )
        out_weight = lax.all_to_all(output_weight, "shard", split_axis=0, concat_axis=1, tiled=True)
        feed_weight = jnp.concatenate([spread(gate_weight), spread(up_weight)], axis=1)

    if not direct:
        all_tokens, all_cot = moves.gather(own_tokens), moves.gather(cot)
    normed_one, lin, rot, val = project(
        all_tokens, input_gain, qkv_weight, cosine, sine, head_gains, q_heads, k_heads
    )
    attended, attended_low, logs = attend(order, rot, val, seg_col, seg_row, q_heads, k_heads, head, shards)
    inputs = own_tokens.astype(f32)
    split = total // 2
    if direct:
        feed_weight = both.finish()
        attended_low = after(attended_low, both.here)
    far_part = dot(attended_low[split:], out_weight).astype(bf16)
    near_part = dot(attended_low[:split], out_weight).astype(bf16)
    residual_one = inputs + moves.scatter(near_part, far_part)
    residual_scale = inverse_root(residual_one)
    normed_two = moves.gather((residual_one * residual_scale * second_gain).astype(bf16))

    *kept, norm_grad, out_part = feed(
        normed_two, all_cot, feed_weight, down_weight, 0, shards, []
    )
    hidden, gate_grad, up_grad, normed_two, all_cot = kept
    share_down = dot_tn(hidden, all_cot).astype(bf16)
    share_gate = dot_tn(normed_two, gate_grad).astype(bf16)
    share_up = dot_tn(normed_two, up_grad).astype(bf16)
    normed_grad_two = moves.scatter(norm_grad[:split], norm_grad[split:])
    mlp_gain_part = jnp.sum(normed_grad_two * residual_one * residual_scale, axis=0)
    residual_grad = cot.astype(f32) + norm_back(
        normed_grad_two * second_gain, residual_one, residual_scale
    )
    branch_grad = moves.gather(residual_grad.astype(bf16))

    out_part = after(out_part, *branch_grad)
    layer_out = (residual_one + moves.scatter(out_part[:split], out_part[split:])).astype(bf16)

    out_grad, branch_grad = branch_back(branch_grad, out_weight)
    share_out = dot_tn(attended_low, branch_grad).astype(bf16)
    query_grad, key_grad, val_grad = attend_back(
        order, rot, val, out_grad, attended, logs, seg_col, seg_row, q_heads, k_heads, head, shards
    )
    query_lin_grad, pair_lin_grad, norm_one_part, gain_part, head_part = unproject(
        query_grad, key_grad, val_grad, lin, cosine, sine, head_gains, qkv_weight, all_tokens,
        q_heads, k_heads,
    )
    share_query = dot_tn(normed_one, query_lin_grad).astype(bf16)
    share_pair = dot_tn(normed_one, pair_lin_grad).astype(bf16)
    normed_grad_one = moves.scatter(norm_one_part[:split], norm_one_part[split:])
    grad_tokens = residual_grad + norm_back(normed_grad_one * input_gain, inputs, inverse_root(inputs))

    gains = jnp.concatenate([gain_part[0], mlp_gain_part, head_part.reshape(2 * head)])[None]
    if direct:
        gains = gains + moves.swap(gains, 1)
        gains = gains + moves.swap(gains, 2)
        for mask in (1, 2, 4):
            gains = gains + moves.cross_rep(gains, mask)
    else:
        gains = lax.psum(gains, ("shard", "rep"))
    gains = gains[0]

    def own_part(begin, size):
        return lax.dynamic_slice_in_dim(gains, begin + mine * size, size, 0)

    grad_attention_gain = own_part(0, slice_width)
    grad_mlp_gain = own_part(width, slice_width)
    grad_query_gain = own_part(2 * width, head_slice)
    grad_key_gain = own_part(2 * width + head, head_slice)

    if direct:
        lines = slice_width // 16
        rest = 2 * units - width
        as_chunks = lambda share: share.reshape(-1, 8, 2, lines, share.shape[1])
        spot_of = lambda values, offset: lax.rem(values[2] + (offset + 8), 8) * (2 * lines)

        downs = units // slice_width
        blocks = (6 + downs, width)
        layout = []
        for i in range(4):
            layout += [
                (0, i, 0, units, i, 0),
                (1, i, 0, width - units, i, units),
                (1, i, width - units, rest, 4 + i // 2, (i % 2) * rest),
            ]
        layout += [(2, b, 0, width, 6 + b, 0) for b in range(downs)]
        chunk = moves.ring_scatter(
            [as_chunks(share_gate), as_chunks(share_up), as_chunks(share_down)], layout, blocks
        )
        own, near, far = moves.exchange(
            chunk, lambda at: [(at, 0, width), (4 + at // 2, (at % 2) * rest, rest)], 2 * units
        )
        layout = []
        for i, (source, index) in enumerate([(0, 0), (1, 0), (2, 0), (2, 1)]):
            layout += [
                (source, index, 0, width, i, 0),
                (source, index, width, rest, 4 + i // 2, (i % 2) * rest),
            ]
        layout += [(3, 6 + b, 0, width, 6 + b, 0) for b in range(downs)]
        parts = moves.ring_gather(
            pack([own, near, far, chunk], layout, (blocks[0], 2, lines, width))
        )
        todo = []
        for source, (part, offset, half) in enumerate(parts):
            for h in range(part.shape[1]):
                line = ((half or 0) + h) * lines
                for i in range(4):

                    def at(*values, i=i, line=line, offset=offset, begin=0):
                        return spot_of(values, offset) + line, (values[0] ^ i) * units + begin

                    first = width - units
                    todo += [
                        (source, (i, h), (0, lines), (0, units), 0, at),
                        (source, (i, h), (0, lines), (units, width), 1, at),
                        (
                            source, (4 + i // 2, h), (0, lines),
                            ((i % 2) * rest, (i % 2) * rest + rest), 1,
                            functools.partial(at, begin=first),
                        ),
                    ]
                for b in range(downs):

                    def at(*values, b=b, line=line, offset=offset):
                        return b * slice_width + spot_of(values, offset) + line, 0

                    todo.append((source, (6 + b, h), (0, lines), (0, width), 2, at))
        shapes = [((slice_width, units * 4), f32)] * 2 + [((units, width), f32)]
        grad_gate, grad_up, grad_down = place(
            moves.scalars, [part for part, _, _ in parts], shapes, todo
        )

        outs = q_width // slice_width
        pair = 2 * k_width
        wide = q_width + pair
        layout = []
        for i in range(4):
            layout += [(0, i, 0, q_width, i, 0), (1, i, 0, pair, i, q_width)]
        layout += [(2, b, 0, width, 4 + b, 0) for b in range(outs)]
        chunk = moves.ring_scatter(
            [as_chunks(share_query), as_chunks(share_pair), as_chunks(share_out)],
            layout,
            (4 + outs, width),
        )
        own, near, far = moves.exchange(
            chunk,
            lambda at: [(at, 0, wide)] + [(4 + b, at * slice_width, slice_width) for b in range(outs)],
            wide + outs * slice_width,
        )
        wide_all = wide + outs * slice_width
        layout = [
            (source, index, 0, wide_all, i, 0)
            for i, (source, index) in enumerate([(0, 0), (1, 0), (2, 0), (2, 1)])
        ]
        parts = moves.ring_gather(pack([own, near, far], layout, (4, 2, lines, wide_all)))
        todo = []
        for source, (part, offset, half) in enumerate(parts):
            for h in range(part.shape[1]):
                line = ((half or 0) + h) * lines
                for i in range(4):
                    begin = 0
                    for target, size in enumerate([q_width, k_width, k_width]):

                        def at(*values, i=i, line=line, offset=offset, size=size):
                            return spot_of(values, offset) + line, (values[0] ^ i) * size

                        todo.append((source, (i, h), (0, lines), (begin, begin + size), target, at))
                        begin += size
                    for b in range(outs):

                        def at(*values, i=i, b=b, line=line, offset=offset):
                            first = (values[0] ^ i) * q_width + b * slice_width
                            return first + spot_of(values, offset) + line, 0

                        todo.append(
                            (source, (i, h), (0, lines), (begin, begin + slice_width), 3, at)
                        )
                        begin += slice_width
        shapes = [((slice_width, size * 4), f32) for size in (q_width, k_width, k_width)]
        shapes.append(((q_width * 4, slice_width), f32))
        grad_query, grad_key, grad_value, grad_output = place(
            moves.scalars, [part for part, _, _ in parts], shapes, todo
        )
    else:

        def finish(share):
            part = lax.all_to_all(share, "shard", split_axis=0, concat_axis=1, tiled=True)
            return lax.psum(part, "rep").astype(f32)

        grad_down = lax.psum(share_down, "rep").astype(f32)
        grad_gate = finish(share_gate)
        grad_up = finish(share_up)
        grad_output = lax.psum(
            lax.all_to_all(share_out, "shard", split_axis=1, concat_axis=0, tiled=True), "rep"
        ).astype(f32)
        grad_query = finish(share_query)
        grad_key = finish(share_pair[:, :k_width])
        grad_value = finish(share_pair[:, k_width:])

    return (
        layer_out[None], grad_tokens[None], grad_attention_gain, grad_query, grad_key, grad_value,
        grad_query_gain, grad_key_gain, grad_output, grad_mlp_gain, grad_gate, grad_up, grad_down,
    )


def solution(mesh):
    rows_over = P("shard", None)
    return jax.shard_map(
        per_device,
        mesh=mesh,
        in_specs=(
            P("rep", "shard", None), P("rep", "shard"), P("rep", "shard", None), P("shard"), rows_over,
            rows_over, rows_over, P("shard"), P("shard"), P(None, "shard"), P("shard"), rows_over,
            rows_over, rows_over,
        ),
        out_specs=(
            P("rep", "shard", None), P("rep", "shard", None), P("shard"), rows_over, rows_over,
            rows_over, P("shard"), P("shard"), P(None, "shard"), P("shard"), rows_over, rows_over,
            rows_over,
        ),
        check_vma=False,
    )
```

time: 463 us -> 392 us (0.85)
  starting transfers between devices: 135 us -> 58.7 us
  Pallas kernels: 70.8 us -> 98.8 us
  waiting for transfers between devices: 167 us -> 152 us
  other arithmetic: 29.4 us -> 23.2 us
    ppermute x44 -> x16, starting transfers between devices: 61.9 us -> 21.8 us  [up(): lax.ppermute(item, 'rep', [(ring[i], ring[(i + 1) % 8]) for i in range(8)])]
    ppermute x44 -> x16, starting transfers between devices: 44.6 us -> 10.5 us  [down(): lax.ppermute(item, 'rep', [(ring[(i + 1) % 8], ring[i]) for i in range(8)])]
    ppermute x44 -> x16, waiting for transfers between devices: 72.4 us -> 41 us  [up(): lax.ppermute(item, 'rep', [(ring[i], ring[(i + 1) % 8]) for i in range(8)])]
    pallas_call x3 -> x20, Pallas kernels: 35.4 us -> 65.1 us  [the longest x10 18.6 us: ring_step(): pl.pallas_call(functools.partial(ring_kernel, layout, plan, len(shares),...]
    ppermute x3 -> x6, waiting for transfers between devices: 5.26 us -> 27.3 us  [cross_rep(): return lax.ppermute(item, 'rep', [(i, i ^ mask) for i in range(8)])]
    concatenate x16 -> x3, other arithmetic: 12.1 us -> 0.07 us  [the longest x2 0.04 us: exchange(): far = self.swap(jnp.concatenate([far, near[1:]], axis=0), 2)]
    ppermute x44 -> x16, waiting for transfers between devices: 40 us -> 33.3 us  [down(): lax.ppermute(item, 'rep', [(ring[(i + 1) % 8], ring[i]) for i in range(8)])]
    dynamic_slice x8 -> x0, local copies, waits for them, and re-layouts: 5.76 us -> none  [the longest x6 5.72 us: columns(): return lax.dynamic_slice(item, (begin, (mine ^ i) * size), (count, size))]
  transfers between devices with their start and end apart: 138 -> 83, of which waited for: 57 -> 34; matrix products, arithmetic and copies ran while one was open for 14% -> 13% of each run, Pallas kernels for 11% -> 20%
where the time goes in v2:
time: 392 us; the launch traced here: 387 us
  waiting for transfers between devices  152 us (39%)
  Pallas kernels  98.8 us (25%)
  starting transfers between devices  58.7 us (15%)
  local copies, waits for them, and re-layouts  35.4 us (9%)
  other arithmetic  23.2 us (6%)
  matrix products  16.5 us (4%)
    ppermute x45, waiting for transfers between devices, swap(): return lax.ppermute(item, 'shard', [(i, i ^ mask) for i in range(4)])  50.9 us
    ppermute x16, waiting for transfers between devices, up(): lax.ppermute(item, 'rep', [(ring[i], ring[(i + 1) % 8]) for i in range(8)])  41 us
    ppermute x16, waiting for transfers between devices, down(): lax.ppermute(item, 'rep', [(ring[(i + 1) % 8], ring[i]) for i in range(8)])  33.3 us
    ppermute x6, waiting for transfers between devices, cross_rep(): return lax.ppermute(item, 'rep', [(i, i ^ mask) for i in range(8)])  27.3 us
    ppermute x45, starting transfers between devices, swap(): return lax.ppermute(item, 'shard', [(i, i ^ mask) for i in range(4)])  21.8 us
    ppermute x16, starting transfers between devices, up(): lax.ppermute(item, 'rep', [(ring[i], ring[(i + 1) % 8]) for i in range(8)])  21.8 us
    unnamed x132, local copies, waits for them, and re-layouts  19.8 us
    pallas_call x10, Pallas kernels, ring_step(): pl.pallas_call(functools.partial(ring_kernel, layout, plan, len(shares),...  18.6 us
  transfers between devices with their start and end apart: 83, of which 34 were waited for; matrix products, arithmetic and copies ran while one was open for 13% of the time, Pallas kernels for 20%

profile of v2, /device:TPU:0, one launch (start us, length us, event | category | flops | bytes accessed | tf_op | source)
XLA Modules:
  0.0 386.8 jit_solution(11962341665564506142)
XLA Ops:
  4.1 3.0 collective-permute-start.1
  30.9 11.8 %collective-permute-done.6.refs_4_ = bf16[2,128,1024]{2,1,0:T(8,128)(2,1)S(1)} collective-permute-done((bf16[2,128,1024]{2,1,0:T(8,128)(2,1)S(1)}, bf16[2,128,1024]{2,1,0:T(8,128)(2,1)S(1)}, u32[]{:S(2)}, u32[]{:S(2)}) %collective-permute-start.6) | collective-permute-done | bytes 524320 | tf_op jit(solution)/shard_map/ppermute | solution.py:593
  45.0 4.9 %collective-permute-done.11.refs_2_ = bf16[2,256,256]{2,1,0:T(8,128)(2,1)S(1)} collective-permute-done((bf16[2,256,256]{2,1,0:T(8,128)(2,1)S(1)}, bf16[2,256,256]{2,1,0:T(8,128)(2,1)S(1)}, u32[]{:S(2)}, u32[]{:S(2)}) %collective-permute-start.11) | collective-permute-done | bytes 262176 | tf_op jit(solution)/shard_map/ppermute | solution.py:590
  58.5 8.0 %shard_map.257 = (bf16[1024,1024]{1,0:T(8,128)(2,1)}, f32[1024,768]{1,0:T(8,128)}, bf16[1024,768]{1,0:T(8,128)(2,1)}, bf16[1024,256]{1,0:T(8,128)(2,1)S(1)}) custom-call(f32[1,1024]{1,0:T(1,128)S(1)} %bitcast.138, bf16[1024,1024]{1,0:T(8,128)(2,1)} %shard_map.256.weight, f32[1024,128]{1,0:T(8,128)S(1)} %get-tuple-element.179.cosine, ...), custom_call_target="tpu_custom_call" | custom-call | flops 2147483648 | bytes 14680064 | tf_op jit(solution)/shard_map/pallas_call | solution.py:97
  68.1 5.5 %shard_map.258 = (f32[1024,512]{1,0:T(8,128)}, bf16[1024,512]{1,0:T(8,128)(2,1)S(1)}, f32[1024,512]{1,0:T(8,128)}) custom-call(s32[1]{0:T(128)} %bitcast.1.order, bf16[1024,768]{1,0:T(8,128)(2,1)S(1)} %copy-done.41, bf16[1024,768]{1,0:T(8,128)(2,1)S(1)} %copy-done.41, bf16[1024,256]{1,0:T(8,128)(2,1)S(1)} %get-tuple-element.83.val, f32[1024,1]{1,0:T(8,128)S(1)} %bitcast.133, ...), custom_call_target="tpu_custom_call" | custom-call | flops 2147483648 | bytes 6291456 | tf_op jit(solution)/shard_map/pallas_call | solution.py:170
  79.9 12.1 %collective-permute-done.19 = bf16[256,1024]{1,0:T(8,128)(2,1)S(1)} collective-permute-done((bf16[256,1024]{1,0:T(8,128)(2,1)S(1)}, bf16[256,1024]{1,0:T(8,128)(2,1)S(1)}, u32[]{:S(2)}, u32[]{:S(2)}) %collective-permute-start.19) | collective-permute-done | bytes 524320 | tf_op jit(solution)/shard_map/ppermute | solution.py:590
  96.1 7.2 %collective-permute-done.28.refs_6_ = bf16[256,1024]{1,0:T(8,128)(2,1)} collective-permute-done((bf16[256,1024]{1,0:T(8,128)(2,1)}, bf16[256,1024]{1,0:T(8,128)(2,1)}, u32[]{:S(2)}, u32[]{:S(2)}) %collective-permute-start.28) | collective-permute-done | bytes 524320 | tf_op jit(solution)/shard_map/ppermute | solution.py:590
  103.8 10.2 %collective-permute-done.25.refs_2_ = bf16[256,1024]{1,0:T(8,128)(2,1)} collective-permute-done((bf16[256,1024]{1,0:T(8,128)(2,1)}, bf16[256,1024]{1,0:T(8,128)(2,1)}, u32[]{:S(2)}, u32[]{:S(2)}) %collective-permute-start.25) | collective-permute-done | bytes 524320 | tf_op jit(solution)/shard_map/ppermute | solution.py:590
  122.8 17.4 %shard_map.262 = (bf16[1024,768]{1,0:T(8,128)(2,1)}, bf16[1024,768]{1,0:T(8,128)(2,1)}, bf16[1024,768]{1,0:T(8,128)(2,1)}, bf16[1024,1024]{1,0:T(8,128)(2,1)}, b...) custom-call(bf16[1024,1536]{1,0:T(8,128)(2,1)} %shard_map.261.weight, ...), custom_call_target="tpu_custom_call" | custom-call | flops 9663676416 | bytes 21495808 | tf_op jit(solution)/shard_map/pallas_call | solution.py:304
  142.9 3.4 convolution_convert_fusion.1
  151.5 3.0 convolution_convert_fusion
  157.6 6.9 %collective-permute-done.65.refs_6_ = bf16[9,1,16,1024]{3,2,1,0:T(8,128)(2,1)S(1)} collective-permute-done((bf16[9,1,16,1024]{3,2,1,0:T(8,128)(2,1)S(1)}, bf16[9,1,16,1024]{3,2,1,0:T(8,128)(2,1)S(1)}, u32[]{:S(2)}, u32[]{:S(2)}) %collective-permute-start.65) | collective-permute-done | bytes 294944 | tf_op jit(solution)/shard_map/ppermute | solution.py:583
  176.1 6.9 %collective-permute-done.67.refs_6_ = bf16[9,2,16,1024]{3,2,1,0:T(8,128)(2,1)S(1)} collective-permute-done((bf16[9,2,16,1024]{3,2,1,0:T(8,128)(2,1)}, bf16[9,2,16,1024]{3,2,1,0:T(8,128)(2,1)S(1)}, u32[]{:S(2)}, u32[]{:S(2)}) %collective-permute-start.67) | collective-permute-done | bytes 589856 | tf_op jit(solution)/shard_map/ppermute | solution.py:583
  184.4 3.0 shard_map.276
  190.0 10.7 %collective-permute-done.69.refs_6_ = bf16[9,2,16,1024]{3,2,1,0:T(8,128)(2,1)S(1)} collective-permute-done((bf16[9,2,16,1024]{3,2,1,0:T(8,128)(2,1)}, bf16[9,2,16,1024]{3,2,1,0:T(8,128)(2,1)S(1)}, u32[]{:S(2)}, u32[]{:S(2)}) %collective-permute-start.69) | collective-permute-done | bytes 589856 | tf_op jit(solution)/shard_map/ppermute | solution.py:583
  201.9 3.0 shard_map.277
  206.9 4.9 %shard_map.263 = (bf16[1024,512]{1,0:T(8,128)(2,1)S(1)}, bf16[1024,1024]{1,0:T(8,128)(2,1)}) custom-call(bf16[512,1024]{1,0:T(8,128)(2,1)} %copy-done.17, bf16[256,1024]{1,0:T(8,128)(2,1)} %get-tuple-element.149.refs_0_, bf16[256,1024]{1,0:T(8,128)(2,1)} %collective-permute-done.33.refs_1_, bf16[256,1024]{1,0:T(8,128)(2,1)} %collective-permute-done.34.refs_2_, ...), custom_call_target="tpu_custom_call" | custom-call | flops 1073741824 | bytes 7340032 | tf_op jit(solution)/shard_map/pallas_call | solution.py:335
  215.7 12.6 %shard_map.264 = (f32[1024,512]{1,0:T(8,128)}, f32[1024,256]{1,0:T(8,128)S(1)}, f32[1024,256]{1,0:T(8,128)S(1)}) custom-call(s32[1]{0:T(128)} %bitcast.1.order, bf16[1024,768]{1,0:T(8,128)(2,1)} %get-tuple-element.82.query.key, bf16[1024,768]{1,0:T(8,128)(2,1)} %get-tuple-element.82.query.key, bf16[1024,256]{1,0:T(8,128)(2,1)S(1)} %copy-done.43, ...), custom_call_target="tpu_custom_call" | custom-call | flops 5368709120 | bytes 10485760 | tf_op jit(solution)/shard_map/pallas_call | solution.py:243
  230.3 11.9 %shard_map.265 = (bf16[1024,512]{1,0:T(8,128)(2,1)}, bf16[1024,512]{1,0:T(8,128)(2,1)}, bf16[1024,1024]{1,0:T(8,128)(2,1)}, f32[1,1024]{1,0:T(1,128)S(1)}, f32[2,128]{1,0:T(2,128)S(1)}) custom-call(f32[1024,512]{1,0:T(8,128)} %get-tuple-element.98.query_grad, f32[1024,256]{1,0:T(8,128)} %copy-done.13, f32[1024,256]{1,0:T(8,128)} %copy-done.14, ...), custom_call_target="tpu_custom_call" | custom-call | flops 2147483648 | bytes 18874368 | tf_op jit(solution)/shard_map/pallas_call | solution.py:394
  248.3 3.6 collective-permute-done.47.refs_6_
  269.0 4.1 %collective-permute-done.74.refs_2_ = bf16[2,2,16,1536]{3,2,1,0:T(8,128)(2,1)S(1)} collective-permute-done((bf16[2,2,16,1536]{3,2,1,0:T(8,128)(2,1)S(1)}, bf16[2,2,16,1536]{3,2,1,0:T(8,128)(2,1)S(1)}, u32[]{:S(2)}, u32[]{:S(2)}) %collective-permute-start.74) | collective-permute-done | bytes 196640 | tf_op jit(solution)/shard_map/ppermute | solution.py:590
  279.8 3.6 collective-permute-done.43
  284.3 11.1 %collective-permute-done.44 = f32[1,2304]{1,0:T(1,128)S(1)} collective-permute-done((f32[1,2304]{1,0:T(1,128)S(1)}, f32[1,2304]{1,0:T(1,128)S(1)}, u32[]{:S(2)}, u32[]{:S(2)}) %collective-permute-start.44) | collective-permute-done | bytes 9248 | tf_op jit(solution)/shard_map/ppermute | solution.py:593
  295.5 3.6 collective-permute-done.45
  307.5 4.2 %collective-permute-done.56.refs_2_ = bf16[2,2,16,1536]{3,2,1,0:T(8,128)(2,1)S(1)} collective-permute-done((bf16[2,2,16,1536]{3,2,1,0:T(8,128)(2,1)S(1)}, bf16[2,2,16,1536]{3,2,1,0:T(8,128)(2,1)S(1)}, u32[]{:S(2)}, u32[]{:S(2)}) %collective-permute-start.56) | collective-permute-done | bytes 196640 | tf_op jit(solution)/shard_map/ppermute | solution.py:590
  324.5 4.0 %collective-permute-done.57.refs_1_ = bf16[4,2,16,1536]{3,2,1,0:T(8,128)(2,1)S(1)} collective-permute-done((bf16[4,2,16,1536]{3,2,1,0:T(8,128)(2,1)S(1)}, bf16[4,2,16,1536]{3,2,1,0:T(8,128)(2,1)S(1)}, u32[]{:S(2)}, u32[]{:S(2)}) %collective-permute-start.57) | collective-permute-done | bytes 393248 | tf_op jit(solution)/shard_map/ppermute | solution.py:583
  332.4 8.9 %collective-permute-done.78.refs_4_ = bf16[9,2,16,1024]{3,2,1,0:T(8,128)(2,1)S(1)} collective-permute-done((bf16[9,2,16,1024]{3,2,1,0:T(8,128)(2,1)S(1)}, bf16[9,2,16,1024]{3,2,1,0:T(8,128)(2,1)S(1)}, u32[]{:S(2)}, u32[]{:S(2)}) %collective-permute-start.78) | collective-permute-done | bytes 589856 | tf_op jit(solution)/shard_map/ppermute | solution.py:587
  343.1 5.0 %collective-permute-done.59.refs_3_ = bf16[4,2,16,1536]{3,2,1,0:T(8,128)(2,1)S(1)} collective-permute-done((bf16[4,2,16,1536]{3,2,1,0:T(8,128)(2,1)S(1)}, bf16[4,2,16,1536]{3,2,1,0:T(8,128)(2,1)S(1)}, u32[]{:S(2)}, u32[]{:S(2)}) %collective-permute-start.59) | collective-permute-done | bytes 393248 | tf_op jit(solution)/shard_map/ppermute | solution.py:583
  353.1 9.3 %collective-permute-done.80.refs_6_ = bf16[9,2,16,1024]{3,2,1,0:T(8,128)(2,1)S(1)} collective-permute-done((bf16[9,2,16,1024]{3,2,1,0:T(8,128)(2,1)S(1)}, bf16[9,2,16,1024]{3,2,1,0:T(8,128)(2,1)S(1)}, u32[]{:S(2)}, u32[]{:S(2)}) %collective-permute-start.80) | collective-permute-done | bytes 589856 | tf_op jit(solution)/shard_map/ppermute | solution.py:587
  364.4 6.3 %collective-permute-done.62.refs_6_ = bf16[4,2,16,1536]{3,2,1,0:T(8,128)(2,1)S(1)} collective-permute-done((bf16[4,2,16,1536]{3,2,1,0:T(8,128)(2,1)S(1)}, bf16[4,2,16,1536]{3,2,1,0:T(8,128)(2,1)S(1)}, u32[]{:S(2)}, u32[]{:S(2)}) %collective-permute-start.62) | collective-permute-done | bytes 393248 | tf_op jit(solution)/shard_map/ppermute | solution.py:587
  377.0 5.6 %shard_map.281 = (f32[256,3072]{1,0:T(8,128)}, f32[256,3072]{1,0:T(8,128)}, f32[768,1024]{1,0:T(8,128)}) custom-call(s32[3]{0:T(128)S(1)} %pad_add_fusion.scalars, bf16[9,2,16,1024]{3,2,1,0:T(8,128)(2,1)S(1)} %shard_map.280.refs_0_, bf16[9,2,16,1024]{3,2,1,0:T(8,128)(2,1)S(1)} %collective-permute-done.75.refs_1_, ...), custom_call_target="tpu_custom_call" | custom-call | bytes 14155776 | tf_op jit(solution)/shard_map/pallas_call | solution.py:442
  382.7 3.9 shard_map.273
  (373 shorter events, 165.7 us)
Async XLA Ops:
  12.9 38.1 %collective-permute-start.3 = (bf16[256,1024]{1,0:T(8,128)(2,1)}, bf16[256,1024]{1,0:T(8,128)(2,1)}, u32[]{:S(2)}, u32[]{:S(2)}) collective-permute-start(bf16[256,1024]{1,0:T(8,128)(2,1)} %get-tuple-element.79), channel_id=1, source_target_pairs={{0,8},{8,0},{16,24},{24,16},{1,9},{9,1},{17,25},{25,17},{2,10},{10... | collective-permute-start | bytes 1572872 | tf_op jit(solution)/shard_map/ppermute | solution.py:590
  30.9 27.1 %collective-permute-start.8 = (bf16[256,1024]{1,0:T(8,128)(2,1)S(1)}, bf16[256,1024]{1,0:T(8,128)(2,1)}, u32[]{:S(2)}, u32[]{:S(2)}) collective-permute-start(bf16[256,1024]{1,0:T(8,128)(2,1)S(1)} %bitcast.130), channel_id=1, source_target_pairs={{0,8},{8,0},{16,24},{24,16},{1,9},{9,1},{17,25},{25,17},{2,10},{10... | collective-permute-start | bytes 1572872 | tf_op jit(solution)/shard_map/ppermute | solution.py:590
  51.0 23.3 %collective-permute-start.12 = (bf16[2,128,1536]{2,1,0:T(8,128)(2,1)}, bf16[2,128,1536]{2,1,0:T(8,128)(2,1)S(1)}, u32[]{:S(2)}, u32[]{:S(2)}) collective-permute-start(bf16[2,128,1536]{2,1,0:T(8,128)(2,1)} %copy-done.39), channel_id=1, source_target_pairs={{0,16},{8,24},{16,0},{24,8},{1,17},{9,25},{17,1},{25,9},{2,18},{10... | collective-permute-start | bytes 2359304 | tf_op jit(solution)/shard_map/ppermute | solution.py:590
  54.2 19.4 %collective-permute-start.13 = (bf16[512,256]{1,0:T(8,128)(2,1)}, bf16[512,256]{1,0:T(8,128)(2,1)S(1)}, u32[]{:S(2)}, u32[]{:S(2)}) collective-permute-start(bf16[512,256]{1,0:T(8,128)(2,1)} %get-tuple-element.161), channel_id=1, source_target_pairs={{0,8},{8,0},{16,24},{24,16},{1,9},{9,1},{17,25},{25,17},{2,10},{10... | collective-permute-start | bytes 786440 | tf_op jit(solution)/shard_map/ppermute | solution.py:590
  78.6 16.1 %collective-permute-start.20 = (bf16[256,1536]{1,0:T(8,128)(2,1)S(1)}, bf16[256,1536]{1,0:T(8,128)(2,1)S(1)}, u32[]{:S(2)}, u32[]{:S(2)}) collective-permute-start(bf16[256,1536]{1,0:T(8,128)(2,1)S(1)} %copy-done.38), channel_id=1, source_target_pairs={{0,8},{8,0},{16,24},{24,16},{1,9},{9,1},{17,25},{25,17},{2,10},{10... | collective-permute-start | bytes 2359304 | tf_op jit(solution)/shard_map/ppermute | solution.py:590
  78.7 24.7 %collective-permute-start.28 = (bf16[256,1024]{1,0:T(8,128)(2,1)}, bf16[256,1024]{1,0:T(8,128)(2,1)}, u32[]{:S(2)}, u32[]{:S(2)}) collective-permute-start(bf16[256,1024]{1,0:T(8,128)(2,1)} %bitcast.12.refs_4_), channel_id=1, source_target_pairs={{0,16},{8,24},{16,0},{24,8},{1,17},{9,25},{17,1},{25,9},{2,18},{10... | collective-permute-start | bytes 1572872 | tf_op jit(solution)/shard_map/ppermute | solution.py:590
  79.4 24.0 %collective-permute-start.22 = (bf16[2,128,1536]{2,1,0:T(8,128)(2,1)S(1)}, bf16[2,128,1536]{2,1,0:T(8,128)(2,1)S(1)}, u32[]{:S(2)}, u32[]{:S(2)}) collective-permute-start(bf16[2,128,1536]{2,1,0:T(8,128)(2,1)S(1)} %collective-permute-done.12.refs_2_), channel_id=1, source_target_pairs={{0,1},{1,0},{2,3},{3,2},{4,5},{5,4},{6,7},{7,6},{8,9},{9,8},{10,11... | collective-permute-start | bytes 2359304 | tf_op jit(solution)/shard_map/ppermute | solution.py:593
  93.4 20.7 %collective-permute-start.25 = (bf16[256,1024]{1,0:T(8,128)(2,1)}, bf16[256,1024]{1,0:T(8,128)(2,1)}, u32[]{:S(2)}, u32[]{:S(2)}) collective-permute-start(bf16[256,1024]{1,0:T(8,128)(2,1)} %multiply_convert_fusion.refs_0_), channel_id=1, source_target_pairs={{0,16},{8,24},{16,0},{24,8},{1,17},{9,25},{17,1},{25,9},{2,18},{10... | collective-permute-start | bytes 1572872 | tf_op jit(solution)/shard_map/ppermute | solution.py:590
  94.7 28.1 %collective-permute-start.27 = (bf16[256,1024]{1,0:T(8,128)(2,1)}, bf16[256,1024]{1,0:T(8,128)(2,1)}, u32[]{:S(2)}, u32[]{:S(2)}) collective-permute-start(bf16[256,1024]{1,0:T(8,128)(2,1)} %bitcast.12.refs_4_), channel_id=1, source_target_pairs={{0,8},{8,0},{16,24},{24,16},{1,9},{9,1},{17,25},{25,17},{2,10},{10... | collective-permute-start | bytes 1572872 | tf_op jit(solution)/shard_map/ppermute | solution.py:590
  95.6 19.2 %collective-permute-start.21 = (bf16[128,1536]{1,0:T(8,128)(2,1)S(1)}, bf16[128,1536]{1,0:T(8,128)(2,1)S(1)}, u32[]{:S(2)}, u32[]{:S(2)}) collective-permute-start(bf16[128,1536]{1,0:T(8,128)(2,1)S(1)} %slice_bitcast_fusion.1), channel_id=1, source_target_pairs={{0,8},{8,0},{16,24},{24,16},{1,9},{9,1},{17,25},{25,17},{2,10},{10... | collective-permute-start | bytes 1179656 | tf_op jit(solution)/shard_map/ppermute | solution.py:590
  103.3 19.5 %collective-permute-start.29 = (bf16[256,1024]{1,0:T(8,128)(2,1)}, bf16[256,1024]{1,0:T(8,128)(2,1)}, u32[]{:S(2)}, u32[]{:S(2)}) collective-permute-start(bf16[256,1024]{1,0:T(8,128)(2,1)} %collective-permute-done.28.refs_6_), channel_id=1, source_target_pairs={{0,8},{8,0},{16,24},{24,16},{1,9},{9,1},{17,25},{25,17},{2,10},{10... | collective-permute-start | bytes 1572872 | tf_op jit(solution)/shard_map/ppermute | solution.py:590
  103.3 19.4 %collective-permute-start.24 = (bf16[256,1024]{1,0:T(8,128)(2,1)}, bf16[256,1024]{1,0:T(8,128)(2,1)}, u32[]{:S(2)}, u32[]{:S(2)}) collective-permute-start(bf16[256,1024]{1,0:T(8,128)(2,1)} %multiply_convert_fusion.refs_0_), channel_id=1, source_target_pairs={{0,8},{8,0},{16,24},{24,16},{1,9},{9,1},{17,25},{25,17},{2,10},{10... | collective-permute-start | bytes 1572872 | tf_op jit(solution)/shard_map/ppermute | solution.py:590
  142.8 27.9 %collective-permute-start.30 = (bf16[256,1024]{1,0:T(8,128)(2,1)}, bf16[256,1024]{1,0:T(8,128)(2,1)}, u32[]{:S(2)}, u32[]{:S(2)}) collective-permute-start(bf16[256,1024]{1,0:T(8,128)(2,1)} %get-tuple-element.157), channel_id=1, source_target_pairs={{0,8},{8,0},{16,24},{24,16},{1,9},{9,1},{17,25},{25,17},{2,10},{10... | collective-permute-start | bytes 1572872 | tf_op jit(solution)/shard_map/ppermute | solution.py:590
  150.1 20.6 %collective-permute-start.32 = (bf16[256,1024]{1,0:T(8,128)(2,1)}, bf16[256,1024]{1,0:T(8,128)(2,1)}, u32[]{:S(2)}, u32[]{:S(2)}) collective-permute-start(bf16[256,1024]{1,0:T(8,128)(2,1)} %slice_add_fusion.3), channel_id=1, source_target_pairs={{0,16},{8,24},{16,0},{24,8},{1,17},{9,25},{17,1},{25,9},{2,18},{10... | collective-permute-start | bytes 1572872 | tf_op jit(solution)/shard_map/ppermute | solution.py:590
  189.4 17.5 %collective-permute-start.33 = (bf16[256,1024]{1,0:T(8,128)(2,1)}, bf16[256,1024]{1,0:T(8,128)(2,1)}, u32[]{:S(2)}, u32[]{:S(2)}) collective-permute-start(bf16[256,1024]{1,0:T(8,128)(2,1)} %get-tuple-element.149.refs_0_), channel_id=1, source_target_pairs={{0,8},{8,0},{16,24},{24,16},{1,9},{9,1},{17,25},{25,17},{2,10},{10... | collective-permute-start | bytes 1572872 | tf_op jit(solution)/shard_map/ppermute | solution.py:590
  189.4 17.5 %collective-permute-start.35 = (bf16[256,1024]{1,0:T(8,128)(2,1)}, bf16[256,1024]{1,0:T(8,128)(2,1)}, u32[]{:S(2)}, u32[]{:S(2)}) collective-permute-start(bf16[256,1024]{1,0:T(8,128)(2,1)} %collective-permute-done.34.refs_2_), channel_id=1, source_target_pairs={{0,8},{8,0},{16,24},{24,16},{1,9},{9,1},{17,25},{25,17},{2,10},{10... | collective-permute-start | bytes 1572872 | tf_op jit(solution)/shard_map/ppermute | solution.py:590
  204.9 52.3 %collective-permute-start.71 = (bf16[9,2,16,1024]{3,2,1,0:T(8,128)(2,1)}, bf16[9,2,16,1024]{3,2,1,0:T(8,128)(2,1)}, u32[]{:S(2)}, u32[]{:S(2)}) collective-permute-start(bf16[9,2,16,1024]{3,2,1,0:T(8,128)(2,1)} %get-tuple-element.135), channel_id=1, source_target_pairs={{0,2},{2,4},{4,6},{6,7},{7,5},{5,3},{3,1},{1,0},{8,10},{10,12},{12... | collective-permute-start | bytes 1769480 | tf_op jit(solution)/shard_map/ppermute | solution.py:583
  205.8 51.4 %collective-permute-start.72 = (bf16[9,2,16,1024]{3,2,1,0:T(8,128)(2,1)}, bf16[9,2,16,1024]{3,2,1,0:T(8,128)(2,1)}, u32[]{:S(2)}, u32[]{:S(2)}) collective-permute-start(bf16[9,2,16,1024]{3,2,1,0:T(8,128)(2,1)} %get-tuple-element.136), channel_id=1, source_target_pairs={{2,0},{4,2},{6,4},{7,6},{5,7},{3,5},{1,3},{0,1},{10,8},{12,10},{14... | collective-permute-start | bytes 1769480 | tf_op jit(solution)/shard_map/ppermute | solution.py:587
  259.7 19.9 %collective-permute-start.42 = (f32[1,2304]{1,0:T(1,128)S(1)}, f32[1,2304]{1,0:T(1,128)S(1)}, u32[]{:S(2)}, u32[]{:S(2)}) collective-permute-start(f32[1,2304]{1,0:T(1,128)S(1)} %broadcast_in_dim.52), channel_id=1, source_target_pairs={{0,8},{8,0},{16,24},{24,16},{1,9},{9,1},{17,25},{25,17},{2,10},{10... | collective-permute-start | bytes 27656 | tf_op jit(solution)/shard_map/ppermute | solution.py:590
  269.0 36.9 %collective-permute-start.40 = (bf16[256,1024]{1,0:T(8,128)(2,1)S(1)}, bf16[256,1024]{1,0:T(8,128)(2,1)S(1)}, u32[]{:S(2)}, u32[]{:S(2)}) collective-permute-start(bf16[256,1024]{1,0:T(8,128)(2,1)S(1)} %get-tuple-element.154), channel_id=1, source_target_pairs={{0,8},{8,0},{16,24},{24,16},{1,9},{9,1},{17,25},{25,17},{2,10},{10... | collective-permute-start | bytes 1572872 | tf_op jit(solution)/shard_map/ppermute | solution.py:590
  273.1 30.7 %collective-permute-start.75 = (bf16[9,2,16,1024]{3,2,1,0:T(8,128)(2,1)S(1)}, bf16[9,2,16,1024]{3,2,1,0:T(8,128)(2,1)S(1)}, u32[]{:S(2)}, u32[]{:S(2)}) collective-permute-start(bf16[9,2,16,1024]{3,2,1,0:T(8,128)(2,1)S(1)} %shard_map.280.refs_0_), channel_id=1, source_target_pairs={{0,2},{2,4},{4,6},{6,7},{7,5},{5,3},{3,1},{1,0},{8,10},{10,12},{12... | collective-permute-start | bytes 1769480 | tf_op jit(solution)/shard_map/ppermute | solution.py:583
  277.5 21.7 %collective-permute-start.53 = (bf16[6,2,16,1024]{3,2,1,0:T(8,128)(2,1)S(1)}, bf16[6,2,16,1024]{3,2,1,0:T(8,128)(2,1)S(1)}, u32[]{:S(2)}, u32[]{:S(2)}) collective-permute-start(bf16[6,2,16,1024]{3,2,1,0:T(8,128)(2,1)S(1)} %get-tuple-element.115), channel_id=1, source_target_pairs={{0,2},{2,4},{4,6},{6,7},{7,5},{5,3},{3,1},{1,0},{8,10},{10,12},{12... | collective-permute-start | bytes 1179656 | tf_op jit(solution)/shard_map/ppermute | solution.py:583
  278.2 21.1 %collective-permute-start.54 = (bf16[6,2,16,1024]{3,2,1,0:T(8,128)(2,1)S(1)}, bf16[6,2,16,1024]{3,2,1,0:T(8,128)(2,1)S(1)}, u32[]{:S(2)}, u32[]{:S(2)}) collective-permute-start(bf16[6,2,16,1024]{3,2,1,0:T(8,128)(2,1)S(1)} %get-tuple-element.116), channel_id=1, source_target_pairs={{2,0},{4,2},{6,4},{7,6},{5,7},{3,5},{1,3},{0,1},{10,8},{12,10},{14... | collective-permute-start | bytes 1179656 | tf_op jit(solution)/shard_map/ppermute | solution.py:587
  303.8 16.3 %collective-permute-start.77 = (bf16[9,2,16,1024]{3,2,1,0:T(8,128)(2,1)S(1)}, bf16[9,2,16,1024]{3,2,1,0:T(8,128)(2,1)S(1)}, u32[]{:S(2)}, u32[]{:S(2)}) collective-permute-start(bf16[9,2,16,1024]{3,2,1,0:T(8,128)(2,1)S(1)} %collective-permute-done.75.refs_1_), channel_id=1, source_target_pairs={{0,2},{2,4},{4,6},{6,7},{7,5},{5,3},{3,1},{1,0},{8,10},{10,12},{12... | collective-permute-start | bytes 1769480 | tf_op jit(solution)/shard_map/ppermute | solution.py:583
  319.3 21.9 %collective-permute-start.78 = (bf16[9,2,16,1024]{3,2,1,0:T(8,128)(2,1)S(1)}, bf16[9,2,16,1024]{3,2,1,0:T(8,128)(2,1)S(1)}, u32[]{:S(2)}, u32[]{:S(2)}) collective-permute-start(bf16[9,2,16,1024]{3,2,1,0:T(8,128)(2,1)S(1)} %collective-permute-done.76.refs_2_), channel_id=1, source_target_pairs={{2,0},{4,2},{6,4},{7,6},{5,7},{3,5},{1,3},{0,1},{10,8},{12,10},{14... | collective-permute-start | bytes 1769480 | tf_op jit(solution)/shard_map/ppermute | solution.py:587
  320.2 21.6 %collective-permute-start.79 = (bf16[9,2,16,1024]{3,2,1,0:T(8,128)(2,1)S(1)}, bf16[9,2,16,1024]{3,2,1,0:T(8,128)(2,1)S(1)}, u32[]{:S(2)}, u32[]{:S(2)}) collective-permute-start(bf16[9,2,16,1024]{3,2,1,0:T(8,128)(2,1)S(1)} %collective-permute-done.77.refs_3_), channel_id=1, source_target_pairs={{0,2},{2,4},{4,6},{6,7},{7,5},{5,3},{3,1},{1,0},{8,10},{10,12},{12... | collective-permute-start | bytes 1769480 | tf_op jit(solution)/shard_map/ppermute | solution.py:583
  324.5 47.9 %collective-permute-start.36 = (bf16[256,1024]{1,0:T(8,128)(2,1)S(1)}, bf16[256,1024]{1,0:T(8,128)(2,1)S(1)}, u32[]{:S(2)}, u32[]{:S(2)}) collective-permute-start(bf16[256,1024]{1,0:T(8,128)(2,1)S(1)} %copy-done.53), channel_id=1, source_target_pairs={{0,8},{8,0},{16,24},{24,16},{1,9},{9,1},{17,25},{25,17},{2,10},{10... | collective-permute-start | bytes 1572872 | tf_op jit(solution)/shard_map/ppermute | solution.py:590
  328.5 19.6 %collective-permute-start.59 = (bf16[4,2,16,1536]{3,2,1,0:T(8,128)(2,1)S(1)}, bf16[4,2,16,1536]{3,2,1,0:T(8,128)(2,1)S(1)}, u32[]{:S(2)}, u32[]{:S(2)}) collective-permute-start(bf16[4,2,16,1536]{3,2,1,0:T(8,128)(2,1)S(1)} %collective-permute-done.57.refs_1_), channel_id=1, source_target_pairs={{0,2},{2,4},{4,6},{6,7},{7,5},{5,3},{3,1},{1,0},{8,10},{10,12},{12... | collective-permute-start | bytes 1179656 | tf_op jit(solution)/shard_map/ppermute | solution.py:583
  330.6 19.2 %collective-permute-start.60 = (bf16[4,2,16,1536]{3,2,1,0:T(8,128)(2,1)S(1)}, bf16[4,2,16,1536]{3,2,1,0:T(8,128)(2,1)S(1)}, u32[]{:S(2)}, u32[]{:S(2)}) collective-permute-start(bf16[4,2,16,1536]{3,2,1,0:T(8,128)(2,1)S(1)} %collective-permute-done.58.refs_2_), channel_id=1, source_target_pairs={{2,0},{4,2},{6,4},{7,6},{5,7},{3,5},{1,3},{0,1},{10,8},{12,10},{14... | collective-permute-start | bytes 1179656 | tf_op jit(solution)/shard_map/ppermute | solution.py:587
  341.2 21.1 %collective-permute-start.80 = (bf16[9,2,16,1024]{3,2,1,0:T(8,128)(2,1)S(1)}, bf16[9,2,16,1024]{3,2,1,0:T(8,128)(2,1)S(1)}, u32[]{:S(2)}, u32[]{:S(2)}) collective-permute-start(bf16[9,2,16,1024]{3,2,1,0:T(8,128)(2,1)S(1)} %collective-permute-done.78.refs_4_), channel_id=1, source_target_pairs={{2,0},{4,2},{6,4},{7,6},{5,7},{3,5},{1,3},{0,1},{10,8},{12,10},{14... | collective-permute-start | bytes 1769480 | tf_op jit(solution)/shard_map/ppermute | solution.py:587
  341.8 31.1 %collective-permute-start.38 = (bf16[256,1024]{1,0:T(8,128)(2,1)S(1)}, bf16[256,1024]{1,0:T(8,128)(2,1)S(1)}, u32[]{:S(2)}, u32[]{:S(2)}) collective-permute-start(bf16[256,1024]{1,0:T(8,128)(2,1)S(1)} %slice_add_fusion.2), channel_id=1, source_target_pairs={{0,16},{8,24},{16,0},{24,8},{1,17},{9,25},{17,1},{25,9},{2,18},{10... | collective-permute-start | bytes 1572872 | tf_op jit(solution)/shard_map/ppermute | solution.py:590
  349.8 20.9 %collective-permute-start.62 = (bf16[4,2,16,1536]{3,2,1,0:T(8,128)(2,1)S(1)}, bf16[4,2,16,1536]{3,2,1,0:T(8,128)(2,1)S(1)}, u32[]{:S(2)}, u32[]{:S(2)}) collective-permute-start(bf16[4,2,16,1536]{3,2,1,0:T(8,128)(2,1)S(1)} %collective-permute-done.60.refs_4_), channel_id=1, source_target_pairs={{2,0},{4,2},{6,4},{7,6},{5,7},{3,5},{1,3},{0,1},{10,8},{12,10},{14... | collective-permute-start | bytes 1179656 | tf_op jit(solution)/shard_map/ppermute | solution.py:587
  (114 other events, 1009.5 us)

commit v3 on v2

--- a/solution.py
+++ b/solution.py
@@ -12,7 +12,8 @@
 theta_base = 1000000.0
 f32 = jnp.float32
 bf16 = jnp.bfloat16
-vmem_bytes = 50 * 1024 * 1024
+vmem_bytes = 32 * 1024 * 1024
+vmem_wide = 52 * 1024 * 1024
 
 
 def dot(left, right):
@@ -37,8 +38,8 @@
     )
 
 
-def params():
-    return pltpu.CompilerParams(vmem_limit_bytes=vmem_bytes)
+def params(limit=vmem_bytes):
+    return pltpu.CompilerParams(vmem_limit_bytes=limit)
 
 
 def cost(flops, moved, trans=0):
@@ -113,7 +114,7 @@
             jax.ShapeDtypeStruct((total, kv), bf16),
         ],
         scratch_shapes=[pltpu.VMEM((block, width), bf16)],
-        compiler_params=params(),
+        compiler_params=params(vmem_wide),
         cost_estimate=cost(2 * total * weight.size, 2 * weight.size + total * width * 12),
     )(gain, weight, cosine, sine, gains, *tok)
 
@@ -312,7 +313,7 @@
         + [jax.ShapeDtypeStruct((block * count, width), bf16)] * 2,
         scratch_shapes=[pltpu.VMEM((block, width), bf16)] * 2,
         input_output_aliases={2 + 2 * count + i: i for i in range(len(before))},
-        compiler_params=params(),
+        compiler_params=params(vmem_wide),
         cost_estimate=cost(
             12 * block * count * down.size, 6 * down.size + block * count * width * 16,
             block * count * units,
@@ -449,14 +450,14 @@
     )(scalars, *inputs)
 
 
-def cut_kernel(sizes, scalars, *refs):
+def cut_kernel(sizes, which, scalars, *refs):
     inputs, (own, near, piece) = refs[: len(sizes)], refs[len(sizes) :]
-    mine, y = scalars[0], scalars[1]
+    mine, part = scalars[0], scalars[which]
     half = piece.shape[1]
     begin = 0
     for ref, size in zip(inputs, sizes):
         lanes = lambda i: pl.ds(pl.multiple_of((mine ^ i) * size, 128), size)
-        rows = pl.ds(pl.multiple_of(y * half, 16), half)
+        rows = pl.ds(pl.multiple_of(part * half, 16), half)
         own[:, begin : begin + size] = ref[:, lanes(0)]
         near[:, begin : begin + size] = ref[:, lanes(1)]
         piece[0, :, begin : begin + size] = ref[rows, lanes(2)]
@@ -464,13 +465,13 @@
         begin += size
 
 
-def cut(scalars, inputs, sizes):
+def cut(scalars, inputs, sizes, parts):
     rows = inputs[0].shape[0]
     wide = sum(sizes)
     whole = pl.BlockSpec(memory_space=pltpu.VMEM)
-    shapes = [(rows, wide), (rows, wide), (2, rows // 2, wide)]
+    shapes = [(rows, wide), (rows, wide), (2, rows // parts, wide)]
     return pl.pallas_call(
-        functools.partial(cut_kernel, sizes),
+        functools.partial(cut_kernel, sizes, parts // 2 if parts == 2 else 3),
         in_specs=[pl.BlockSpec(memory_space=pltpu.SMEM)] + [whole] * len(inputs),
         out_specs=[whole] * 3,
         out_shape=[jax.ShapeDtypeStruct(shape, bf16) for shape in shapes],
@@ -576,7 +577,8 @@
         self.bits = {1: rep % 2, 2: (rep // 2) % 2, 4: rep // 4}
         self.pos = jnp.where(rep % 2 == 0, rep // 2, 7 - rep // 2)
         self.ring = [0, 2, 4, 6, 7, 5, 3, 1]
-        self.scalars = jnp.stack([self.mine, self.bits[1], self.pos]).astype(jnp.int32)
+        self.quarter = self.bits[1] * 2 + self.bits[2]
+        self.scalars = jnp.stack([self.mine, self.bits[1], self.pos, self.quarter]).astype(jnp.int32)
 
     def up(self, item):
         ring = self.ring
@@ -612,20 +614,7 @@
         return near_part[:rows].astype(f32) + near.astype(f32) + far.astype(f32)
 
     def ring_scatter(self, shares, layout, blocks):
-        step = functools.partial(ring_step, shares, layout, blocks)
-        chunk = lambda offset: (self.pos + offset) % 8
-        both = (0, 1)
-        u, d = step([chunk(4)], [(0, (0,), []), (0, (1,), [])], [])
-        u, d = self.up(u), self.down(d)
-        plan = [(0, both, [(0, (0,))]), (1, both, [(1, (1,))])]
-        u, d = step([chunk(3), chunk(5)], plan, [u, d])
-        u, d = self.up(u), self.down(d)
-        plan = [(0, both, [(0, both)]), (1, both, [(1, both)])]
-        u, d = step([chunk(2), chunk(6)], plan, [u, d])
-        u, d = self.up(u), self.down(d)
-        u, d = step([chunk(1), chunk(7)], plan, [u, d])
-        u, d = self.up(u), self.down(d)
-        return step([chunk(0)], [(0, both, [(0, both), (1, both)])], [u, d])[0]
+        return RingSum(self, shares, layout, blocks)
 
     def ring_gather(self, item):
         u1, d1 = self.up(item), self.down(item)
@@ -642,6 +631,36 @@
         near = self.swap(near, 1)
         far = self.swap(jnp.concatenate([far, near[1:]], axis=0), 2)
         return own, near, far
+
+
+class RingSum:
+    def __init__(self, moves, shares, layout, blocks):
+        self.moves = moves
+        self.step = functools.partial(ring_step, shares, layout, blocks)
+        self.send(*self.step([self.chunk(4)], [(0, (0,), []), (0, (1,), [])], []))
+        self.at = 4
+
+    def chunk(self, offset):
+        return (self.moves.pos + offset) % 8
+
+    def send(self, u, d):
+        self.sent = u
+        self.arrived = [self.moves.up(u), self.moves.down(d)]
+
+    def advance(self, *before):
+        self.at -= 1
+        both = (0, 1)
+        u, d = self.arrived
+        u = after(u, *before) if before else u
+        held = [(0,), (1,)] if self.at == 3 else [both, both]
+        plan = [(0, both, [(0, held[0])]), (1, both, [(1, held[1])])]
+        self.send(*self.step([self.chunk(self.at), self.chunk(8 - self.at)], plan, [u, d]))
+
+    def finish(self, *before):
+        both = (0, 1)
+        u, d = self.arrived
+        u = after(u, *before) if before else u
+        return self.step([self.chunk(0)], [(0, both, [(0, both), (1, both)])], [u, d])[0]
 
 
 class Fetch:
@@ -667,6 +686,34 @@
             (4, (0,), (0, half), (0, width), 0, lambda shard, y, *_: spot(shard ^ 2, (1 - y) * half)),
             (5, (), (0, half), (0, width), 0, lambda shard, y, *_: spot(shard ^ 3, (1 - y) * half)),
         ]
+        return place(moves.scalars, inputs, [(self.shape, bf16)], todo)[0]
+
+
+class DeepFetch(Fetch):
+    def start(self, *before):
+        moves = self.moves
+        self.here = moves.swap(after(self.piece, *before), 2)
+        pair = jnp.concatenate([self.here, moves.cross_rep(self.here, 1)], axis=0)
+        self.parts = [pair, moves.cross_rep(pair, 2)]
+
+    def finish(self):
+        moves, spot = self.moves, self.spot
+        first, second = self.parts
+        rows, width = self.own.shape
+        size = rows // 4
+        cross = moves.swap(jnp.stack([first[1], first[3], second[1], second[3]]), 1)
+        inputs = [self.own, moves.swap(self.near, 1), first, second, cross]
+        todo = [
+            (0, (), (0, rows), (0, width), 0, lambda shard, *_: spot(shard, 0)),
+            (1, (), (0, rows), (0, width), 0, lambda shard, *_: spot(shard ^ 1, 0)),
+        ]
+        for i, (source, index, mask) in enumerate([(2, 0, 0), (2, 2, 2), (3, 0, 1), (3, 2, 3)]):
+            for which, where, at in ((2, source, index), (3, 4, i)):
+
+                def to(shard, y, pos, quarter, which=which, mask=mask):
+                    return spot(shard ^ which, (quarter ^ mask) * size)
+
+                todo.append((where, (at,), (0, size), (0, width), 0, to))
         return place(moves.scalars, inputs, [(self.shape, bf16)], todo)[0]
 
 
@@ -692,6 +739,16 @@
     own_tokens = tokens[0]
     cot = grad_out[0]
 
+    if direct:
+        by_rows = lambda source, line: (source * slice_width + line, 0)
+        qkv = Fetch(
+            moves,
+            *cut(moves.scalars, [query_weight, key_matrix, value_matrix], [q_width, k_width, k_width], 2),
+            by_rows,
+            (width, q_width + 2 * k_width),
+        )
+        qkv.start()
+        attention_gain = after(attention_gain, qkv.here)
     small = jnp.concatenate(
         [attention_gain, mlp_gain, query_gain, key_gain, segments[0].astype(bf16)]
     )[None]
@@ -723,13 +780,6 @@
 
     all_tokens = all_cot = None
     if direct:
-        by_rows = lambda source, line: (source * slice_width + line, 0)
-        qkv = Fetch(
-            moves,
-            *cut(moves.scalars, [query_weight, key_matrix, value_matrix], [q_width, k_width, k_width]),
-            by_rows,
-            (width, q_width + 2 * k_width),
-        )
         outer = lambda i, begin, n: lax.dynamic_slice(
             output_weight, ((mine ^ i) * q_width + begin, 0), (n, slice_width)
         )
@@ -742,13 +792,12 @@
             lambda source, line: (line, source * slice_width),
             (q_width, width),
         )
-        both = Fetch(
+        both = DeepFetch(
             moves,
-            *cut(moves.scalars, [gate_weight, up_weight], [units, units]),
+            *cut(moves.scalars, [gate_weight, up_weight], [units, units], 4),
             by_rows,
             (width, 2 * units),
         )
-        qkv.start()
         all_tokens = moves.gather(after(own_tokens, qkv.here))
         output.start(all_tokens[2], qkv.there)
         qkv_weight = qkv.finish()
@@ -784,51 +833,23 @@
         normed_two, all_cot, feed_weight, down_weight, 0, shards, []
     )
     hidden, gate_grad, up_grad, normed_two, all_cot = kept
+    if direct:
+        crossed = norm_grad[2 * rows : 3 * rows] + moves.swap(norm_grad[3 * rows :], 1)
+        hidden, gate_grad = after(hidden, crossed), after(gate_grad, crossed)
+        up_grad = after(up_grad, crossed)
+        near_grad = norm_grad[:rows].astype(f32) + moves.swap(norm_grad[rows : 2 * rows], 1).astype(f32)
+        normed_grad_two = near_grad + moves.swap(crossed, 2).astype(f32)
+    else:
+        normed_grad_two = moves.scatter(norm_grad[:split], norm_grad[split:])
     share_down = dot_tn(hidden, all_cot).astype(bf16)
     share_gate = dot_tn(normed_two, gate_grad).astype(bf16)
     share_up = dot_tn(normed_two, up_grad).astype(bf16)
-    normed_grad_two = moves.scatter(norm_grad[:split], norm_grad[split:])
     mlp_gain_part = jnp.sum(normed_grad_two * residual_one * residual_scale, axis=0)
     residual_grad = cot.astype(f32) + norm_back(
         normed_grad_two * second_gain, residual_one, residual_scale
     )
-    branch_grad = moves.gather(residual_grad.astype(bf16))
-
-    out_part = after(out_part, *branch_grad)
-    layer_out = (residual_one + moves.scatter(out_part[:split], out_part[split:])).astype(bf16)
-
-    out_grad, branch_grad = branch_back(branch_grad, out_weight)
-    share_out = dot_tn(attended_low, branch_grad).astype(bf16)
-    query_grad, key_grad, val_grad = attend_back(
-        order, rot, val, out_grad, attended, logs, seg_col, seg_row, q_heads, k_heads, head, shards
-    )
-    query_lin_grad, pair_lin_grad, norm_one_part, gain_part, head_part = unproject(
-        query_grad, key_grad, val_grad, lin, cosine, sine, head_gains, qkv_weight, all_tokens,
-        q_heads, k_heads,
-    )
-    share_query = dot_tn(normed_one, query_lin_grad).astype(bf16)
-    share_pair = dot_tn(normed_one, pair_lin_grad).astype(bf16)
-    normed_grad_one = moves.scatter(norm_one_part[:split], norm_one_part[split:])
-    grad_tokens = residual_grad + norm_back(normed_grad_one * input_gain, inputs, inverse_root(inputs))
-
-    gains = jnp.concatenate([gain_part[0], mlp_gain_part, head_part.reshape(2 * head)])[None]
-    if direct:
-        gains = gains + moves.swap(gains, 1)
-        gains = gains + moves.swap(gains, 2)
-        for mask in (1, 2, 4):
-            gains = gains + moves.cross_rep(gains, mask)
-    else:
-        gains = lax.psum(gains, ("shard", "rep"))
-    gains = gains[0]
-
-    def own_part(begin, size):
-        return lax.dynamic_slice_in_dim(gains, begin + mine * size, size, 0)
-
-    grad_attention_gain = own_part(0, slice_width)
-    grad_mlp_gain = own_part(width, slice_width)
-    grad_query_gain = own_part(2 * width, head_slice)
-    grad_key_gain = own_part(2 * width + head, head_slice)
-
+    branch_low = residual_grad.astype(bf16)
+    branch_grad = moves.gather(branch_low)
     if direct:
         lines = slice_width // 16
         rest = 2 * units - width
@@ -845,9 +866,55 @@
                 (1, i, width - units, rest, 4 + i // 2, (i % 2) * rest),
             ]
         layout += [(2, b, 0, width, 6 + b, 0) for b in range(downs)]
-        chunk = moves.ring_scatter(
+        ring = moves.ring_scatter(
             [as_chunks(share_gate), as_chunks(share_up), as_chunks(share_down)], layout, blocks
         )
+        ring.advance(branch_low)
+
+    out_part = after(out_part, *branch_grad)
+    layer_out = (residual_one + moves.scatter(out_part[:split], out_part[split:])).astype(bf16)
+
+    far_branch = branch_grad[2]
+    out_grad, branch_grad = branch_back(branch_grad, out_weight)
+    share_out = dot_tn(attended_low, branch_grad).astype(bf16)
+    if direct:
+        ring.advance(far_branch)
+        out_grad = after(out_grad, ring.sent)
+    query_grad, key_grad, val_grad = attend_back(
+        order, rot, val, out_grad, attended, logs, seg_col, seg_row, q_heads, k_heads, head, shards
+    )
+    if direct:
+        ring.advance(query_grad)
+        query_grad = after(query_grad, ring.sent)
+    query_lin_grad, pair_lin_grad, norm_one_part, gain_part, head_part = unproject(
+        query_grad, key_grad, val_grad, lin, cosine, sine, head_gains, qkv_weight, all_tokens,
+        q_heads, k_heads,
+    )
+    share_query = dot_tn(normed_one, query_lin_grad).astype(bf16)
+    share_pair = dot_tn(normed_one, pair_lin_grad).astype(bf16)
+    normed_grad_one = moves.scatter(norm_one_part[:split], norm_one_part[split:])
+    grad_tokens = residual_grad + norm_back(normed_grad_one * input_gain, inputs, inverse_root(inputs))
+
+    gains = jnp.concatenate([gain_part[0], mlp_gain_part, head_part.reshape(2 * head)])[None]
+    if direct:
+        gains = gains + moves.swap(gains, 1)
+        gains = gains + moves.swap(gains, 2)
+        for mask in (1, 2, 4):
+            gains = gains + moves.cross_rep(gains, mask)
+    else:
+        gains = lax.psum(gains, ("shard", "rep"))
+    gains = gains[0]
+
+    def own_part(begin, size):
+        return lax.dynamic_slice_in_dim(gains, begin + mine * size, size, 0)
+
+    grad_attention_gain = own_part(0, slice_width)
+    grad_mlp_gain = own_part(width, slice_width)
+    grad_query_gain = own_part(2 * width, head_slice)
+    grad_key_gain = own_part(2 * width + head, head_slice)
+
+    if direct:
+        chunk = ring.finish()
         own, near, far = moves.exchange(
             chunk, lambda at: [(at, 0, width), (4 + at // 2, (at % 2) * rest, rest)], 2 * units
         )
@@ -891,6 +958,8 @@
             moves.scalars, [part for part, _, _ in parts], shapes, todo
         )
 
+        first_near, first_packed = near, parts[0][0]
+
         outs = q_width // slice_width
         pair = 2 * k_width
         wide = q_width + pair
@@ -898,11 +967,15 @@
         for i in range(4):
             layout += [(0, i, 0, q_width, i, 0), (1, i, 0, pair, i, q_width)]
         layout += [(2, b, 0, width, 4 + b, 0) for b in range(outs)]
-        chunk = moves.ring_scatter(
+        ring = moves.ring_scatter(
             [as_chunks(share_query), as_chunks(share_pair), as_chunks(share_out)],
             layout,
             (4 + outs, width),
         )
+        ring.advance(first_near)
+        ring.advance(first_packed)
+        ring.advance()
+        chunk = ring.finish()
         own, near, far = moves.exchange(
             chunk,
             lambda at: [(at, 0, wide)] + [(4 + b, at * slice_width, slice_width) for b in range(outs)],

time: 392 us -> 368 us (0.939)
  Pallas kernels: 98.8 us -> 78.1 us
  other arithmetic: 23.2 us -> 17.9 us
    ppermute x16, waiting for transfers between devices: 33.3 us -> 8.77 us  [down(): lax.ppermute(item, 'rep', [(ring[(i + 1) % 8], ring[i]) for i in range(8)])]
    ppermute x16, waiting for transfers between devices: 41 us -> 61.4 us  [up(): lax.ppermute(item, 'rep', [(ring[i], ring[(i + 1) % 8]) for i in range(8)])]
    pallas_call x10, Pallas kernels: 18.6 us -> 8.98 us  [ring_step(): pl.pallas_call(functools.partial(ring_kernel, layout, plan, len(shares),...]
    ppermute x6 -> x7, waiting for transfers between devices: 27.3 us -> 32.9 us  [cross_rep(): return lax.ppermute(item, 'rep', [(i, i ^ mask) for i in range(8)])]
    unnamed x132 -> x159, local copies, waits for them, and re-layouts: 19.8 us -> 25.1 us
    ppermute x16, starting transfers between devices: 10.5 us -> 15.7 us  [down(): lax.ppermute(item, 'rep', [(ring[(i + 1) % 8], ring[i]) for i in range(8)])]
    ppermute x16, starting transfers between devices: 21.8 us -> 17.6 us  [up(): lax.ppermute(item, 'rep', [(ring[i], ring[(i + 1) % 8]) for i in range(8)])]
    ppermute x6 -> x7, starting transfers between devices: 4.59 us -> 8.27 us  [cross_rep(): return lax.ppermute(item, 'rep', [(i, i ^ mask) for i in range(8)])]
  transfers between devices with their start and end apart: 83 -> 83, of which waited for: 34 -> 33; matrix products, arithmetic and copies ran while one was open for 13% -> 10% of each run, Pallas kernels for 20% -> 15%
where the time goes in v3:
time: 368 us; the launch traced here: 363 us
  waiting for transfers between devices  154 us (42%)
  Pallas kernels  78.1 us (21%)
  starting transfers between devices  62.3 us (17%)
  local copies, waits for them, and re-layouts  35.5 us (10%)
  other arithmetic  17.9 us (5%)
  matrix products  12.6 us (3%)
    ppermute x16, waiting for transfers between devices, up(): lax.ppermute(item, 'rep', [(ring[i], ring[(i + 1) % 8]) for i in range(8)])  61.4 us
    ppermute x44, waiting for transfers between devices, swap(): return lax.ppermute(item, 'shard', [(i, i ^ mask) for i in range(4)])  51.4 us
    ppermute x7, waiting for transfers between devices, cross_rep(): return lax.ppermute(item, 'rep', [(i, i ^ mask) for i in range(8)])  32.9 us
    unnamed x159, local copies, waits for them, and re-layouts  25.1 us
    ppermute x44, starting transfers between devices, swap(): return lax.ppermute(item, 'shard', [(i, i ^ mask) for i in range(4)])  20.8 us
    ppermute x16, starting transfers between devices, up(): lax.ppermute(item, 'rep', [(ring[i], ring[(i + 1) % 8]) for i in range(8)])  17.6 us
    pallas_call x1, Pallas kernels, feed(): pl.pallas_call(functools.partial(feed_kernel, count, len(before)), grid=(...  16.8 us
    ppermute x16, starting transfers between devices, down(): lax.ppermute(item, 'rep', [(ring[(i + 1) % 8], ring[i]) for i in range(8)])  15.7 us
  transfers between devices with their start and end apart: 83, of which 33 were waited for; matrix products, arithmetic and copies ran while one was open for 10% of the time, Pallas kernels for 15%

profile of v3, /device:TPU:0, one launch (start us, length us, event | category | flops | bytes accessed | tf_op | source)
XLA Modules:
  0.0 362.9 jit_solution(6036399925087689542)
XLA Ops:
  6.4 2.9 collective-permute-start
  13.0 8.3 %collective-permute-done.refs_2_ = bf16[2,128,1024]{2,1,0:T(8,128)(2,1)S(1)} collective-permute-done((bf16[2,128,1024]{2,1,0:T(8,128)(2,1)S(1)}, bf16[2,128,1024]{2,1,0:T(8,128)(2,1)S(1)}, u32[]{:S(2)}, u32[]{:S(2)}) %collective-permute-start) | collective-permute-done | bytes 524320 | tf_op jit(solution)/shard_map/ppermute | solution.py:592
  37.0 6.4 %collective-permute-done.6.refs_4_ = bf16[2,128,1024]{2,1,0:T(8,128)(2,1)S(1)} collective-permute-done((bf16[2,128,1024]{2,1,0:T(8,128)(2,1)S(1)}, bf16[2,128,1024]{2,1,0:T(8,128)(2,1)S(1)}, u32[]{:S(2)}, u32[]{:S(2)}) %collective-permute-start.6) | collective-permute-done | bytes 524320 | tf_op jit(solution)/shard_map/ppermute | solution.py:595
  47.4 3.8 %collective-permute-done.11.refs_2_ = bf16[2,256,256]{2,1,0:T(8,128)(2,1)S(1)} collective-permute-done((bf16[2,256,256]{2,1,0:T(8,128)(2,1)}, bf16[2,256,256]{2,1,0:T(8,128)(2,1)S(1)}, u32[]{:S(2)}, u32[]{:S(2)}) %collective-permute-start.11) | collective-permute-done | bytes 262176 | tf_op jit(solution)/shard_map/ppermute | solution.py:592
  58.4 8.2 %shard_map.257 = (bf16[1024,1024]{1,0:T(8,128)(2,1)}, f32[1024,768]{1,0:T(8,128)}, bf16[1024,768]{1,0:T(8,128)(2,1)}, bf16[1024,256]{1,0:T(8,128)(2,1)S(1)}) custom-call(f32[1,1024]{1,0:T(1,128)S(1)} %bitcast.143, bf16[1024,1024]{1,0:T(8,128)(2,1)} %copy-done.4, f32[1024,128]{1,0:T(8,128)S(1)} %get-tuple-element.205.cosine, ...), custom_call_target="tpu_custom_call" | custom-call | flops 2147483648 | bytes 14680064 | tf_op jit(solution)/shard_map/pallas_call | solution.py:98
  68.4 4.4 %shard_map.258 = (f32[1024,512]{1,0:T(8,128)S(1)}, bf16[1024,512]{1,0:T(8,128)(2,1)S(1)}, f32[1024,512]{1,0:T(8,128)S(1)}) custom-call(s32[1]{0:T(128)} %bitcast.1.order, bf16[1024,768]{1,0:T(8,128)(2,1)S(1)} %copy-done.40, bf16[1024,768]{1,0:T(8,128)(2,1)S(1)} %copy-done.40, bf16[1024,256]{1,0:T(8,128)(2,1)S(1)} %get-tuple-element.95.val, ...), custom_call_target="tpu_custom_call" | custom-call | flops 2147483648 | bytes 6291456 | tf_op jit(solution)/shard_map/pallas_call | solution.py:171
  80.0 8.3 %collective-permute-done.21 = bf16[2,64,1536]{2,1,0:T(8,128)(2,1)S(1)} collective-permute-done((bf16[2,64,1536]{2,1,0:T(8,128)(2,1)S(1)}, bf16[2,64,1536]{2,1,0:T(8,128)(2,1)S(1)}, u32[]{:S(2)}, u32[]{:S(2)}) %collective-permute-start.21) | collective-permute-done | bytes 393248 | tf_op jit(solution)/shard_map/ppermute | solution.py:595
  94.7 12.5 %collective-permute-done.22.refs_3_ = bf16[4,64,1536]{2,1,0:T(8,128)(2,1)S(1)} collective-permute-done((bf16[4,64,1536]{2,1,0:T(8,128)(2,1)S(1)}, bf16[4,64,1536]{2,1,0:T(8,128)(2,1)S(1)}, u32[]{:S(2)}, u32[]{:S(2)}) %collective-permute-start.22) | collective-permute-done | bytes 786464 | tf_op jit(solution)/shard_map/ppermute | solution.py:595
  108.4 5.8 %collective-permute-done.25.refs_2_ = bf16[256,1024]{1,0:T(8,128)(2,1)S(1)} collective-permute-done((bf16[256,1024]{1,0:T(8,128)(2,1)S(1)}, bf16[256,1024]{1,0:T(8,128)(2,1)S(1)}, u32[]{:S(2)}, u32[]{:S(2)}) %collective-permute-start.25) | collective-permute-done | bytes 524320 | tf_op jit(solution)/shard_map/ppermute | solution.py:592
  118.5 16.8 %shard_map.262 = (bf16[1024,768]{1,0:T(8,128)(2,1)}, bf16[1024,768]{1,0:T(8,128)(2,1)}, bf16[1024,768]{1,0:T(8,128)(2,1)}, bf16[1024,1024]{1,0:T(8,128)(2,1)}, b...) custom-call(bf16[1024,1536]{1,0:T(8,128)(2,1)} %copy-done.12, ...), custom_call_target="tpu_custom_call" | custom-call | flops 9663676416 | bytes 21495808 | tf_op jit(solution)/shard_map/pallas_call | solution.py:305
  142.0 3.6 convolution_convert_fusion.1
  147.5 8.0 %collective-permute-done.32 = bf16[256,1024]{1,0:T(8,128)(2,1)S(1)} collective-permute-done((bf16[256,1024]{1,0:T(8,128)(2,1)S(1)}, bf16[256,1024]{1,0:T(8,128)(2,1)S(1)}, u32[]{:S(2)}, u32[]{:S(2)}) %collective-permute-start.32) | collective-permute-done | bytes 524320 | tf_op jit(solution)/shard_map/ppermute | solution.py:592
  164.0 6.6 %collective-permute-done.39.refs_6_ = bf16[9,1,16,1024]{3,2,1,0:T(8,128)(2,1)S(1)} collective-permute-done((bf16[9,1,16,1024]{3,2,1,0:T(8,128)(2,1)}, bf16[9,1,16,1024]{3,2,1,0:T(8,128)(2,1)S(1)}, u32[]{:S(2)}, u32[]{:S(2)}) %collective-permute-start.39) | collective-permute-done | bytes 294944 | tf_op jit(solution)/shard_map/ppermute | solution.py:585
  173.4 2.6 shard_map.265
  178.8 11.2 %collective-permute-done.41.refs_6_ = bf16[9,2,16,1024]{3,2,1,0:T(8,128)(2,1)} collective-permute-done((bf16[9,2,16,1024]{3,2,1,0:T(8,128)(2,1)}, bf16[9,2,16,1024]{3,2,1,0:T(8,128)(2,1)}, u32[]{:S(2)}, u32[]{:S(2)}) %collective-permute-start.41) | collective-permute-done | bytes 589856 | tf_op jit(solution)/shard_map/ppermute | solution.py:585
  196.9 4.1 %shard_map.263 = (bf16[1024,512]{1,0:T(8,128)(2,1)S(1)}, bf16[1024,1024]{1,0:T(8,128)(2,1)S(1)}) custom-call(bf16[512,1024]{1,0:T(8,128)(2,1)S(1)} %copy-done.22, bf16[256,1024]{1,0:T(8,128)(2,1)} %get-tuple-element.171.refs_0_, bf16[256,1024]{1,0:T(8,128)(2,1)} %collective-permute-done.33.refs_1_, bf16[256,1024]{1,0:T(8,128)(2,1)} %collective-permute-done.34.refs_2_, ...), custom_call_target="tpu_custom_call" | custom-call | flops 1073741824 | bytes 7340032 | tf_op jit(solution)/shard_map/pallas_call | solution.py:336
  203.3 10.3 %shard_map.267 = (f32[1024,512]{1,0:T(8,128)S(1)}, f32[1024,256]{1,0:T(8,128)S(1)}, f32[1024,256]{1,0:T(8,128)S(1)}) custom-call(s32[1]{0:T(128)} %bitcast.1.order, bf16[1024,768]{1,0:T(8,128)(2,1)S(1)} %copy-done.41, bf16[1024,768]{1,0:T(8,128)(2,1)S(1)} %copy-done.41, bf16[1024,256]{1,0:T(8,128)(2,1)S(1)} %copy-done.47, ...), custom_call_target="tpu_custom_call" | custom-call | flops 5368709120 | bytes 10485760 | tf_op jit(solution)/shard_map/pallas_call | solution.py:244
  216.6 9.9 %shard_map.269 = (bf16[1024,512]{1,0:T(8,128)(2,1)S(1)}, bf16[1024,512]{1,0:T(8,128)(2,1)S(1)}, bf16[1024,1024]{1,0:T(8,128)(2,1)S(1)}, f32[1,1024]{1,0:T(1,128)S(1)}, f32[2,128]{1,0:T(2,128)S(1)}) custom-call(f32[1024,512]{1,0:T(8,128)S(1)} %get-tuple-element.130.query_grad, f32[1024,256]{1,0:T(8,128)S(1)} %get-tuple-element.131.key_grad, ...), custom_call_target="tpu_custom_call" | custom-call | flops 2147483648 | bytes 18874368 | tf_op jit(solution)/shard_map/pallas_call | solution.py:395
  232.2 2.7 collective-permute-done.53.refs_6_
  234.9 4.1 %collective-permute-done.57.refs_7_ = bf16[6,1,16,1024]{3,2,1,0:T(8,128)(2,1)S(1)} collective-permute-done((bf16[6,1,16,1024]{3,2,1,0:T(8,128)(2,1)S(1)}, bf16[6,1,16,1024]{3,2,1,0:T(8,128)(2,1)S(1)}, u32[]{:S(2)}, u32[]{:S(2)}) %collective-permute-start.57) | collective-permute-done | bytes 196640 | tf_op jit(solution)/shard_map/ppermute | solution.py:589
  242.3 5.4 %collective-permute-done.59.refs_2_ = bf16[2,2,16,1536]{3,2,1,0:T(8,128)(2,1)S(1)} collective-permute-done((bf16[2,2,16,1536]{3,2,1,0:T(8,128)(2,1)S(1)}, bf16[2,2,16,1536]{3,2,1,0:T(8,128)(2,1)S(1)}, u32[]{:S(2)}, u32[]{:S(2)}) %collective-permute-start.59) | collective-permute-done | bytes 196640 | tf_op jit(solution)/shard_map/ppermute | solution.py:592
  247.8 2.6 collective-permute-done.58.refs_6_
  255.2 6.4 %collective-permute-done.61.refs_6_ = bf16[6,2,16,1024]{3,2,1,0:T(8,128)(2,1)S(1)} collective-permute-done((bf16[6,2,16,1024]{3,2,1,0:T(8,128)(2,1)S(1)}, bf16[6,2,16,1024]{3,2,1,0:T(8,128)(2,1)S(1)}, u32[]{:S(2)}, u32[]{:S(2)}) %collective-permute-start.61) | collective-permute-done | bytes 393248 | tf_op jit(solution)/shard_map/ppermute | solution.py:585
  265.5 3.2 collective-permute-done.49
  282.9 5.6 %collective-permute-done.66.refs_2_ = bf16[2,2,16,1536]{3,2,1,0:T(8,128)(2,1)S(1)} collective-permute-done((bf16[2,2,16,1536]{3,2,1,0:T(8,128)(2,1)S(1)}, bf16[2,2,16,1536]{3,2,1,0:T(8,128)(2,1)S(1)}, u32[]{:S(2)}, u32[]{:S(2)}) %collective-permute-start.66) | collective-permute-done | bytes 196640 | tf_op jit(solution)/shard_map/ppermute | solution.py:592
  296.7 5.9 %collective-permute-done.38 = bf16[256,1024]{1,0:T(8,128)(2,1)} collective-permute-done((bf16[256,1024]{1,0:T(8,128)(2,1)}, bf16[256,1024]{1,0:T(8,128)(2,1)}, u32[]{:S(2)}, u32[]{:S(2)}) %collective-permute-start.38) | collective-permute-done | bytes 524320 | tf_op jit(solution)/shard_map/ppermute | solution.py:592
  304.2 10.0 %collective-permute-done.67.refs_1_ = bf16[4,2,16,1536]{3,2,1,0:T(8,128)(2,1)S(1)} collective-permute-done((bf16[4,2,16,1536]{3,2,1,0:T(8,128)(2,1)S(1)}, bf16[4,2,16,1536]{3,2,1,0:T(8,128)(2,1)S(1)}, u32[]{:S(2)}, u32[]{:S(2)}) %collective-permute-start.67) | collective-permute-done | bytes 393248 | tf_op jit(solution)/shard_map/ppermute | solution.py:585
  322.2 4.1 %collective-permute-done.69.refs_3_ = bf16[4,2,16,1536]{3,2,1,0:T(8,128)(2,1)S(1)} collective-permute-done((bf16[4,2,16,1536]{3,2,1,0:T(8,128)(2,1)S(1)}, bf16[4,2,16,1536]{3,2,1,0:T(8,128)(2,1)S(1)}, u32[]{:S(2)}, u32[]{:S(2)}) %collective-permute-start.69) | collective-permute-done | bytes 393248 | tf_op jit(solution)/shard_map/ppermute | solution.py:585
  328.3 10.6 %collective-permute-done.79.refs_5_ = bf16[9,2,16,1024]{3,2,1,0:T(8,128)(2,1)S(1)} collective-permute-done((bf16[9,2,16,1024]{3,2,1,0:T(8,128)(2,1)S(1)}, bf16[9,2,16,1024]{3,2,1,0:T(8,128)(2,1)S(1)}, u32[]{:S(2)}, u32[]{:S(2)}) %collective-permute-start.79) | collective-permute-done | bytes 589856 | tf_op jit(solution)/shard_map/ppermute | solution.py:585
  341.1 6.2 %collective-permute-done.71.refs_5_ = bf16[4,2,16,1536]{3,2,1,0:T(8,128)(2,1)S(1)} collective-permute-done((bf16[4,2,16,1536]{3,2,1,0:T(8,128)(2,1)S(1)}, bf16[4,2,16,1536]{3,2,1,0:T(8,128)(2,1)S(1)}, u32[]{:S(2)}, u32[]{:S(2)}) %collective-permute-start.71) | collective-permute-done | bytes 393248 | tf_op jit(solution)/shard_map/ppermute | solution.py:585
  353.3 5.5 %shard_map.281 = (f32[256,3072]{1,0:T(8,128)}, f32[256,3072]{1,0:T(8,128)}, f32[768,1024]{1,0:T(8,128)}) custom-call(s32[4]{0:T(128)S(1)} %pad_add_fusion.scalars, bf16[9,2,16,1024]{3,2,1,0:T(8,128)(2,1)S(1)} %shard_map.274.refs_0_, bf16[9,2,16,1024]{3,2,1,0:T(8,128)(2,1)S(1)} %collective-permute-done.75.refs_1_, ...), custom_call_target="tpu_custom_call" | custom-call | bytes 14155776 | tf_op jit(solution)/shard_map/pallas_call | solution.py:443
  358.8 3.9 %shard_map.280 = (f32[256,2048]{1,0:T(8,128)}, f32[256,1024]{1,0:T(8,128)}, f32[256,1024]{1,0:T(8,128)}, f32[2048,256]{1,0:T(8,128)}) custom-call(s32[4]{0:T(128)S(1)} %pad_add_fusion.scalars, bf16[4,2,16,1536]{3,2,1,0:T(8,128)(2,1)S(1)} %shard_map.279.refs_0_, bf16[4,2,16,1536]{3,2,1,0:T(8,128)(2,1)S(1)} %collective-permute-done.67.refs_1_, ...), custom_call_target="tpu_custom_call" | custom-call | bytes 9437184 | tf_op jit(solution)/shard_map/pallas_call | solution.py:443
  (403 shorter events, 150.9 us)
Async XLA Ops:
  6.4 14.8 %collective-permute-start = (bf16[2,128,1024]{2,1,0:T(8,128)(2,1)S(1)}, bf16[2,128,1024]{2,1,0:T(8,128)(2,1)S(1)}, u32[]{:S(2)}, u32[]{:S(2)}) collective-permute-start(bf16[2,128,1024]{2,1,0:T(8,128)(2,1)S(1)} %get-tuple-element.89), channel_id=1, source_target_pairs={{0,16},{8,24},{16,0},{24,8},{1,17},{9,25},{17,1},{25,9},{2,18},{10... | collective-permute-start | bytes 1572872 | tf_op jit(solution)/shard_map/ppermute | solution.py:592
  9.4 36.4 %collective-permute-start.4 = (bf16[256,1024]{1,0:T(8,128)(2,1)}, bf16[256,1024]{1,0:T(8,128)(2,1)}, u32[]{:S(2)}, u32[]{:S(2)}) collective-permute-start(bf16[256,1024]{1,0:T(8,128)(2,1)} %get-tuple-element.92), channel_id=1, source_target_pairs={{0,8},{8,0},{16,24},{24,16},{1,9},{9,1},{17,25},{25,17},{2,10},{10... | collective-permute-start | bytes 1572872 | tf_op jit(solution)/shard_map/ppermute | solution.py:592
  27.1 16.3 %collective-permute-start.9 = (bf16[256,1024]{1,0:T(8,128)(2,1)S(1)}, bf16[256,1024]{1,0:T(8,128)(2,1)}, u32[]{:S(2)}, u32[]{:S(2)}) collective-permute-start(bf16[256,1024]{1,0:T(8,128)(2,1)S(1)} %bitcast.135), channel_id=1, source_target_pairs={{0,16},{8,24},{16,0},{24,8},{1,17},{9,25},{17,1},{25,9},{2,18},{10... | collective-permute-start | bytes 1572872 | tf_op jit(solution)/shard_map/ppermute | solution.py:592
  27.4 30.7 %collective-permute-start.8 = (bf16[256,1024]{1,0:T(8,128)(2,1)S(1)}, bf16[256,1024]{1,0:T(8,128)(2,1)}, u32[]{:S(2)}, u32[]{:S(2)}) collective-permute-start(bf16[256,1024]{1,0:T(8,128)(2,1)S(1)} %bitcast.136), channel_id=1, source_target_pairs={{0,8},{8,0},{16,24},{24,16},{1,9},{9,1},{17,25},{25,17},{2,10},{10... | collective-permute-start | bytes 1572872 | tf_op jit(solution)/shard_map/ppermute | solution.py:592
  28.7 24.2 %collective-permute-start.5 = (bf16[128,1024]{1,0:T(8,128)(2,1)}, bf16[128,1024]{1,0:T(8,128)(2,1)S(1)}, u32[]{:S(2)}, u32[]{:S(2)}) collective-permute-start(bf16[128,1024]{1,0:T(8,128)(2,1)} %slice_bitcast_fusion.1), channel_id=1, source_target_pairs={{0,8},{8,0},{16,24},{24,16},{1,9},{9,1},{17,25},{25,17},{2,10},{10... | collective-permute-start | bytes 786440 | tf_op jit(solution)/shard_map/ppermute | solution.py:592
  51.2 15.4 %collective-permute-start.15 = (bf16[2,256,256]{2,1,0:T(8,128)(2,1)S(1)}, bf16[2,256,256]{2,1,0:T(8,128)(2,1)S(1)}, u32[]{:S(2)}, u32[]{:S(2)}) collective-permute-start(bf16[2,256,256]{2,1,0:T(8,128)(2,1)S(1)} %collective-permute-done.11.refs_2_), channel_id=1, source_target_pairs={{0,1},{1,0},{2,3},{3,2},{4,5},{5,4},{6,7},{7,6},{8,9},{9,8},{10,11... | collective-permute-start | bytes 786440 | tf_op jit(solution)/shard_map/ppermute | solution.py:595
  52.9 21.3 %collective-permute-start.13 = (bf16[512,256]{1,0:T(8,128)(2,1)}, bf16[512,256]{1,0:T(8,128)(2,1)S(1)}, u32[]{:S(2)}, u32[]{:S(2)}) collective-permute-start(bf16[512,256]{1,0:T(8,128)(2,1)} %get-tuple-element.183), channel_id=1, source_target_pairs={{0,8},{8,0},{16,24},{24,16},{1,9},{9,1},{17,25},{25,17},{2,10},{10... | collective-permute-start | bytes 786440 | tf_op jit(solution)/shard_map/ppermute | solution.py:592
  53.0 21.2 %collective-permute-start.12 = (bf16[2,64,1536]{2,1,0:T(8,128)(2,1)}, bf16[2,64,1536]{2,1,0:T(8,128)(2,1)S(1)}, u32[]{:S(2)}, u32[]{:S(2)}) collective-permute-start(bf16[2,64,1536]{2,1,0:T(8,128)(2,1)} %copy-done.39), channel_id=1, source_target_pairs={{0,16},{8,24},{16,0},{24,8},{1,17},{9,25},{17,1},{25,9},{2,18},{10... | collective-permute-start | bytes 1179656 | tf_op jit(solution)/shard_map/ppermute | solution.py:592
  58.2 16.0 %collective-permute-start.14 = (bf16[256,256]{1,0:T(8,128)(2,1)S(1)}, bf16[256,256]{1,0:T(8,128)(2,1)S(1)}, u32[]{:S(2)}, u32[]{:S(2)}) collective-permute-start(bf16[256,256]{1,0:T(8,128)(2,1)S(1)} %slice_bitcast_fusion.3), channel_id=1, source_target_pairs={{0,8},{8,0},{16,24},{24,16},{1,9},{9,1},{17,25},{25,17},{2,10},{10... | collective-permute-start | bytes 393224 | tf_op jit(solution)/shard_map/ppermute | solution.py:592
  77.8 14.8 %collective-permute-start.19 = (bf16[256,1024]{1,0:T(8,128)(2,1)S(1)}, bf16[256,1024]{1,0:T(8,128)(2,1)S(1)}, u32[]{:S(2)}, u32[]{:S(2)}) collective-permute-start(bf16[256,1024]{1,0:T(8,128)(2,1)S(1)} %slice_add_fusion), channel_id=1, source_target_pairs={{0,16},{8,24},{16,0},{24,8},{1,17},{9,25},{17,1},{25,9},{2,18},{10... | collective-permute-start | bytes 1572872 | tf_op jit(solution)/shard_map/ppermute | solution.py:592
  78.4 29.6 %collective-permute-start.20 = (bf16[256,1536]{1,0:T(8,128)(2,1)S(1)}, bf16[256,1536]{1,0:T(8,128)(2,1)S(1)}, u32[]{:S(2)}, u32[]{:S(2)}) collective-permute-start(bf16[256,1536]{1,0:T(8,128)(2,1)S(1)} %copy-done.38), channel_id=1, source_target_pairs={{0,8},{8,0},{16,24},{24,16},{1,9},{9,1},{17,25},{25,17},{2,10},{10... | collective-permute-start | bytes 2359304 | tf_op jit(solution)/shard_map/ppermute | solution.py:592
  78.4 29.5 %collective-permute-start.28 = (bf16[256,1024]{1,0:T(8,128)(2,1)S(1)}, bf16[256,1024]{1,0:T(8,128)(2,1)S(1)}, u32[]{:S(2)}, u32[]{:S(2)}) collective-permute-start(bf16[256,1024]{1,0:T(8,128)(2,1)S(1)} %bitcast.147), channel_id=1, source_target_pairs={{0,16},{8,24},{16,0},{24,8},{1,17},{9,25},{17,1},{25,9},{2,18},{10... | collective-permute-start | bytes 1572872 | tf_op jit(solution)/shard_map/ppermute | solution.py:592
  88.4 18.8 %collective-permute-start.22 = (bf16[4,64,1536]{2,1,0:T(8,128)(2,1)S(1)}, bf16[4,64,1536]{2,1,0:T(8,128)(2,1)S(1)}, u32[]{:S(2)}, u32[]{:S(2)}) collective-permute-start(bf16[4,64,1536]{2,1,0:T(8,128)(2,1)S(1)} %constant_dynamic-update-slice_fusion.refs_2_), channel_id=1, source_target_pairs={{0,2},{1,3},{2,0},{3,1},{4,6},{5,7},{6,4},{7,5},{8,10},{9,11},{10,... | collective-permute-start | bytes 2359304 | tf_op jit(solution)/shard_map/ppermute | solution.py:595
  94.1 20.2 %collective-permute-start.25 = (bf16[256,1024]{1,0:T(8,128)(2,1)S(1)}, bf16[256,1024]{1,0:T(8,128)(2,1)S(1)}, u32[]{:S(2)}, u32[]{:S(2)}) collective-permute-start(bf16[256,1024]{1,0:T(8,128)(2,1)S(1)} %multiply_convert_fusion.refs_0_), channel_id=1, source_target_pairs={{0,16},{8,24},{16,0},{24,8},{1,17},{9,25},{17,1},{25,9},{2,18},{10... | collective-permute-start | bytes 1572872 | tf_op jit(solution)/shard_map/ppermute | solution.py:592
  157.8 20.3 %collective-permute-start.34 = (bf16[256,1024]{1,0:T(8,128)(2,1)}, bf16[256,1024]{1,0:T(8,128)(2,1)}, u32[]{:S(2)}, u32[]{:S(2)}) collective-permute-start(bf16[256,1024]{1,0:T(8,128)(2,1)} %get-tuple-element.171.refs_0_), channel_id=1, source_target_pairs={{0,16},{8,24},{16,0},{24,8},{1,17},{9,25},{17,1},{25,9},{2,18},{10... | collective-permute-start | bytes 1572872 | tf_op jit(solution)/shard_map/ppermute | solution.py:592
  178.1 18.7 %collective-permute-start.33 = (bf16[256,1024]{1,0:T(8,128)(2,1)}, bf16[256,1024]{1,0:T(8,128)(2,1)}, u32[]{:S(2)}, u32[]{:S(2)}) collective-permute-start(bf16[256,1024]{1,0:T(8,128)(2,1)} %get-tuple-element.171.refs_0_), channel_id=1, source_target_pairs={{0,8},{8,0},{16,24},{24,16},{1,9},{9,1},{17,25},{25,17},{2,10},{10... | collective-permute-start | bytes 1572872 | tf_op jit(solution)/shard_map/ppermute | solution.py:592
  178.1 18.7 %collective-permute-start.35 = (bf16[256,1024]{1,0:T(8,128)(2,1)}, bf16[256,1024]{1,0:T(8,128)(2,1)}, u32[]{:S(2)}, u32[]{:S(2)}) collective-permute-start(bf16[256,1024]{1,0:T(8,128)(2,1)} %collective-permute-done.34.refs_2_), channel_id=1, source_target_pairs={{0,8},{8,0},{16,24},{24,16},{1,9},{9,1},{17,25},{25,17},{2,10},{10... | collective-permute-start | bytes 1572872 | tf_op jit(solution)/shard_map/ppermute | solution.py:592
  194.8 18.8 %collective-permute-start.43 = (bf16[9,2,16,1024]{3,2,1,0:T(8,128)(2,1)S(1)}, bf16[9,2,16,1024]{3,2,1,0:T(8,128)(2,1)S(1)}, u32[]{:S(2)}, u32[]{:S(2)}) collective-permute-start(bf16[9,2,16,1024]{3,2,1,0:T(8,128)(2,1)S(1)} %get-tuple-element.122), channel_id=1, source_target_pairs={{0,2},{2,4},{4,6},{6,7},{7,5},{5,3},{3,1},{1,0},{8,10},{10,12},{12... | collective-permute-start | bytes 1769480 | tf_op jit(solution)/shard_map/ppermute | solution.py:585
  196.4 17.2 %collective-permute-start.44 = (bf16[9,2,16,1024]{3,2,1,0:T(8,128)(2,1)S(1)}, bf16[9,2,16,1024]{3,2,1,0:T(8,128)(2,1)S(1)}, u32[]{:S(2)}, u32[]{:S(2)}) collective-permute-start(bf16[9,2,16,1024]{3,2,1,0:T(8,128)(2,1)S(1)} %get-tuple-element.128), channel_id=1, source_target_pairs={{2,0},{4,2},{6,4},{7,6},{5,7},{3,5},{1,3},{0,1},{10,8},{12,10},{14... | collective-permute-start | bytes 1769480 | tf_op jit(solution)/shard_map/ppermute | solution.py:589
  214.5 16.3 %collective-permute-start.54 = (bf16[9,2,16,1024]{3,2,1,0:T(8,128)(2,1)S(1)}, bf16[9,2,16,1024]{3,2,1,0:T(8,128)(2,1)S(1)}, u32[]{:S(2)}, u32[]{:S(2)}) collective-permute-start(bf16[9,2,16,1024]{3,2,1,0:T(8,128)(2,1)S(1)} %get-tuple-element.129), channel_id=1, source_target_pairs={{0,2},{2,4},{4,6},{6,7},{7,5},{5,3},{3,1},{1,0},{8,10},{10,12},{12... | collective-permute-start | bytes 1769480 | tf_op jit(solution)/shard_map/ppermute | solution.py:585
  254.5 26.5 %collective-permute-start.37 = (bf16[256,1024]{1,0:T(8,128)(2,1)S(1)}, bf16[256,1024]{1,0:T(8,128)(2,1)S(1)}, u32[]{:S(2)}, u32[]{:S(2)}) collective-permute-start(bf16[256,1024]{1,0:T(8,128)(2,1)S(1)} %get-tuple-element.178), channel_id=1, source_target_pairs={{0,8},{8,0},{16,24},{24,16},{1,9},{9,1},{17,25},{25,17},{2,10},{10... | collective-permute-start | bytes 1572872 | tf_op jit(solution)/shard_map/ppermute | solution.py:592
  255.1 26.4 %collective-permute-start.36 = (bf16[256,1024]{1,0:T(8,128)(2,1)S(1)}, bf16[256,1024]{1,0:T(8,128)(2,1)S(1)}, u32[]{:S(2)}, u32[]{:S(2)}) collective-permute-start(bf16[256,1024]{1,0:T(8,128)(2,1)S(1)} %get-tuple-element.177), channel_id=1, source_target_pairs={{0,8},{8,0},{16,24},{24,16},{1,9},{9,1},{17,25},{25,17},{2,10},{10... | collective-permute-start | bytes 1572872 | tf_op jit(solution)/shard_map/ppermute | solution.py:592
  277.5 15.0 %collective-permute-start.76 = (bf16[9,2,16,1024]{3,2,1,0:T(8,128)(2,1)S(1)}, bf16[9,2,16,1024]{3,2,1,0:T(8,128)(2,1)}, u32[]{:S(2)}, u32[]{:S(2)}) collective-permute-start(bf16[9,2,16,1024]{3,2,1,0:T(8,128)(2,1)S(1)} %shard_map.274.refs_0_), channel_id=1, source_target_pairs={{2,0},{4,2},{6,4},{7,6},{5,7},{3,5},{1,3},{0,1},{10,8},{12,10},{14... | collective-permute-start | bytes 1769480 | tf_op jit(solution)/shard_map/ppermute | solution.py:589
  291.5 27.2 %collective-permute-start.77 = (bf16[9,2,16,1024]{3,2,1,0:T(8,128)(2,1)S(1)}, bf16[9,2,16,1024]{3,2,1,0:T(8,128)(2,1)S(1)}, u32[]{:S(2)}, u32[]{:S(2)}) collective-permute-start(bf16[9,2,16,1024]{3,2,1,0:T(8,128)(2,1)S(1)} %collective-permute-done.75.refs_1_), channel_id=1, source_target_pairs={{0,2},{2,4},{4,6},{6,7},{7,5},{5,3},{3,1},{1,0},{8,10},{10,12},{12... | collective-permute-start | bytes 1769480 | tf_op jit(solution)/shard_map/ppermute | solution.py:585
  292.5 27.0 %collective-permute-start.78 = (bf16[9,2,16,1024]{3,2,1,0:T(8,128)(2,1)}, bf16[9,2,16,1024]{3,2,1,0:T(8,128)(2,1)S(1)}, u32[]{:S(2)}, u32[]{:S(2)}) collective-permute-start(bf16[9,2,16,1024]{3,2,1,0:T(8,128)(2,1)} %collective-permute-done.76.refs_2_), channel_id=1, source_target_pairs={{2,0},{4,2},{6,4},{7,6},{5,7},{3,5},{1,3},{0,1},{10,8},{12,10},{14... | collective-permute-start | bytes 1769480 | tf_op jit(solution)/shard_map/ppermute | solution.py:589
  293.6 20.7 %collective-permute-start.67 = (bf16[4,2,16,1536]{3,2,1,0:T(8,128)(2,1)S(1)}, bf16[4,2,16,1536]{3,2,1,0:T(8,128)(2,1)S(1)}, u32[]{:S(2)}, u32[]{:S(2)}) collective-permute-start(bf16[4,2,16,1536]{3,2,1,0:T(8,128)(2,1)S(1)} %shard_map.279.refs_0_), channel_id=1, source_target_pairs={{0,2},{2,4},{4,6},{6,7},{7,5},{5,3},{3,1},{1,0},{8,10},{10,12},{12... | collective-permute-start | bytes 1179656 | tf_op jit(solution)/shard_map/ppermute | solution.py:585
  294.5 20.6 %collective-permute-start.68 = (bf16[4,2,16,1536]{3,2,1,0:T(8,128)(2,1)S(1)}, bf16[4,2,16,1536]{3,2,1,0:T(8,128)(2,1)S(1)}, u32[]{:S(2)}, u32[]{:S(2)}) collective-permute-start(bf16[4,2,16,1536]{3,2,1,0:T(8,128)(2,1)S(1)} %shard_map.279.refs_0_), channel_id=1, source_target_pairs={{2,0},{4,2},{6,4},{7,6},{5,7},{3,5},{1,3},{0,1},{10,8},{12,10},{14... | collective-permute-start | bytes 1179656 | tf_op jit(solution)/shard_map/ppermute | solution.py:589
  302.6 18.1 %collective-permute-start.47 = (bf16[256,1024]{1,0:T(8,128)(2,1)S(1)}, bf16[256,1024]{1,0:T(8,128)(2,1)S(1)}, u32[]{:S(2)}, u32[]{:S(2)}) collective-permute-start(bf16[256,1024]{1,0:T(8,128)(2,1)S(1)} %slice_add_fusion.1), channel_id=1, source_target_pairs={{0,16},{8,24},{16,0},{24,8},{1,17},{9,25},{17,1},{25,9},{2,18},{10... | collective-permute-start | bytes 1572872 | tf_op jit(solution)/shard_map/ppermute | solution.py:592
  318.6 20.3 %collective-permute-start.79 = (bf16[9,2,16,1024]{3,2,1,0:T(8,128)(2,1)S(1)}, bf16[9,2,16,1024]{3,2,1,0:T(8,128)(2,1)S(1)}, u32[]{:S(2)}, u32[]{:S(2)}) collective-permute-start(bf16[9,2,16,1024]{3,2,1,0:T(8,128)(2,1)S(1)} %collective-permute-done.77.refs_3_), channel_id=1, source_target_pairs={{0,2},{2,4},{4,6},{6,7},{7,5},{5,3},{3,1},{1,0},{8,10},{10,12},{12... | collective-permute-start | bytes 1769480 | tf_op jit(solution)/shard_map/ppermute | solution.py:585
  319.5 20.4 %collective-permute-start.80 = (bf16[9,2,16,1024]{3,2,1,0:T(8,128)(2,1)S(1)}, bf16[9,2,16,1024]{3,2,1,0:T(8,128)(2,1)S(1)}, u32[]{:S(2)}, u32[]{:S(2)}) collective-permute-start(bf16[9,2,16,1024]{3,2,1,0:T(8,128)(2,1)S(1)} %collective-permute-done.78.refs_4_), channel_id=1, source_target_pairs={{2,0},{4,2},{6,4},{7,6},{5,7},{3,5},{1,3},{0,1},{10,8},{12,10},{14... | collective-permute-start | bytes 1769480 | tf_op jit(solution)/shard_map/ppermute | solution.py:589
  326.3 21.1 %collective-permute-start.71 = (bf16[4,2,16,1536]{3,2,1,0:T(8,128)(2,1)S(1)}, bf16[4,2,16,1536]{3,2,1,0:T(8,128)(2,1)S(1)}, u32[]{:S(2)}, u32[]{:S(2)}) collective-permute-start(bf16[4,2,16,1536]{3,2,1,0:T(8,128)(2,1)S(1)} %collective-permute-done.69.refs_3_), channel_id=1, source_target_pairs={{0,2},{2,4},{4,6},{6,7},{7,5},{5,3},{3,1},{1,0},{8,10},{10,12},{12... | collective-permute-start | bytes 1179656 | tf_op jit(solution)/shard_map/ppermute | solution.py:585
  327.1 21.1 %collective-permute-start.72 = (bf16[4,2,16,1536]{3,2,1,0:T(8,128)(2,1)S(1)}, bf16[4,2,16,1536]{3,2,1,0:T(8,128)(2,1)S(1)}, u32[]{:S(2)}, u32[]{:S(2)}) collective-permute-start(bf16[4,2,16,1536]{3,2,1,0:T(8,128)(2,1)S(1)} %collective-permute-done.70.refs_4_), channel_id=1, source_target_pairs={{2,0},{4,2},{6,4},{7,6},{5,7},{3,5},{1,3},{0,1},{10,8},{12,10},{14... | collective-permute-start | bytes 1179656 | tf_op jit(solution)/shard_map/ppermute | solution.py:589
  (128 other events, 1052.1 us)

commit v4 on v3

--- a/solution.py
+++ b/solution.py
@@ -13,7 +13,7 @@
 f32 = jnp.float32
 bf16 = jnp.bfloat16
 vmem_bytes = 32 * 1024 * 1024
-vmem_wide = 52 * 1024 * 1024
+vmem_wide = 42 * 1024 * 1024
 
 
 def dot(left, right):
@@ -270,7 +270,7 @@
 
 def feed_kernel(count, kept, weight, down, *refs):
     norm, cot = refs[:count], refs[count : 2 * count]
-    hidden, gate_out, up_out, norm_all, cot_all, norm_grad, out, low_held, cot_held = refs[
+    hidden, gate_out, up_out, norm_all, cot_all, out, *norm_grad, low_held, cot_held = refs[
         2 * count + kept :
     ]
     pick(norm, low_held)
@@ -290,9 +290,15 @@
     up_grad = (back * silu).astype(bf16)
     gate_out[...] = gate_grad
     up_out[...] = up_grad
-    norm_grad[...] = (
+    back_low = (
         dot_nt(gate_grad, weight[:, :units]) + dot_nt(up_grad, weight[:, units:])
     ).astype(bf16)
+    for k, ref in enumerate(norm_grad):
+
+        @pl.when(pl.program_id(0) == k)
+        def _(ref=ref):
+            ref[...] = back_low
+
     out[...] = dot(hid, down[...]).astype(bf16)
 
 
@@ -308,9 +314,11 @@
         in_specs=[fixed_block(*weight.shape), fixed_block(*down.shape)]
         + [fixed_block(block, width)] * (2 * count)
         + [pl.BlockSpec(memory_space=pl.ANY)] * len(before),
-        out_specs=[row_block(block, n, first) for n in kept] + [row_block(block, width)] * 2,
+        out_specs=[row_block(block, n, first) for n in kept] + [row_block(block, width)]
+        + [fixed_block(block, width)] * count,
         out_shape=[jax.ShapeDtypeStruct((total, n), bf16) for n in kept]
-        + [jax.ShapeDtypeStruct((block * count, width), bf16)] * 2,
+        + [jax.ShapeDtypeStruct((block * count, width), bf16)]
+        + [jax.ShapeDtypeStruct((block, width), bf16)] * count,
         scratch_shapes=[pltpu.VMEM((block, width), bf16)] * 2,
         input_output_aliases={2 + 2 * count + i: i for i in range(len(before))},
         compiler_params=params(vmem_wide),
@@ -616,11 +624,12 @@
     def ring_scatter(self, shares, layout, blocks):
         return RingSum(self, shares, layout, blocks)
 
-    def ring_gather(self, item):
+    def ring_gather(self, item, *before):
         u1, d1 = self.up(item), self.down(item)
         u2, d2 = self.up(u1), self.down(d1)
         u3, d3 = self.up(u2), self.down(d2)
-        u4, d4 = self.up(u3[:, :1]), self.down(d3[:, 1:])
+        last = after(u3, *before) if before else u3
+        u4, d4 = self.up(last[:, :1]), self.down(d3[:, 1:])
         return [
             (item, 0, None), (u1, -1, None), (d1, 1, None), (u2, -2, None), (d2, 2, None),
             (u3, -3, None), (d3, 3, None), (u4, 4, 0), (d4, 4, 1),
@@ -748,7 +757,7 @@
             (width, q_width + 2 * k_width),
         )
         qkv.start()
-        attention_gain = after(attention_gain, qkv.here)
+        attention_gain = after(attention_gain, qkv.piece)
     small = jnp.concatenate(
         [attention_gain, mlp_gain, query_gain, key_gain, segments[0].astype(bf16)]
     )[None]
@@ -817,39 +826,35 @@
     normed_one, lin, rot, val = project(
         all_tokens, input_gain, qkv_weight, cosine, sine, head_gains, q_heads, k_heads
     )
+    if direct:
+        rot = after(rot, both.here)
     attended, attended_low, logs = attend(order, rot, val, seg_col, seg_row, q_heads, k_heads, head, shards)
     inputs = own_tokens.astype(f32)
     split = total // 2
     if direct:
         feed_weight = both.finish()
-        attended_low = after(attended_low, both.here)
+        attended_low = after(attended_low, all_cot[2])
     far_part = dot(attended_low[split:], out_weight).astype(bf16)
     near_part = dot(attended_low[:split], out_weight).astype(bf16)
     residual_one = inputs + moves.scatter(near_part, far_part)
     residual_scale = inverse_root(residual_one)
     normed_two = moves.gather((residual_one * residual_scale * second_gain).astype(bf16))
 
-    *kept, norm_grad, out_part = feed(
+    hidden, gate_grad, up_grad, normed_two, all_cot, out_part, *norm_grad = feed(
         normed_two, all_cot, feed_weight, down_weight, 0, shards, []
     )
-    hidden, gate_grad, up_grad, normed_two, all_cot = kept
-    if direct:
-        crossed = norm_grad[2 * rows : 3 * rows] + moves.swap(norm_grad[3 * rows :], 1)
+    if direct:
+        crossed = norm_grad[2] + moves.swap(norm_grad[3], 1)
         hidden, gate_grad = after(hidden, crossed), after(gate_grad, crossed)
         up_grad = after(up_grad, crossed)
-        near_grad = norm_grad[:rows].astype(f32) + moves.swap(norm_grad[rows : 2 * rows], 1).astype(f32)
-        normed_grad_two = near_grad + moves.swap(crossed, 2).astype(f32)
+        near_grad = norm_grad[0].astype(f32) + moves.swap(norm_grad[1], 1).astype(f32)
+        far_grad = moves.swap(crossed, 2)
     else:
+        norm_grad = jnp.concatenate(norm_grad, axis=0)
         normed_grad_two = moves.scatter(norm_grad[:split], norm_grad[split:])
     share_down = dot_tn(hidden, all_cot).astype(bf16)
     share_gate = dot_tn(normed_two, gate_grad).astype(bf16)
     share_up = dot_tn(normed_two, up_grad).astype(bf16)
-    mlp_gain_part = jnp.sum(normed_grad_two * residual_one * residual_scale, axis=0)
-    residual_grad = cot.astype(f32) + norm_back(
-        normed_grad_two * second_gain, residual_one, residual_scale
-    )
-    branch_low = residual_grad.astype(bf16)
-    branch_grad = moves.gather(branch_low)
     if direct:
         lines = slice_width // 16
         rest = 2 * units - width
@@ -869,16 +874,27 @@
         ring = moves.ring_scatter(
             [as_chunks(share_gate), as_chunks(share_up), as_chunks(share_down)], layout, blocks
         )
+        normed_grad_two = near_grad + after(far_grad, ring.sent).astype(f32)
+    mlp_gain_part = jnp.sum(normed_grad_two * residual_one * residual_scale, axis=0)
+    residual_grad = cot.astype(f32) + norm_back(
+        normed_grad_two * second_gain, residual_one, residual_scale
+    )
+    branch_low = residual_grad.astype(bf16)
+    if direct:
         ring.advance(branch_low)
-
+        far_branch = after(moves.swap(branch_low, 2), ring.sent)
+        branch_grad = [
+            branch_low, moves.swap(branch_low, 1), far_branch, moves.swap(far_branch, 1),
+        ]
+    else:
+        branch_grad = moves.gather(branch_low)
     out_part = after(out_part, *branch_grad)
     layer_out = (residual_one + moves.scatter(out_part[:split], out_part[split:])).astype(bf16)
 
-    far_branch = branch_grad[2]
     out_grad, branch_grad = branch_back(branch_grad, out_weight)
     share_out = dot_tn(attended_low, branch_grad).astype(bf16)
     if direct:
-        ring.advance(far_branch)
+        ring.advance(out_grad)
         out_grad = after(out_grad, ring.sent)
     query_grad, key_grad, val_grad = attend_back(
         order, rot, val, out_grad, attended, logs, seg_col, seg_row, q_heads, k_heads, head, shards
@@ -958,7 +974,7 @@
             moves.scalars, [part for part, _, _ in parts], shapes, todo
         )
 
-        first_near, first_packed = near, parts[0][0]
+        first_near, first_packed, first_last = near, parts[0][0], parts[-1][0]
 
         outs = q_width // slice_width
         pair = 2 * k_width
@@ -986,7 +1002,7 @@
             (source, index, 0, wide_all, i, 0)
             for i, (source, index) in enumerate([(0, 0), (1, 0), (2, 0), (2, 1)])
         ]
-        parts = moves.ring_gather(pack([own, near, far], layout, (4, 2, lines, wide_all)))
+        parts = moves.ring_gather(pack([own, near, far], layout, (4, 2, lines, wide_all)), first_last)
         todo = []
         for source, (part, offset, half) in enumerate(parts):
             for h in range(part.shape[1]):

time: 368 us -> 351 us (0.954)
  waiting for transfers between devices: 154 us -> 143 us
  local copies, waits for them, and re-layouts: 35.5 us -> 31.2 us
    ppermute x16, waiting for transfers between devices: 8.77 us -> 32.5 us  [down(): lax.ppermute(item, 'rep', [(ring[(i + 1) % 8], ring[i]) for i in range(8)])]
    ppermute x44, waiting for transfers between devices: 51.4 us -> 29.9 us  [swap(): return lax.ppermute(item, 'shard', [(i, i ^ mask) for i in range(4)])]
    ppermute x16, waiting for transfers between devices: 61.4 us -> 44.8 us  [up(): lax.ppermute(item, 'rep', [(ring[i], ring[(i + 1) % 8]) for i in range(8)])]
    ppermute x16, starting transfers between devices: 15.7 us -> 11.8 us  [down(): lax.ppermute(item, 'rep', [(ring[(i + 1) % 8], ring[i]) for i in range(8)])]
    unnamed x159 -> x151, local copies, waits for them, and re-layouts: 25.1 us -> 22 us
  transfers between devices with their start and end apart: 83 -> 83, of which waited for: 33 -> 38; matrix products, arithmetic and copies ran while one was open for 10% -> 11% of each run, Pallas kernels for 15% -> 14%
where the time goes in v4:
time: 351 us; the launch traced here: 345 us
  waiting for transfers between devices  143 us (41%)
  Pallas kernels  77.6 us (22%)
  starting transfers between devices  62.6 us (18%)
  local copies, waits for them, and re-layouts  31.2 us (9%)
  other arithmetic  16.5 us (5%)
  matrix products  12.6 us (4%)
    ppermute x16, waiting for transfers between devices, up(): lax.ppermute(item, 'rep', [(ring[i], ring[(i + 1) % 8]) for i in range(8)])  44.8 us
    ppermute x7, waiting for transfers between devices, cross_rep(): return lax.ppermute(item, 'rep', [(i, i ^ mask) for i in range(8)])  35.6 us
    ppermute x16, waiting for transfers between devices, down(): lax.ppermute(item, 'rep', [(ring[(i + 1) % 8], ring[i]) for i in range(8)])  32.5 us
    ppermute x44, waiting for transfers between devices, swap(): return lax.ppermute(item, 'shard', [(i, i ^ mask) for i in range(4)])  29.9 us
    ppermute x44, starting transfers between devices, swap(): return lax.ppermute(item, 'shard', [(i, i ^ mask) for i in range(4)])  23.5 us
    unnamed x151, local copies, waits for them, and re-layouts  22 us
    pallas_call x1, Pallas kernels, feed(): pl.pallas_call(functools.partial(feed_kernel, count, len(before)), grid=(...  18.2 us
    ppermute x16, starting transfers between devices, up(): lax.ppermute(item, 'rep', [(ring[i], ring[(i + 1) % 8]) for i in range(8)])  17.7 us
  transfers between devices with their start and end apart: 83, of which 38 were waited for; matrix products, arithmetic and copies ran while one was open for 11% of the time, Pallas kernels for 14%

profile of v4, /device:TPU:0, one launch (start us, length us, event | category | flops | bytes accessed | tf_op | source)
XLA Modules:
  0.0 345.3 jit_solution(18100238635073036665)
XLA Ops:
  6.6 3.0 collective-permute-start.1
  28.7 8.9 %collective-permute-done.6.refs_4_ = bf16[2,128,1024]{2,1,0:T(8,128)(2,1)S(1)} collective-permute-done((bf16[2,128,1024]{2,1,0:T(8,128)(2,1)S(1)}, bf16[2,128,1024]{2,1,0:T(8,128)(2,1)S(1)}, u32[]{:S(2)}, u32[]{:S(2)}) %collective-permute-start.6) | collective-permute-done | bytes 524320 | tf_op jit(solution)/shard_map/ppermute | solution.py:603
  40.1 4.4 %collective-permute-done.11.refs_2_ = bf16[2,256,256]{2,1,0:T(8,128)(2,1)S(1)} collective-permute-done((bf16[2,256,256]{2,1,0:T(8,128)(2,1)S(1)}, bf16[2,256,256]{2,1,0:T(8,128)(2,1)S(1)}, u32[]{:S(2)}, u32[]{:S(2)}) %collective-permute-start.11) | collective-permute-done | bytes 262176 | tf_op jit(solution)/shard_map/ppermute | solution.py:600
  56.8 6.5 %shard_map.257 = (bf16[1024,1024]{1,0:T(8,128)(2,1)S(1)}, f32[1024,768]{1,0:T(8,128)}, bf16[1024,768]{1,0:T(8,128)(2,1)S(1)}, bf16[1024,256]{1,0:T(8,128)(2,1)S(1)}) custom-call(f32[1,1024]{1,0:T(1,128)S(1)} %bitcast.146, bf16[1024,1024]{1,0:T(8,128)(2,1)S(1)} %shard_map.256.weight, f32[1024,128]{1,0:T(8,128)S(1)} %get-tuple-element.217.cosine, ...), custom_call_target="tpu_custom_call" | custom-call | flops 2147483648 | bytes 14680064 | tf_op jit(solution)/shard_map/pallas_call | solution.py:98
  64.8 4.4 %shard_map.259 = (f32[1024,512]{1,0:T(8,128)S(1)}, bf16[1024,512]{1,0:T(8,128)(2,1)S(1)}, f32[1024,512]{1,0:T(8,128)S(1)}) custom-call(s32[1]{0:T(128)} %bitcast.1.order, bf16[1024,768]{1,0:T(8,128)(2,1)S(1)} %get-tuple-element.105.query.key, bf16[1024,768]{1,0:T(8,128)(2,1)S(1)} %get-tuple-element.105.query.key, ...), custom_call_target="tpu_custom_call" | custom-call | flops 2147483648 | bytes 6291456 | tf_op jit(solution)/shard_map/pallas_call | solution.py:171
  76.8 5.1 %collective-permute-done.22 = bf16[2,64,1536]{2,1,0:T(8,128)(2,1)S(1)} collective-permute-done((bf16[2,64,1536]{2,1,0:T(8,128)(2,1)}, bf16[2,64,1536]{2,1,0:T(8,128)(2,1)S(1)}, u32[]{:S(2)}, u32[]{:S(2)}) %collective-permute-start.22) | collective-permute-done | bytes 393248 | tf_op jit(solution)/shard_map/ppermute | solution.py:603
  83.6 3.9 %collective-permute-done.20 = bf16[256,1024]{1,0:T(8,128)(2,1)S(1)} collective-permute-done((bf16[256,1024]{1,0:T(8,128)(2,1)S(1)}, bf16[256,1024]{1,0:T(8,128)(2,1)S(1)}, u32[]{:S(2)}, u32[]{:S(2)}) %collective-permute-start.20) | collective-permute-done | bytes 524320 | tf_op jit(solution)/shard_map/ppermute | solution.py:600
  89.6 11.1 %collective-permute-done.23.refs_3_ = bf16[4,64,1536]{2,1,0:T(8,128)(2,1)S(1)} collective-permute-done((bf16[4,64,1536]{2,1,0:T(8,128)(2,1)S(1)}, bf16[4,64,1536]{2,1,0:T(8,128)(2,1)S(1)}, u32[]{:S(2)}, u32[]{:S(2)}) %collective-permute-start.23) | collective-permute-done | bytes 786464 | tf_op jit(solution)/shard_map/ppermute | solution.py:603
  106.1 18.2 %shard_map.262 = (bf16[1024,768]{1,0:T(8,128)(2,1)S(1)}, bf16[1024,768]{1,0:T(8,128)(2,1)S(1)}, bf16[1024,768]{1,0:T(8,128)(2,1)S(1)}, bf16[1024,1024]{1,0:T(8,1...) custom-call(bf16[1024,1536]{1,0:T(8,128)(2,1)} %copy-done.10, ...), custom_call_target="tpu_custom_call" | custom-call | flops 9663676416 | bytes 21495808 | tf_op jit(solution)/shard_map/pallas_call | solution.py:311
  131.2 3.6 %convolution_convert_fusion.1 = bf16[1024,768]{1,0:T(8,128)(2,1)S(1)} fusion(bf16[1024,1024]{1,0:T(8,128)(2,1)} %get-tuple-element.117, bf16[1024,768]{1,0:T(8,128)(2,1)S(1)} %get-tuple-element.121), kind=kOutput, calls=%fused_computation.7 | convolution fusion | flops 1611399168 | bytes 5242880 | tf_op jit(solution)/shard_map/dot_general | solution.py:28
  140.1 3.6 %collective-permute-done.32 = bf16[256,1024]{1,0:T(8,128)(2,1)S(1)} collective-permute-done((bf16[256,1024]{1,0:T(8,128)(2,1)S(1)}, bf16[256,1024]{1,0:T(8,128)(2,1)S(1)}, u32[]{:S(2)}, u32[]{:S(2)}) %collective-permute-start.32) | collective-permute-done | bytes 524320 | tf_op jit(solution)/shard_map/ppermute | solution.py:600
  149.5 6.0 %collective-permute-done.35.refs_6_ = bf16[9,1,16,1024]{3,2,1,0:T(8,128)(2,1)S(1)} collective-permute-done((bf16[9,1,16,1024]{3,2,1,0:T(8,128)(2,1)}, bf16[9,1,16,1024]{3,2,1,0:T(8,128)(2,1)S(1)}, u32[]{:S(2)}, u32[]{:S(2)}) %collective-permute-start.35) | collective-permute-done | bytes 294944 | tf_op jit(solution)/shard_map/ppermute | solution.py:593
  158.4 2.6 shard_map.264
  164.6 3.7 %shard_map.265 = (bf16[1024,512]{1,0:T(8,128)(2,1)S(1)}, bf16[1024,1024]{1,0:T(8,128)(2,1)S(1)}) custom-call(bf16[512,1024]{1,0:T(8,128)(2,1)S(1)} %copy-done.22, bf16[256,1024]{1,0:T(8,128)(2,1)} %get-tuple-element.185.refs_0_, bf16[256,1024]{1,0:T(8,128)(2,1)} %collective-permute-done.33.refs_1_, bf16[256,1024]{1,0:T(8,128)(2,1)} %collective-permute-done.34.refs_2_, ...), custom_call_target="tpu_custom_call" | custom-call | flops 1073741824 | bytes 7340032 | tf_op jit(solution)/shard_map/pallas_call | solution.py:344
  168.3 8.8 %collective-permute-done.41.refs_6_ = bf16[9,2,16,1024]{3,2,1,0:T(8,128)(2,1)} collective-permute-done((bf16[9,2,16,1024]{3,2,1,0:T(8,128)(2,1)}, bf16[9,2,16,1024]{3,2,1,0:T(8,128)(2,1)}, u32[]{:S(2)}, u32[]{:S(2)}) %collective-permute-start.41) | collective-permute-done | bytes 589856 | tf_op jit(solution)/shard_map/ppermute | solution.py:593
  185.0 10.5 %shard_map.267 = (f32[1024,512]{1,0:T(8,128)S(1)}, f32[1024,256]{1,0:T(8,128)S(1)}, f32[1024,256]{1,0:T(8,128)S(1)}) custom-call(s32[1]{0:T(128)} %bitcast.1.order, bf16[1024,768]{1,0:T(8,128)(2,1)S(1)} %copy-done.45, bf16[1024,768]{1,0:T(8,128)(2,1)S(1)} %copy-done.45, bf16[1024,256]{1,0:T(8,128)(2,1)S(1)} %copy-done.51, ...), custom_call_target="tpu_custom_call" | custom-call | flops 5368709120 | bytes 10485760 | tf_op jit(solution)/shard_map/pallas_call | solution.py:244
  199.6 9.5 %shard_map.269 = (bf16[1024,512]{1,0:T(8,128)(2,1)S(1)}, bf16[1024,512]{1,0:T(8,128)(2,1)S(1)}, bf16[1024,1024]{1,0:T(8,128)(2,1)S(1)}, f32[1,1024]{1,0:T(1,128)S(1)}, f32[2,128]{1,0:T(2,128)S(1)}) custom-call(f32[1024,512]{1,0:T(8,128)S(1)} %get-tuple-element.143.query_grad, f32[1024,256]{1,0:T(8,128)S(1)} %get-tuple-element.144.key_grad, ...), custom_call_target="tpu_custom_call" | custom-call | flops 2147483648 | bytes 18874368 | tf_op jit(solution)/shard_map/pallas_call | solution.py:403
  214.7 2.7 collective-permute-done.53.refs_6_
  217.4 4.0 %collective-permute-done.57.refs_7_ = bf16[6,1,16,1024]{3,2,1,0:T(8,128)(2,1)S(1)} collective-permute-done((bf16[6,1,16,1024]{3,2,1,0:T(8,128)(2,1)S(1)}, bf16[6,1,16,1024]{3,2,1,0:T(8,128)(2,1)S(1)}, u32[]{:S(2)}, u32[]{:S(2)}) %collective-permute-start.57) | collective-permute-done | bytes 196640 | tf_op jit(solution)/shard_map/ppermute | solution.py:597
  224.8 5.4 %collective-permute-done.59.refs_2_ = bf16[2,2,16,1536]{3,2,1,0:T(8,128)(2,1)S(1)} collective-permute-done((bf16[2,2,16,1536]{3,2,1,0:T(8,128)(2,1)S(1)}, bf16[2,2,16,1536]{3,2,1,0:T(8,128)(2,1)S(1)}, u32[]{:S(2)}, u32[]{:S(2)}) %collective-permute-start.59) | collective-permute-done | bytes 196640 | tf_op jit(solution)/shard_map/ppermute | solution.py:600
  236.8 6.7 %collective-permute-done.61.refs_6_ = bf16[6,2,16,1024]{3,2,1,0:T(8,128)(2,1)S(1)} collective-permute-done((bf16[6,2,16,1024]{3,2,1,0:T(8,128)(2,1)S(1)}, bf16[6,2,16,1024]{3,2,1,0:T(8,128)(2,1)S(1)}, u32[]{:S(2)}, u32[]{:S(2)}) %collective-permute-start.61) | collective-permute-done | bytes 393248 | tf_op jit(solution)/shard_map/ppermute | solution.py:593
  247.6 2.8 collective-permute-done.49
  260.8 7.4 %collective-permute-done.52 = f32[1,2304]{1,0:T(1,128)S(1)} collective-permute-done((f32[1,2304]{1,0:T(1,128)S(1)}, f32[1,2304]{1,0:T(1,128)S(1)}, u32[]{:S(2)}, u32[]{:S(2)}) %collective-permute-start.52) | collective-permute-done | bytes 9248 | tf_op jit(solution)/shard_map/ppermute | solution.py:603
  269.4 4.5 %collective-permute-done.66.refs_2_ = bf16[2,2,16,1536]{3,2,1,0:T(8,128)(2,1)S(1)} collective-permute-done((bf16[2,2,16,1536]{3,2,1,0:T(8,128)(2,1)S(1)}, bf16[2,2,16,1536]{3,2,1,0:T(8,128)(2,1)S(1)}, u32[]{:S(2)}, u32[]{:S(2)}) %collective-permute-start.66) | collective-permute-done | bytes 196640 | tf_op jit(solution)/shard_map/ppermute | solution.py:600
  281.1 9.0 %collective-permute-done.74.refs_4_ = bf16[9,2,16,1024]{3,2,1,0:T(8,128)(2,1)S(1)} collective-permute-done((bf16[9,2,16,1024]{3,2,1,0:T(8,128)(2,1)S(1)}, bf16[9,2,16,1024]{3,2,1,0:T(8,128)(2,1)S(1)}, u32[]{:S(2)}, u32[]{:S(2)}) %collective-permute-start.74) | collective-permute-done | bytes 589856 | tf_op jit(solution)/shard_map/ppermute | solution.py:597
  290.7 7.1 %collective-permute-done.67.refs_1_ = bf16[4,2,16,1536]{3,2,1,0:T(8,128)(2,1)S(1)} collective-permute-done((bf16[4,2,16,1536]{3,2,1,0:T(8,128)(2,1)S(1)}, bf16[4,2,16,1536]{3,2,1,0:T(8,128)(2,1)S(1)}, u32[]{:S(2)}, u32[]{:S(2)}) %collective-permute-start.67) | collective-permute-done | bytes 393248 | tf_op jit(solution)/shard_map/ppermute | solution.py:593
  304.7 6.6 %collective-permute-done.75.refs_6_ = bf16[9,2,16,1024]{3,2,1,0:T(8,128)(2,1)S(1)} collective-permute-done((bf16[9,2,16,1024]{3,2,1,0:T(8,128)(2,1)S(1)}, bf16[9,2,16,1024]{3,2,1,0:T(8,128)(2,1)S(1)}, u32[]{:S(2)}, u32[]{:S(2)}) %collective-permute-start.75) | collective-permute-done | bytes 589856 | tf_op jit(solution)/shard_map/ppermute | solution.py:597
  313.3 6.3 %collective-permute-done.70.refs_4_ = bf16[4,2,16,1536]{3,2,1,0:T(8,128)(2,1)S(1)} collective-permute-done((bf16[4,2,16,1536]{3,2,1,0:T(8,128)(2,1)S(1)}, bf16[4,2,16,1536]{3,2,1,0:T(8,128)(2,1)S(1)}, u32[]{:S(2)}, u32[]{:S(2)}) %collective-permute-start.70) | collective-permute-done | bytes 393248 | tf_op jit(solution)/shard_map/ppermute | solution.py:597
  319.7 2.9 collective-permute-done.81.refs_5_
  325.1 5.8 %collective-permute-done.71.refs_5_ = bf16[4,2,16,1536]{3,2,1,0:T(8,128)(2,1)S(1)} collective-permute-done((bf16[4,2,16,1536]{3,2,1,0:T(8,128)(2,1)S(1)}, bf16[4,2,16,1536]{3,2,1,0:T(8,128)(2,1)S(1)}, u32[]{:S(2)}, u32[]{:S(2)}) %collective-permute-start.71) | collective-permute-done | bytes 393248 | tf_op jit(solution)/shard_map/ppermute | solution.py:593
  336.3 4.9 %shard_map.281 = (f32[256,3072]{1,0:T(8,128)}, f32[256,3072]{1,0:T(8,128)}, f32[768,1024]{1,0:T(8,128)}) custom-call(s32[4]{0:T(128)S(1)} %pad_add_fusion.scalars, bf16[9,2,16,1024]{3,2,1,0:T(8,128)(2,1)S(1)} %shard_map.274.refs_0_, bf16[9,2,16,1024]{3,2,1,0:T(8,128)(2,1)S(1)} %collective-permute-done.79.refs_1_, ...), custom_call_target="tpu_custom_call" | custom-call | bytes 14155776 | tf_op jit(solution)/shard_map/pallas_call | solution.py:451
  341.3 3.9 %shard_map.280 = (f32[256,2048]{1,0:T(8,128)}, f32[256,1024]{1,0:T(8,128)}, f32[256,1024]{1,0:T(8,128)}, f32[2048,256]{1,0:T(8,128)}) custom-call(s32[4]{0:T(128)S(1)} %pad_add_fusion.scalars, bf16[4,2,16,1536]{3,2,1,0:T(8,128)(2,1)S(1)} %shard_map.279.refs_0_, bf16[4,2,16,1536]{3,2,1,0:T(8,128)(2,1)S(1)} %collective-permute-done.67.refs_1_, ...), custom_call_target="tpu_custom_call" | custom-call | bytes 9437184 | tf_op jit(solution)/shard_map/pallas_call | solution.py:451
  (394 shorter events, 149.3 us)
Async XLA Ops:
  9.6 14.3 %collective-permute-start.4 = (bf16[2,128,1024]{2,1,0:T(8,128)(2,1)S(1)}, bf16[2,128,1024]{2,1,0:T(8,128)(2,1)S(1)}, u32[]{:S(2)}, u32[]{:S(2)}) collective-permute-start(bf16[2,128,1024]{2,1,0:T(8,128)(2,1)S(1)} %get-tuple-element.96), channel_id=1, source_target_pairs={{0,16},{8,24},{16,0},{24,8},{1,17},{9,25},{17,1},{25,9},{2,18},{10... | collective-permute-start | bytes 1572872 | tf_op jit(solution)/shard_map/ppermute | solution.py:600
  9.8 36.8 %collective-permute-start.3 = (bf16[256,1024]{1,0:T(8,128)(2,1)}, bf16[256,1024]{1,0:T(8,128)(2,1)}, u32[]{:S(2)}, u32[]{:S(2)}) collective-permute-start(bf16[256,1024]{1,0:T(8,128)(2,1)} %get-tuple-element.99), channel_id=1, source_target_pairs={{0,8},{8,0},{16,24},{24,16},{1,9},{9,1},{17,25},{25,17},{2,10},{10... | collective-permute-start | bytes 1572872 | tf_op jit(solution)/shard_map/ppermute | solution.py:600
  28.7 18.4 %collective-permute-start.5 = (bf16[128,1024]{1,0:T(8,128)(2,1)}, bf16[128,1024]{1,0:T(8,128)(2,1)S(1)}, u32[]{:S(2)}, u32[]{:S(2)}) collective-permute-start(bf16[128,1024]{1,0:T(8,128)(2,1)} %slice_bitcast_fusion.1), channel_id=1, source_target_pairs={{0,8},{8,0},{16,24},{24,16},{1,9},{9,1},{17,25},{25,17},{2,10},{10... | collective-permute-start | bytes 786440 | tf_op jit(solution)/shard_map/ppermute | solution.py:600
  73.0 14.4 %collective-permute-start.20 = (bf16[256,1024]{1,0:T(8,128)(2,1)S(1)}, bf16[256,1024]{1,0:T(8,128)(2,1)S(1)}, u32[]{:S(2)}, u32[]{:S(2)}) collective-permute-start(bf16[256,1024]{1,0:T(8,128)(2,1)S(1)} %slice_add_fusion), channel_id=1, source_target_pairs={{0,16},{8,24},{16,0},{24,8},{1,17},{9,25},{17,1},{25,9},{2,18},{10... | collective-permute-start | bytes 1572872 | tf_op jit(solution)/shard_map/ppermute | solution.py:600
  74.6 26.9 %collective-permute-start.21 = (bf16[256,1536]{1,0:T(8,128)(2,1)S(1)}, bf16[256,1536]{1,0:T(8,128)(2,1)S(1)}, u32[]{:S(2)}, u32[]{:S(2)}) collective-permute-start(bf16[256,1536]{1,0:T(8,128)(2,1)S(1)} %copy-done.41), channel_id=1, source_target_pairs={{0,8},{8,0},{16,24},{24,16},{1,9},{9,1},{17,25},{25,17},{2,10},{10... | collective-permute-start | bytes 2359304 | tf_op jit(solution)/shard_map/ppermute | solution.py:600
  81.9 18.7 %collective-permute-start.23 = (bf16[4,64,1536]{2,1,0:T(8,128)(2,1)S(1)}, bf16[4,64,1536]{2,1,0:T(8,128)(2,1)S(1)}, u32[]{:S(2)}, u32[]{:S(2)}) collective-permute-start(bf16[4,64,1536]{2,1,0:T(8,128)(2,1)S(1)} %constant_dynamic-update-slice_fusion.refs_2_), channel_id=1, source_target_pairs={{0,2},{1,3},{2,0},{3,1},{4,6},{5,7},{6,4},{7,5},{8,10},{9,11},{10,... | collective-permute-start | bytes 2359304 | tf_op jit(solution)/shard_map/ppermute | solution.py:603
  88.0 13.9 %collective-permute-start.26 = (bf16[256,1024]{1,0:T(8,128)(2,1)S(1)}, bf16[256,1024]{1,0:T(8,128)(2,1)S(1)}, u32[]{:S(2)}, u32[]{:S(2)}) collective-permute-start(bf16[256,1024]{1,0:T(8,128)(2,1)S(1)} %multiply_convert_fusion.refs_0_), channel_id=1, source_target_pairs={{0,16},{8,24},{16,0},{24,8},{1,17},{9,25},{17,1},{25,9},{2,18},{10... | collective-permute-start | bytes 1572872 | tf_op jit(solution)/shard_map/ppermute | solution.py:600
  127.6 16.0 %collective-permute-start.30 = (bf16[256,1024]{1,0:T(8,128)(2,1)}, bf16[256,1024]{1,0:T(8,128)(2,1)S(1)}, u32[]{:S(2)}, u32[]{:S(2)}) collective-permute-start(bf16[256,1024]{1,0:T(8,128)(2,1)} %get-tuple-element.114), channel_id=1, source_target_pairs={{0,8},{8,0},{16,24},{24,16},{1,9},{9,1},{17,25},{25,17},{2,10},{10... | collective-permute-start | bytes 1572872 | tf_op jit(solution)/shard_map/ppermute | solution.py:600
  129.6 14.0 %collective-permute-start.32 = (bf16[256,1024]{1,0:T(8,128)(2,1)S(1)}, bf16[256,1024]{1,0:T(8,128)(2,1)S(1)}, u32[]{:S(2)}, u32[]{:S(2)}) collective-permute-start(bf16[256,1024]{1,0:T(8,128)(2,1)S(1)} %add.249), channel_id=1, source_target_pairs={{0,16},{8,24},{16,0},{24,8},{1,17},{9,25},{17,1},{25,9},{2,18},{10... | collective-permute-start | bytes 1572872 | tf_op jit(solution)/shard_map/ppermute | solution.py:600
  145.9 15.1 %collective-permute-start.34 = (bf16[256,1024]{1,0:T(8,128)(2,1)}, bf16[256,1024]{1,0:T(8,128)(2,1)}, u32[]{:S(2)}, u32[]{:S(2)}) collective-permute-start(bf16[256,1024]{1,0:T(8,128)(2,1)} %get-tuple-element.185.refs_0_), channel_id=1, source_target_pairs={{0,16},{8,24},{16,0},{24,8},{1,17},{9,25},{17,1},{25,9},{2,18},{10... | collective-permute-start | bytes 1572872 | tf_op jit(solution)/shard_map/ppermute | solution.py:600
  161.0 16.1 %collective-permute-start.41 = (bf16[9,2,16,1024]{3,2,1,0:T(8,128)(2,1)}, bf16[9,2,16,1024]{3,2,1,0:T(8,128)(2,1)}, u32[]{:S(2)}, u32[]{:S(2)}) collective-permute-start(bf16[9,2,16,1024]{3,2,1,0:T(8,128)(2,1)} %get-tuple-element.129), channel_id=1, source_target_pairs={{0,2},{2,4},{4,6},{6,7},{7,5},{5,3},{3,1},{1,0},{8,10},{10,12},{12... | collective-permute-start | bytes 1769480 | tf_op jit(solution)/shard_map/ppermute | solution.py:593
  162.6 15.8 %collective-permute-start.42 = (bf16[9,2,16,1024]{3,2,1,0:T(8,128)(2,1)}, bf16[9,2,16,1024]{3,2,1,0:T(8,128)(2,1)}, u32[]{:S(2)}, u32[]{:S(2)}) collective-permute-start(bf16[9,2,16,1024]{3,2,1,0:T(8,128)(2,1)} %get-tuple-element.134), channel_id=1, source_target_pairs={{2,0},{4,2},{6,4},{7,6},{5,7},{3,5},{1,3},{0,1},{10,8},{12,10},{14... | collective-permute-start | bytes 1769480 | tf_op jit(solution)/shard_map/ppermute | solution.py:597
  180.6 14.8 %collective-permute-start.43 = (bf16[9,2,16,1024]{3,2,1,0:T(8,128)(2,1)S(1)}, bf16[9,2,16,1024]{3,2,1,0:T(8,128)(2,1)S(1)}, u32[]{:S(2)}, u32[]{:S(2)}) collective-permute-start(bf16[9,2,16,1024]{3,2,1,0:T(8,128)(2,1)S(1)} %get-tuple-element.135), channel_id=1, source_target_pairs={{0,2},{2,4},{4,6},{6,7},{7,5},{5,3},{3,1},{1,0},{8,10},{10,12},{12... | collective-permute-start | bytes 1769480 | tf_op jit(solution)/shard_map/ppermute | solution.py:593
  182.3 14.4 %collective-permute-start.44 = (bf16[9,2,16,1024]{3,2,1,0:T(8,128)(2,1)S(1)}, bf16[9,2,16,1024]{3,2,1,0:T(8,128)(2,1)S(1)}, u32[]{:S(2)}, u32[]{:S(2)}) collective-permute-start(bf16[9,2,16,1024]{3,2,1,0:T(8,128)(2,1)S(1)} %get-tuple-element.141), channel_id=1, source_target_pairs={{2,0},{4,2},{6,4},{7,6},{5,7},{3,5},{1,3},{0,1},{10,8},{12,10},{14... | collective-permute-start | bytes 1769480 | tf_op jit(solution)/shard_map/ppermute | solution.py:597
  197.4 15.8 %collective-permute-start.54 = (bf16[9,2,16,1024]{3,2,1,0:T(8,128)(2,1)S(1)}, bf16[9,2,16,1024]{3,2,1,0:T(8,128)(2,1)S(1)}, u32[]{:S(2)}, u32[]{:S(2)}) collective-permute-start(bf16[9,2,16,1024]{3,2,1,0:T(8,128)(2,1)S(1)} %get-tuple-element.142), channel_id=1, source_target_pairs={{0,2},{2,4},{4,6},{6,7},{7,5},{5,3},{3,1},{1,0},{8,10},{10,12},{12... | collective-permute-start | bytes 1769480 | tf_op jit(solution)/shard_map/ppermute | solution.py:593
  199.0 14.3 %collective-permute-start.55 = (bf16[9,2,16,1024]{3,2,1,0:T(8,128)(2,1)S(1)}, bf16[9,2,16,1024]{3,2,1,0:T(8,128)(2,1)S(1)}, u32[]{:S(2)}, u32[]{:S(2)}) collective-permute-start(bf16[9,2,16,1024]{3,2,1,0:T(8,128)(2,1)S(1)} %get-tuple-element.155), channel_id=1, source_target_pairs={{2,0},{4,2},{6,4},{7,6},{5,7},{3,5},{1,3},{0,1},{10,8},{12,10},{14... | collective-permute-start | bytes 1769480 | tf_op jit(solution)/shard_map/ppermute | solution.py:597
  236.3 15.7 %collective-permute-start.39 = (bf16[256,1024]{1,0:T(8,128)(2,1)S(1)}, bf16[256,1024]{1,0:T(8,128)(2,1)S(1)}, u32[]{:S(2)}, u32[]{:S(2)}) collective-permute-start(bf16[256,1024]{1,0:T(8,128)(2,1)S(1)} %get-tuple-element.192), channel_id=1, source_target_pairs={{0,8},{8,0},{16,24},{24,16},{1,9},{9,1},{17,25},{25,17},{2,10},{10... | collective-permute-start | bytes 1572872 | tf_op jit(solution)/shard_map/ppermute | solution.py:600
  252.0 24.1 %collective-permute-start.40 = (bf16[256,1024]{1,0:T(8,128)(2,1)S(1)}, bf16[256,1024]{1,0:T(8,128)(2,1)}, u32[]{:S(2)}, u32[]{:S(2)}) collective-permute-start(bf16[256,1024]{1,0:T(8,128)(2,1)S(1)} %slice_add_fusion.2), channel_id=1, source_target_pairs={{0,16},{8,24},{16,0},{24,8},{1,17},{9,25},{17,1},{25,9},{2,18},{10... | collective-permute-start | bytes 1572872 | tf_op jit(solution)/shard_map/ppermute | solution.py:600
  255.0 14.4 %collective-permute-start.73 = (bf16[9,2,16,1024]{3,2,1,0:T(8,128)(2,1)S(1)}, bf16[9,2,16,1024]{3,2,1,0:T(8,128)(2,1)S(1)}, u32[]{:S(2)}, u32[]{:S(2)}) collective-permute-start(bf16[9,2,16,1024]{3,2,1,0:T(8,128)(2,1)S(1)} %shard_map.274.refs_0_), channel_id=1, source_target_pairs={{2,0},{4,2},{6,4},{7,6},{5,7},{3,5},{1,3},{0,1},{10,8},{12,10},{14... | collective-permute-start | bytes 1769480 | tf_op jit(solution)/shard_map/ppermute | solution.py:597
  259.0 19.1 %collective-permute-start.46 = (bf16[256,1024]{1,0:T(8,128)(2,1)}, bf16[256,1024]{1,0:T(8,128)(2,1)}, u32[]{:S(2)}, u32[]{:S(2)}) collective-permute-start(bf16[256,1024]{1,0:T(8,128)(2,1)} %get-tuple-element.190), channel_id=1, source_target_pairs={{0,8},{8,0},{16,24},{24,16},{1,9},{9,1},{17,25},{25,17},{2,10},{10... | collective-permute-start | bytes 1572872 | tf_op jit(solution)/shard_map/ppermute | solution.py:600
  260.3 15.0 %collective-permute-start.79 = (bf16[9,2,16,1024]{3,2,1,0:T(8,128)(2,1)S(1)}, bf16[9,2,16,1024]{3,2,1,0:T(8,128)(2,1)S(1)}, u32[]{:S(2)}, u32[]{:S(2)}) collective-permute-start(bf16[9,2,16,1024]{3,2,1,0:T(8,128)(2,1)S(1)} %shard_map.274.refs_0_), channel_id=1, source_target_pairs={{0,2},{2,4},{4,6},{6,7},{7,5},{5,3},{3,1},{1,0},{8,10},{10,12},{12... | collective-permute-start | bytes 1769480 | tf_op jit(solution)/shard_map/ppermute | solution.py:593
  273.9 16.3 %collective-permute-start.74 = (bf16[9,2,16,1024]{3,2,1,0:T(8,128)(2,1)S(1)}, bf16[9,2,16,1024]{3,2,1,0:T(8,128)(2,1)S(1)}, u32[]{:S(2)}, u32[]{:S(2)}) collective-permute-start(bf16[9,2,16,1024]{3,2,1,0:T(8,128)(2,1)S(1)} %collective-permute-done.73.refs_2_), channel_id=1, source_target_pairs={{2,0},{4,2},{6,4},{7,6},{5,7},{3,5},{1,3},{0,1},{10,8},{12,10},{14... | collective-permute-start | bytes 1769480 | tf_op jit(solution)/shard_map/ppermute | solution.py:597
  275.3 27.0 %collective-permute-start.80 = (bf16[9,2,16,1024]{3,2,1,0:T(8,128)(2,1)S(1)}, bf16[9,2,16,1024]{3,2,1,0:T(8,128)(2,1)S(1)}, u32[]{:S(2)}, u32[]{:S(2)}) collective-permute-start(bf16[9,2,16,1024]{3,2,1,0:T(8,128)(2,1)S(1)} %collective-permute-done.79.refs_1_), channel_id=1, source_target_pairs={{0,2},{2,4},{4,6},{6,7},{7,5},{5,3},{3,1},{1,0},{8,10},{10,12},{12... | collective-permute-start | bytes 1769480 | tf_op jit(solution)/shard_map/ppermute | solution.py:593
  276.1 21.8 %collective-permute-start.67 = (bf16[4,2,16,1536]{3,2,1,0:T(8,128)(2,1)S(1)}, bf16[4,2,16,1536]{3,2,1,0:T(8,128)(2,1)S(1)}, u32[]{:S(2)}, u32[]{:S(2)}) collective-permute-start(bf16[4,2,16,1536]{3,2,1,0:T(8,128)(2,1)S(1)} %shard_map.279.refs_0_), channel_id=1, source_target_pairs={{0,2},{2,4},{4,6},{6,7},{7,5},{5,3},{3,1},{1,0},{8,10},{10,12},{12... | collective-permute-start | bytes 1179656 | tf_op jit(solution)/shard_map/ppermute | solution.py:593
  278.1 20.4 %collective-permute-start.68 = (bf16[4,2,16,1536]{3,2,1,0:T(8,128)(2,1)S(1)}, bf16[4,2,16,1536]{3,2,1,0:T(8,128)(2,1)S(1)}, u32[]{:S(2)}, u32[]{:S(2)}) collective-permute-start(bf16[4,2,16,1536]{3,2,1,0:T(8,128)(2,1)S(1)} %shard_map.279.refs_0_), channel_id=1, source_target_pairs={{2,0},{4,2},{6,4},{7,6},{5,7},{3,5},{1,3},{0,1},{10,8},{12,10},{14... | collective-permute-start | bytes 1179656 | tf_op jit(solution)/shard_map/ppermute | solution.py:597
  279.4 23.7 %collective-permute-start.47 = (bf16[256,1024]{1,0:T(8,128)(2,1)S(1)}, bf16[256,1024]{1,0:T(8,128)(2,1)S(1)}, u32[]{:S(2)}, u32[]{:S(2)}) collective-permute-start(bf16[256,1024]{1,0:T(8,128)(2,1)S(1)} %slice_add_fusion.1), channel_id=1, source_target_pairs={{0,16},{8,24},{16,0},{24,8},{1,17},{9,25},{17,1},{25,9},{2,18},{10... | collective-permute-start | bytes 1572872 | tf_op jit(solution)/shard_map/ppermute | solution.py:600
  290.1 21.1 %collective-permute-start.75 = (bf16[9,2,16,1024]{3,2,1,0:T(8,128)(2,1)S(1)}, bf16[9,2,16,1024]{3,2,1,0:T(8,128)(2,1)S(1)}, u32[]{:S(2)}, u32[]{:S(2)}) collective-permute-start(bf16[9,2,16,1024]{3,2,1,0:T(8,128)(2,1)S(1)} %collective-permute-done.74.refs_4_), channel_id=1, source_target_pairs={{2,0},{4,2},{6,4},{7,6},{5,7},{3,5},{1,3},{0,1},{10,8},{12,10},{14... | collective-permute-start | bytes 1769480 | tf_op jit(solution)/shard_map/ppermute | solution.py:597
  298.6 21.1 %collective-permute-start.70 = (bf16[4,2,16,1536]{3,2,1,0:T(8,128)(2,1)S(1)}, bf16[4,2,16,1536]{3,2,1,0:T(8,128)(2,1)S(1)}, u32[]{:S(2)}, u32[]{:S(2)}) collective-permute-start(bf16[4,2,16,1536]{3,2,1,0:T(8,128)(2,1)S(1)} %collective-permute-done.68.refs_2_), channel_id=1, source_target_pairs={{2,0},{4,2},{6,4},{7,6},{5,7},{3,5},{1,3},{0,1},{10,8},{12,10},{14... | collective-permute-start | bytes 1179656 | tf_op jit(solution)/shard_map/ppermute | solution.py:597
  302.4 20.2 %collective-permute-start.81 = (bf16[9,2,16,1024]{3,2,1,0:T(8,128)(2,1)S(1)}, bf16[9,2,16,1024]{3,2,1,0:T(8,128)(2,1)S(1)}, u32[]{:S(2)}, u32[]{:S(2)}) collective-permute-start(bf16[9,2,16,1024]{3,2,1,0:T(8,128)(2,1)S(1)} %collective-permute-done.80.refs_3_), channel_id=1, source_target_pairs={{0,2},{2,4},{4,6},{6,7},{7,5},{5,3},{3,1},{1,0},{8,10},{10,12},{12... | collective-permute-start | bytes 1769480 | tf_op jit(solution)/shard_map/ppermute | solution.py:593
  311.2 13.9 %collective-permute-start.76 = (bf16[9,1,16,1024]{3,2,1,0:T(8,128)(2,1)S(1)}, bf16[9,1,16,1024]{3,2,1,0:T(8,128)(2,1)S(1)}, u32[]{:S(2)}, u32[]{:S(2)}) collective-permute-start(bf16[9,1,16,1024]{3,2,1,0:T(8,128)(2,1)S(1)} %slice.167), channel_id=1, source_target_pairs={{2,0},{4,2},{6,4},{7,6},{5,7},{3,5},{1,3},{0,1},{10,8},{12,10},{14... | collective-permute-start | bytes 884744 | tf_op jit(solution)/shard_map/ppermute | solution.py:597
  311.3 19.7 %collective-permute-start.71 = (bf16[4,2,16,1536]{3,2,1,0:T(8,128)(2,1)S(1)}, bf16[4,2,16,1536]{3,2,1,0:T(8,128)(2,1)S(1)}, u32[]{:S(2)}, u32[]{:S(2)}) collective-permute-start(bf16[4,2,16,1536]{3,2,1,0:T(8,128)(2,1)S(1)} %collective-permute-done.69.refs_3_), channel_id=1, source_target_pairs={{0,2},{2,4},{4,6},{6,7},{7,5},{5,3},{3,1},{1,0},{8,10},{10,12},{12... | collective-permute-start | bytes 1179656 | tf_op jit(solution)/shard_map/ppermute | solution.py:593
  322.6 13.7 %collective-permute-start.82 = (bf16[9,1,16,1024]{3,2,1,0:T(8,128)(2,1)S(1)}, bf16[9,1,16,1024]{3,2,1,0:T(8,128)(2,1)S(1)}, u32[]{:S(2)}, u32[]{:S(2)}) collective-permute-start(bf16[9,1,16,1024]{3,2,1,0:T(8,128)(2,1)S(1)} %slice.169), channel_id=1, source_target_pairs={{0,2},{2,4},{4,6},{6,7},{7,5},{5,3},{3,1},{1,0},{8,10},{10,12},{12... | collective-permute-start | bytes 884744 | tf_op jit(solution)/shard_map/ppermute | solution.py:593
  (124 other events, 925.3 us)

commit v5 on v4

--- a/solution.py
+++ b/solution.py
@@ -12,8 +12,9 @@
 theta_base = 1000000.0
 f32 = jnp.float32
 bf16 = jnp.bfloat16
-vmem_bytes = 32 * 1024 * 1024
+vmem_bytes = 24 * 1024 * 1024
 vmem_wide = 42 * 1024 * 1024
+vmem_feed = 48 * 1024 * 1024
 
 
 def dot(left, right):
@@ -51,11 +52,14 @@
 
 
 def pick(refs, held):
-    for k, ref in enumerate(refs):
+    rows = refs[0].shape[0]
+    count = held.shape[0] // rows
+    for k in range(len(refs) // count):
 
         @pl.when(pl.program_id(0) == k)
-        def _(ref=ref):
-            held[...] = ref[...]
+        def _(k=k):
+            for i in range(count):
+                held[i * rows : (i + 1) * rows, :] = refs[k * count + i][...]
 
 
 def project_kernel(
@@ -86,6 +90,10 @@
 
 def fixed_block(rows, columns):
     return pl.BlockSpec((rows, columns), lambda i: (0, 0))
+
+
+def once_block(rows, columns):
+    return pl.BlockSpec((rows, columns), lambda i: (0, 0), pipeline_mode=pl.Buffered(1))
 
 
 def project(tok, gain, weight, cosine, sine, gains, q_heads, k_heads):
@@ -295,9 +303,10 @@
     ).astype(bf16)
     for k, ref in enumerate(norm_grad):
 
-        @pl.when(pl.program_id(0) == k)
-        def _(ref=ref):
-            ref[...] = back_low
+        @pl.when(pl.program_id(0) == k // 2)
+        def _(k=k, ref=ref):
+            rows = ref.shape[0]
+            ref[...] = back_low[(k % 2) * rows : (k % 2 + 1) * rows]
 
     out[...] = dot(hid, down[...]).astype(bf16)
 
@@ -306,22 +315,23 @@
     count = len(norm)
     block, width = norm[0].shape
     total = block * blocks
+    tall = 2 * block
     units = down.shape[0]
     kept = [units, units, units, width, width]
     return pl.pallas_call(
         functools.partial(feed_kernel, count, len(before)),
-        grid=(count,),
-        in_specs=[fixed_block(*weight.shape), fixed_block(*down.shape)]
-        + [fixed_block(block, width)] * (2 * count)
+        grid=(count // 2,),
+        in_specs=[once_block(*weight.shape), once_block(*down.shape)]
+        + [once_block(block, width)] * (2 * count)
         + [pl.BlockSpec(memory_space=pl.ANY)] * len(before),
-        out_specs=[row_block(block, n, first) for n in kept] + [row_block(block, width)]
+        out_specs=[row_block(tall, n, first) for n in kept] + [row_block(tall, width)]
         + [fixed_block(block, width)] * count,
         out_shape=[jax.ShapeDtypeStruct((total, n), bf16) for n in kept]
         + [jax.ShapeDtypeStruct((block * count, width), bf16)]
         + [jax.ShapeDtypeStruct((block, width), bf16)] * count,
-        scratch_shapes=[pltpu.VMEM((block, width), bf16)] * 2,
+        scratch_shapes=[pltpu.VMEM((tall, width), bf16)] * 2,
         input_output_aliases={2 + 2 * count + i: i for i in range(len(before))},
-        compiler_params=params(vmem_wide),
+        compiler_params=params(vmem_feed),
         cost_estimate=cost(
             12 * block * count * down.size, 6 * down.size + block * count * width * 16,
             block * count * units,
@@ -1002,7 +1012,7 @@
             (source, index, 0, wide_all, i, 0)
             for i, (source, index) in enumerate([(0, 0), (1, 0), (2, 0), (2, 1)])
         ]
-        parts = moves.ring_gather(pack([own, near, far], layout, (4, 2, lines, wide_all)), first_last)
+        parts = moves.ring_gather(pack([own, near, far], layout, (4, 2, lines, wide_all)))
         todo = []
         for source, (part, offset, half) in enumerate(parts):
             for h in range(part.shape[1]):

time: 351 us -> 346 us (0.986)
  waiting for transfers between devices: 143 us -> 137 us
    ppermute x16, waiting for transfers between devices: 44.8 us -> 68.6 us  [up(): lax.ppermute(item, 'rep', [(ring[i], ring[(i + 1) % 8]) for i in range(8)])]
    ppermute x16, waiting for transfers between devices: 32.5 us -> 8.85 us  [down(): lax.ppermute(item, 'rep', [(ring[(i + 1) % 8], ring[i]) for i in range(8)])]
    ppermute x7, waiting for transfers between devices: 35.6 us -> 29.8 us  [cross_rep(): return lax.ppermute(item, 'rep', [(i, i ^ mask) for i in range(8)])]
    ppermute x16, starting transfers between devices: 11.8 us -> 16.4 us  [down(): lax.ppermute(item, 'rep', [(ring[(i + 1) % 8], ring[i]) for i in range(8)])]
    unnamed x151 -> x153, local copies, waits for them, and re-layouts: 22 us -> 19.9 us
  transfers between devices with their start and end apart: 83 -> 83, of which waited for: 38 -> 36; matrix products, arithmetic and copies ran while one was open for 11% -> 11% of each run, Pallas kernels for 14% -> 15%
where the time goes in v5:
time: 346 us; the launch traced here: 341 us
  waiting for transfers between devices  137 us (40%)
  Pallas kernels  77.1 us (22%)
  starting transfers between devices  65.3 us (19%)
  local copies, waits for them, and re-layouts  29.1 us (8%)
  other arithmetic  17.1 us (5%)
  matrix products  13 us (4%)
    ppermute x16, waiting for transfers between devices, up(): lax.ppermute(item, 'rep', [(ring[i], ring[(i + 1) % 8]) for i in range(8)])  68.6 us
    ppermute x44, waiting for transfers between devices, swap(): return lax.ppermute(item, 'shard', [(i, i ^ mask) for i in range(4)])  29.9 us
    ppermute x7, waiting for transfers between devices, cross_rep(): return lax.ppermute(item, 'rep', [(i, i ^ mask) for i in range(8)])  29.8 us
    ppermute x44, starting transfers between devices, swap(): return lax.ppermute(item, 'shard', [(i, i ^ mask) for i in range(4)])  22.6 us
    unnamed x153, local copies, waits for them, and re-layouts  19.9 us
    pallas_call x1, Pallas kernels, feed(): pl.pallas_call(functools.partial(feed_kernel, count, len(before)), grid=(...  17.8 us
    ppermute x16, starting transfers between devices, up(): lax.ppermute(item, 'rep', [(ring[i], ring[(i + 1) % 8]) for i in range(8)])  16.8 us
    ppermute x16, starting transfers between devices, down(): lax.ppermute(item, 'rep', [(ring[(i + 1) % 8], ring[i]) for i in range(8)])  16.4 us
  transfers between devices with their start and end apart: 83, of which 36 were waited for; matrix products, arithmetic and copies ran while one was open for 11% of the time, Pallas kernels for 15%

profile of v5, /device:TPU:0, one launch (start us, length us, event | category | flops | bytes accessed | tf_op | source)
XLA Modules:
  0.0 341.0 jit_solution(4916486045702616352)
XLA Ops:
  6.6 3.0 collective-permute-start.1
  28.7 8.9 %collective-permute-done.6.refs_4_ = bf16[2,128,1024]{2,1,0:T(8,128)(2,1)S(1)} collective-permute-done((bf16[2,128,1024]{2,1,0:T(8,128)(2,1)S(1)}, bf16[2,128,1024]{2,1,0:T(8,128)(2,1)S(1)}, u32[]{:S(2)}, u32[]{:S(2)}) %collective-permute-start.6) | collective-permute-done | bytes 524320 | tf_op jit(solution)/shard_map/ppermute | solution.py:613
  40.1 4.4 %collective-permute-done.11.refs_2_ = bf16[2,256,256]{2,1,0:T(8,128)(2,1)S(1)} collective-permute-done((bf16[2,256,256]{2,1,0:T(8,128)(2,1)S(1)}, bf16[2,256,256]{2,1,0:T(8,128)(2,1)S(1)}, u32[]{:S(2)}, u32[]{:S(2)}) %collective-permute-start.11) | collective-permute-done | bytes 262176 | tf_op jit(solution)/shard_map/ppermute | solution.py:610
  56.8 6.5 %shard_map.257 = (bf16[1024,1024]{1,0:T(8,128)(2,1)S(1)}, f32[1024,768]{1,0:T(8,128)}, bf16[1024,768]{1,0:T(8,128)(2,1)S(1)}, bf16[1024,256]{1,0:T(8,128)(2,1)S(1)}) custom-call(f32[1,1024]{1,0:T(1,128)S(1)} %bitcast.146, bf16[1024,1024]{1,0:T(8,128)(2,1)S(1)} %shard_map.256.weight, f32[1024,128]{1,0:T(8,128)S(1)} %get-tuple-element.215.cosine, ...), custom_call_target="tpu_custom_call" | custom-call | flops 2147483648 | bytes 14680064 | tf_op jit(solution)/shard_map/pallas_call | solution.py:106
  64.7 4.4 %shard_map.259 = (f32[1024,512]{1,0:T(8,128)S(1)}, bf16[1024,512]{1,0:T(8,128)(2,1)S(1)}, f32[1024,512]{1,0:T(8,128)S(1)}) custom-call(s32[1]{0:T(128)} %bitcast.1.order, bf16[1024,768]{1,0:T(8,128)(2,1)S(1)} %get-tuple-element.104.query.key, bf16[1024,768]{1,0:T(8,128)(2,1)S(1)} %get-tuple-element.104.query.key, ...), custom_call_target="tpu_custom_call" | custom-call | flops 2147483648 | bytes 6291456 | tf_op jit(solution)/shard_map/pallas_call | solution.py:179
  76.8 5.1 %collective-permute-done.22 = bf16[2,64,1536]{2,1,0:T(8,128)(2,1)S(1)} collective-permute-done((bf16[2,64,1536]{2,1,0:T(8,128)(2,1)}, bf16[2,64,1536]{2,1,0:T(8,128)(2,1)S(1)}, u32[]{:S(2)}, u32[]{:S(2)}) %collective-permute-start.22) | collective-permute-done | bytes 393248 | tf_op jit(solution)/shard_map/ppermute | solution.py:613
  83.6 3.9 %collective-permute-done.20 = bf16[256,1024]{1,0:T(8,128)(2,1)S(1)} collective-permute-done((bf16[256,1024]{1,0:T(8,128)(2,1)S(1)}, bf16[256,1024]{1,0:T(8,128)(2,1)S(1)}, u32[]{:S(2)}, u32[]{:S(2)}) %collective-permute-start.20) | collective-permute-done | bytes 524320 | tf_op jit(solution)/shard_map/ppermute | solution.py:610
  89.6 11.1 %collective-permute-done.23.refs_3_ = bf16[4,64,1536]{2,1,0:T(8,128)(2,1)S(1)} collective-permute-done((bf16[4,64,1536]{2,1,0:T(8,128)(2,1)S(1)}, bf16[4,64,1536]{2,1,0:T(8,128)(2,1)S(1)}, u32[]{:S(2)}, u32[]{:S(2)}) %collective-permute-start.23) | collective-permute-done | bytes 786464 | tf_op jit(solution)/shard_map/ppermute | solution.py:613
  106.4 17.8 %shard_map.262 = (bf16[1024,768]{1,0:T(8,128)(2,1)}, bf16[1024,768]{1,0:T(8,128)(2,1)}, bf16[1024,768]{1,0:T(8,128)(2,1)}, bf16[1024,1024]{1,0:T(8,128)(2,1)}, b...) custom-call(bf16[1024,1536]{1,0:T(8,128)(2,1)} %copy-done.10, ...), custom_call_target="tpu_custom_call" | custom-call | flops 9663676416 | bytes 21495808 | tf_op jit(solution)/shard_map/pallas_call | solution.py:321
  128.7 4.0 %convolution_convert_fusion.1 = bf16[1024,768]{1,0:T(8,128)(2,1)S(1)} fusion(bf16[1024,1024]{1,0:T(8,128)(2,1)} %get-tuple-element.116, bf16[1024,768]{1,0:T(8,128)(2,1)} %get-tuple-element.120), kind=kOutput, calls=%fused_computation.7 | convolution fusion | flops 1611399168 | bytes 5242880 | tf_op jit(solution)/shard_map/dot_general | solution.py:29
  137.9 3.2 collective-permute-done.32
  147.0 6.0 %collective-permute-done.35.refs_6_ = bf16[9,1,16,1024]{3,2,1,0:T(8,128)(2,1)S(1)} collective-permute-done((bf16[9,1,16,1024]{3,2,1,0:T(8,128)(2,1)}, bf16[9,1,16,1024]{3,2,1,0:T(8,128)(2,1)S(1)}, u32[]{:S(2)}, u32[]{:S(2)}) %collective-permute-start.35) | collective-permute-done | bytes 294944 | tf_op jit(solution)/shard_map/ppermute | solution.py:603
  155.8 2.6 shard_map.264
  162.0 3.7 %shard_map.265 = (bf16[1024,512]{1,0:T(8,128)(2,1)S(1)}, bf16[1024,1024]{1,0:T(8,128)(2,1)S(1)}) custom-call(bf16[512,1024]{1,0:T(8,128)(2,1)S(1)} %copy-done.22, bf16[256,1024]{1,0:T(8,128)(2,1)} %get-tuple-element.183.refs_0_, bf16[256,1024]{1,0:T(8,128)(2,1)} %collective-permute-done.33.refs_1_, bf16[256,1024]{1,0:T(8,128)(2,1)} %collective-permute-done.34.refs_2_, ...), custom_call_target="tpu_custom_call" | custom-call | flops 1073741824 | bytes 7340032 | tf_op jit(solution)/shard_map/pallas_call | solution.py:354
  165.7 8.8 %collective-permute-done.41.refs_6_ = bf16[9,2,16,1024]{3,2,1,0:T(8,128)(2,1)} collective-permute-done((bf16[9,2,16,1024]{3,2,1,0:T(8,128)(2,1)}, bf16[9,2,16,1024]{3,2,1,0:T(8,128)(2,1)}, u32[]{:S(2)}, u32[]{:S(2)}) %collective-permute-start.41) | collective-permute-done | bytes 589856 | tf_op jit(solution)/shard_map/ppermute | solution.py:603
  182.4 10.5 %shard_map.267 = (f32[1024,512]{1,0:T(8,128)S(1)}, f32[1024,256]{1,0:T(8,128)S(1)}, f32[1024,256]{1,0:T(8,128)S(1)}) custom-call(s32[1]{0:T(128)} %bitcast.1.order, bf16[1024,768]{1,0:T(8,128)(2,1)S(1)} %copy-done.45, bf16[1024,768]{1,0:T(8,128)(2,1)S(1)} %copy-done.45, bf16[1024,256]{1,0:T(8,128)(2,1)S(1)} %copy-done.51, ...), custom_call_target="tpu_custom_call" | custom-call | flops 5368709120 | bytes 10485760 | tf_op jit(solution)/shard_map/pallas_call | solution.py:252
  197.0 9.5 %shard_map.269 = (bf16[1024,512]{1,0:T(8,128)(2,1)S(1)}, bf16[1024,512]{1,0:T(8,128)(2,1)S(1)}, bf16[1024,1024]{1,0:T(8,128)(2,1)S(1)}, f32[1,1024]{1,0:T(1,128)S(1)}, f32[2,128]{1,0:T(2,128)S(1)}) custom-call(f32[1024,512]{1,0:T(8,128)S(1)} %get-tuple-element.142.query_grad, f32[1024,256]{1,0:T(8,128)S(1)} %get-tuple-element.143.key_grad, ...), custom_call_target="tpu_custom_call" | custom-call | flops 2147483648 | bytes 18874368 | tf_op jit(solution)/shard_map/pallas_call | solution.py:413
  212.2 2.7 collective-permute-done.53.refs_6_
  214.9 4.0 %collective-permute-done.57.refs_7_ = bf16[6,1,16,1024]{3,2,1,0:T(8,128)(2,1)S(1)} collective-permute-done((bf16[6,1,16,1024]{3,2,1,0:T(8,128)(2,1)S(1)}, bf16[6,1,16,1024]{3,2,1,0:T(8,128)(2,1)S(1)}, u32[]{:S(2)}, u32[]{:S(2)}) %collective-permute-start.57) | collective-permute-done | bytes 196640 | tf_op jit(solution)/shard_map/ppermute | solution.py:607
  222.3 5.4 %collective-permute-done.59.refs_2_ = bf16[2,2,16,1536]{3,2,1,0:T(8,128)(2,1)S(1)} collective-permute-done((bf16[2,2,16,1536]{3,2,1,0:T(8,128)(2,1)S(1)}, bf16[2,2,16,1536]{3,2,1,0:T(8,128)(2,1)S(1)}, u32[]{:S(2)}, u32[]{:S(2)}) %collective-permute-start.59) | collective-permute-done | bytes 196640 | tf_op jit(solution)/shard_map/ppermute | solution.py:610
  227.7 2.6 collective-permute-done.58.refs_6_
  234.3 6.7 %collective-permute-done.61.refs_6_ = bf16[6,2,16,1024]{3,2,1,0:T(8,128)(2,1)S(1)} collective-permute-done((bf16[6,2,16,1024]{3,2,1,0:T(8,128)(2,1)S(1)}, bf16[6,2,16,1024]{3,2,1,0:T(8,128)(2,1)S(1)}, u32[]{:S(2)}, u32[]{:S(2)}) %collective-permute-start.61) | collective-permute-done | bytes 393248 | tf_op jit(solution)/shard_map/ppermute | solution.py:603
  245.2 2.8 collective-permute-done.49
  261.1 4.9 %collective-permute-done.66.refs_2_ = bf16[2,2,16,1536]{3,2,1,0:T(8,128)(2,1)S(1)} collective-permute-done((bf16[2,2,16,1536]{3,2,1,0:T(8,128)(2,1)S(1)}, bf16[2,2,16,1536]{3,2,1,0:T(8,128)(2,1)S(1)}, u32[]{:S(2)}, u32[]{:S(2)}) %collective-permute-start.66) | collective-permute-done | bytes 196640 | tf_op jit(solution)/shard_map/ppermute | solution.py:610
  266.1 5.0 %collective-permute-done.75.refs_1_ = bf16[9,2,16,1024]{3,2,1,0:T(8,128)(2,1)S(1)} collective-permute-done((bf16[9,2,16,1024]{3,2,1,0:T(8,128)(2,1)S(1)}, bf16[9,2,16,1024]{3,2,1,0:T(8,128)(2,1)S(1)}, u32[]{:S(2)}, u32[]{:S(2)}) %collective-permute-start.75) | collective-permute-done | bytes 589856 | tf_op jit(solution)/shard_map/ppermute | solution.py:603
  278.2 15.2 %collective-permute-done.67.refs_1_ = bf16[4,2,16,1536]{3,2,1,0:T(8,128)(2,1)S(1)} collective-permute-done((bf16[4,2,16,1536]{3,2,1,0:T(8,128)(2,1)S(1)}, bf16[4,2,16,1536]{3,2,1,0:T(8,128)(2,1)S(1)}, u32[]{:S(2)}, u32[]{:S(2)}) %collective-permute-start.67) | collective-permute-done | bytes 393248 | tf_op jit(solution)/shard_map/ppermute | solution.py:603
  301.3 4.2 %collective-permute-done.69.refs_3_ = bf16[4,2,16,1536]{3,2,1,0:T(8,128)(2,1)S(1)} collective-permute-done((bf16[4,2,16,1536]{3,2,1,0:T(8,128)(2,1)S(1)}, bf16[4,2,16,1536]{3,2,1,0:T(8,128)(2,1)S(1)}, u32[]{:S(2)}, u32[]{:S(2)}) %collective-permute-start.69) | collective-permute-done | bytes 393248 | tf_op jit(solution)/shard_map/ppermute | solution.py:603
  307.5 10.6 %collective-permute-done.79.refs_5_ = bf16[9,2,16,1024]{3,2,1,0:T(8,128)(2,1)S(1)} collective-permute-done((bf16[9,2,16,1024]{3,2,1,0:T(8,128)(2,1)S(1)}, bf16[9,2,16,1024]{3,2,1,0:T(8,128)(2,1)S(1)}, u32[]{:S(2)}, u32[]{:S(2)}) %collective-permute-start.79) | collective-permute-done | bytes 589856 | tf_op jit(solution)/shard_map/ppermute | solution.py:603
  320.3 6.2 %collective-permute-done.71.refs_5_ = bf16[4,2,16,1536]{3,2,1,0:T(8,128)(2,1)S(1)} collective-permute-done((bf16[4,2,16,1536]{3,2,1,0:T(8,128)(2,1)S(1)}, bf16[4,2,16,1536]{3,2,1,0:T(8,128)(2,1)S(1)}, u32[]{:S(2)}, u32[]{:S(2)}) %collective-permute-start.71) | collective-permute-done | bytes 393248 | tf_op jit(solution)/shard_map/ppermute | solution.py:603
  328.7 2.5 fusion.4
  332.0 4.9 %shard_map.281 = (f32[256,3072]{1,0:T(8,128)}, f32[256,3072]{1,0:T(8,128)}, f32[768,1024]{1,0:T(8,128)}) custom-call(s32[4]{0:T(128)S(1)} %pad_add_fusion.scalars, bf16[9,2,16,1024]{3,2,1,0:T(8,128)(2,1)S(1)} %shard_map.274.refs_0_, bf16[9,2,16,1024]{3,2,1,0:T(8,128)(2,1)S(1)} %collective-permute-done.75.refs_1_, ...), custom_call_target="tpu_custom_call" | custom-call | bytes 14155776 | tf_op jit(solution)/shard_map/pallas_call | solution.py:461
  336.9 3.9 %shard_map.280 = (f32[256,2048]{1,0:T(8,128)}, f32[256,1024]{1,0:T(8,128)}, f32[256,1024]{1,0:T(8,128)}, f32[2048,256]{1,0:T(8,128)}) custom-call(s32[4]{0:T(128)S(1)} %pad_add_fusion.scalars, bf16[4,2,16,1536]{3,2,1,0:T(8,128)(2,1)S(1)} %shard_map.279.refs_0_, bf16[4,2,16,1536]{3,2,1,0:T(8,128)(2,1)S(1)} %collective-permute-done.67.refs_1_, ...), custom_call_target="tpu_custom_call" | custom-call | bytes 9437184 | tf_op jit(solution)/shard_map/pallas_call | solution.py:461
  (396 shorter events, 143.9 us)
Async XLA Ops:
  9.6 14.3 %collective-permute-start.4 = (bf16[2,128,1024]{2,1,0:T(8,128)(2,1)S(1)}, bf16[2,128,1024]{2,1,0:T(8,128)(2,1)S(1)}, u32[]{:S(2)}, u32[]{:S(2)}) collective-permute-start(bf16[2,128,1024]{2,1,0:T(8,128)(2,1)S(1)} %get-tuple-element.95), channel_id=1, source_target_pairs={{0,16},{8,24},{16,0},{24,8},{1,17},{9,25},{17,1},{25,9},{2,18},{10... | collective-permute-start | bytes 1572872 | tf_op jit(solution)/shard_map/ppermute | solution.py:610
  9.8 36.8 %collective-permute-start.3 = (bf16[256,1024]{1,0:T(8,128)(2,1)}, bf16[256,1024]{1,0:T(8,128)(2,1)}, u32[]{:S(2)}, u32[]{:S(2)}) collective-permute-start(bf16[256,1024]{1,0:T(8,128)(2,1)} %get-tuple-element.98), channel_id=1, source_target_pairs={{0,8},{8,0},{16,24},{24,16},{1,9},{9,1},{17,25},{25,17},{2,10},{10... | collective-permute-start | bytes 1572872 | tf_op jit(solution)/shard_map/ppermute | solution.py:610
  23.9 13.7 %collective-permute-start.9 = (bf16[256,1024]{1,0:T(8,128)(2,1)S(1)}, bf16[256,1024]{1,0:T(8,128)(2,1)S(1)}, u32[]{:S(2)}, u32[]{:S(2)}) collective-permute-start(bf16[256,1024]{1,0:T(8,128)(2,1)S(1)} %bitcast.134), channel_id=1, source_target_pairs={{0,16},{8,24},{16,0},{24,8},{1,17},{9,25},{17,1},{25,9},{2,18},{10... | collective-permute-start | bytes 1572872 | tf_op jit(solution)/shard_map/ppermute | solution.py:610
  28.7 18.4 %collective-permute-start.5 = (bf16[128,1024]{1,0:T(8,128)(2,1)}, bf16[128,1024]{1,0:T(8,128)(2,1)S(1)}, u32[]{:S(2)}, u32[]{:S(2)}) collective-permute-start(bf16[128,1024]{1,0:T(8,128)(2,1)} %slice_bitcast_fusion.1), channel_id=1, source_target_pairs={{0,8},{8,0},{16,24},{24,16},{1,9},{9,1},{17,25},{25,17},{2,10},{10... | collective-permute-start | bytes 786440 | tf_op jit(solution)/shard_map/ppermute | solution.py:610
  73.1 14.4 %collective-permute-start.20 = (bf16[256,1024]{1,0:T(8,128)(2,1)S(1)}, bf16[256,1024]{1,0:T(8,128)(2,1)S(1)}, u32[]{:S(2)}, u32[]{:S(2)}) collective-permute-start(bf16[256,1024]{1,0:T(8,128)(2,1)S(1)} %slice_add_fusion), channel_id=1, source_target_pairs={{0,16},{8,24},{16,0},{24,8},{1,17},{9,25},{17,1},{25,9},{2,18},{10... | collective-permute-start | bytes 1572872 | tf_op jit(solution)/shard_map/ppermute | solution.py:610
  74.6 26.9 %collective-permute-start.21 = (bf16[256,1536]{1,0:T(8,128)(2,1)S(1)}, bf16[256,1536]{1,0:T(8,128)(2,1)S(1)}, u32[]{:S(2)}, u32[]{:S(2)}) collective-permute-start(bf16[256,1536]{1,0:T(8,128)(2,1)S(1)} %copy-done.41), channel_id=1, source_target_pairs={{0,8},{8,0},{16,24},{24,16},{1,9},{9,1},{17,25},{25,17},{2,10},{10... | collective-permute-start | bytes 2359304 | tf_op jit(solution)/shard_map/ppermute | solution.py:610
  81.9 18.7 %collective-permute-start.23 = (bf16[4,64,1536]{2,1,0:T(8,128)(2,1)S(1)}, bf16[4,64,1536]{2,1,0:T(8,128)(2,1)S(1)}, u32[]{:S(2)}, u32[]{:S(2)}) collective-permute-start(bf16[4,64,1536]{2,1,0:T(8,128)(2,1)S(1)} %constant_dynamic-update-slice_fusion.refs_2_), channel_id=1, source_target_pairs={{0,2},{1,3},{2,0},{3,1},{4,6},{5,7},{6,4},{7,5},{8,10},{9,11},{10,... | collective-permute-start | bytes 2359304 | tf_op jit(solution)/shard_map/ppermute | solution.py:613
  88.0 13.9 %collective-permute-start.26 = (bf16[256,1024]{1,0:T(8,128)(2,1)S(1)}, bf16[256,1024]{1,0:T(8,128)(2,1)S(1)}, u32[]{:S(2)}, u32[]{:S(2)}) collective-permute-start(bf16[256,1024]{1,0:T(8,128)(2,1)S(1)} %multiply_convert_fusion.refs_0_), channel_id=1, source_target_pairs={{0,16},{8,24},{16,0},{24,8},{1,17},{9,25},{17,1},{25,9},{2,18},{10... | collective-permute-start | bytes 1572872 | tf_op jit(solution)/shard_map/ppermute | solution.py:610
  125.1 16.0 %collective-permute-start.30 = (bf16[256,1024]{1,0:T(8,128)(2,1)}, bf16[256,1024]{1,0:T(8,128)(2,1)S(1)}, u32[]{:S(2)}, u32[]{:S(2)}) collective-permute-start(bf16[256,1024]{1,0:T(8,128)(2,1)} %get-tuple-element.113), channel_id=1, source_target_pairs={{0,8},{8,0},{16,24},{24,16},{1,9},{9,1},{17,25},{25,17},{2,10},{10... | collective-permute-start | bytes 1572872 | tf_op jit(solution)/shard_map/ppermute | solution.py:610
  127.1 14.0 %collective-permute-start.32 = (bf16[256,1024]{1,0:T(8,128)(2,1)S(1)}, bf16[256,1024]{1,0:T(8,128)(2,1)S(1)}, u32[]{:S(2)}, u32[]{:S(2)}) collective-permute-start(bf16[256,1024]{1,0:T(8,128)(2,1)S(1)} %add.249), channel_id=1, source_target_pairs={{0,16},{8,24},{16,0},{24,8},{1,17},{9,25},{17,1},{25,9},{2,18},{10... | collective-permute-start | bytes 1572872 | tf_op jit(solution)/shard_map/ppermute | solution.py:610
  143.3 15.1 %collective-permute-start.34 = (bf16[256,1024]{1,0:T(8,128)(2,1)}, bf16[256,1024]{1,0:T(8,128)(2,1)}, u32[]{:S(2)}, u32[]{:S(2)}) collective-permute-start(bf16[256,1024]{1,0:T(8,128)(2,1)} %get-tuple-element.183.refs_0_), channel_id=1, source_target_pairs={{0,16},{8,24},{16,0},{24,8},{1,17},{9,25},{17,1},{25,9},{2,18},{10... | collective-permute-start | bytes 1572872 | tf_op jit(solution)/shard_map/ppermute | solution.py:610
  147.0 13.7 %collective-permute-start.33 = (bf16[256,1024]{1,0:T(8,128)(2,1)}, bf16[256,1024]{1,0:T(8,128)(2,1)}, u32[]{:S(2)}, u32[]{:S(2)}) collective-permute-start(bf16[256,1024]{1,0:T(8,128)(2,1)} %get-tuple-element.183.refs_0_), channel_id=1, source_target_pairs={{0,8},{8,0},{16,24},{24,16},{1,9},{9,1},{17,25},{25,17},{2,10},{10... | collective-permute-start | bytes 1572872 | tf_op jit(solution)/shard_map/ppermute | solution.py:610
  158.4 16.1 %collective-permute-start.41 = (bf16[9,2,16,1024]{3,2,1,0:T(8,128)(2,1)}, bf16[9,2,16,1024]{3,2,1,0:T(8,128)(2,1)}, u32[]{:S(2)}, u32[]{:S(2)}) collective-permute-start(bf16[9,2,16,1024]{3,2,1,0:T(8,128)(2,1)} %get-tuple-element.128), channel_id=1, source_target_pairs={{0,2},{2,4},{4,6},{6,7},{7,5},{5,3},{3,1},{1,0},{8,10},{10,12},{12... | collective-permute-start | bytes 1769480 | tf_op jit(solution)/shard_map/ppermute | solution.py:603
  160.0 15.8 %collective-permute-start.42 = (bf16[9,2,16,1024]{3,2,1,0:T(8,128)(2,1)}, bf16[9,2,16,1024]{3,2,1,0:T(8,128)(2,1)}, u32[]{:S(2)}, u32[]{:S(2)}) collective-permute-start(bf16[9,2,16,1024]{3,2,1,0:T(8,128)(2,1)} %get-tuple-element.133), channel_id=1, source_target_pairs={{2,0},{4,2},{6,4},{7,6},{5,7},{3,5},{1,3},{0,1},{10,8},{12,10},{14... | collective-permute-start | bytes 1769480 | tf_op jit(solution)/shard_map/ppermute | solution.py:607
  178.1 14.8 %collective-permute-start.43 = (bf16[9,2,16,1024]{3,2,1,0:T(8,128)(2,1)S(1)}, bf16[9,2,16,1024]{3,2,1,0:T(8,128)(2,1)S(1)}, u32[]{:S(2)}, u32[]{:S(2)}) collective-permute-start(bf16[9,2,16,1024]{3,2,1,0:T(8,128)(2,1)S(1)} %get-tuple-element.134), channel_id=1, source_target_pairs={{0,2},{2,4},{4,6},{6,7},{7,5},{5,3},{3,1},{1,0},{8,10},{10,12},{12... | collective-permute-start | bytes 1769480 | tf_op jit(solution)/shard_map/ppermute | solution.py:603
  179.7 14.4 %collective-permute-start.44 = (bf16[9,2,16,1024]{3,2,1,0:T(8,128)(2,1)S(1)}, bf16[9,2,16,1024]{3,2,1,0:T(8,128)(2,1)S(1)}, u32[]{:S(2)}, u32[]{:S(2)}) collective-permute-start(bf16[9,2,16,1024]{3,2,1,0:T(8,128)(2,1)S(1)} %get-tuple-element.140), channel_id=1, source_target_pairs={{2,0},{4,2},{6,4},{7,6},{5,7},{3,5},{1,3},{0,1},{10,8},{12,10},{14... | collective-permute-start | bytes 1769480 | tf_op jit(solution)/shard_map/ppermute | solution.py:607
  194.9 15.8 %collective-permute-start.54 = (bf16[9,2,16,1024]{3,2,1,0:T(8,128)(2,1)S(1)}, bf16[9,2,16,1024]{3,2,1,0:T(8,128)(2,1)S(1)}, u32[]{:S(2)}, u32[]{:S(2)}) collective-permute-start(bf16[9,2,16,1024]{3,2,1,0:T(8,128)(2,1)S(1)} %get-tuple-element.141), channel_id=1, source_target_pairs={{0,2},{2,4},{4,6},{6,7},{7,5},{5,3},{3,1},{1,0},{8,10},{10,12},{12... | collective-permute-start | bytes 1769480 | tf_op jit(solution)/shard_map/ppermute | solution.py:603
  196.5 14.3 %collective-permute-start.55 = (bf16[9,2,16,1024]{3,2,1,0:T(8,128)(2,1)S(1)}, bf16[9,2,16,1024]{3,2,1,0:T(8,128)(2,1)S(1)}, u32[]{:S(2)}, u32[]{:S(2)}) collective-permute-start(bf16[9,2,16,1024]{3,2,1,0:T(8,128)(2,1)S(1)} %get-tuple-element.154), channel_id=1, source_target_pairs={{2,0},{4,2},{6,4},{7,6},{5,7},{3,5},{1,3},{0,1},{10,8},{12,10},{14... | collective-permute-start | bytes 1769480 | tf_op jit(solution)/shard_map/ppermute | solution.py:607
  233.7 15.8 %collective-permute-start.39 = (bf16[256,1024]{1,0:T(8,128)(2,1)S(1)}, bf16[256,1024]{1,0:T(8,128)(2,1)S(1)}, u32[]{:S(2)}, u32[]{:S(2)}) collective-permute-start(bf16[256,1024]{1,0:T(8,128)(2,1)S(1)} %get-tuple-element.190), channel_id=1, source_target_pairs={{0,8},{8,0},{16,24},{24,16},{1,9},{9,1},{17,25},{25,17},{2,10},{10... | collective-permute-start | bytes 1572872 | tf_op jit(solution)/shard_map/ppermute | solution.py:610
  250.4 22.7 %collective-permute-start.40 = (bf16[256,1024]{1,0:T(8,128)(2,1)}, bf16[256,1024]{1,0:T(8,128)(2,1)}, u32[]{:S(2)}, u32[]{:S(2)}) collective-permute-start(bf16[256,1024]{1,0:T(8,128)(2,1)} %slice_add_fusion.2), channel_id=1, source_target_pairs={{0,16},{8,24},{16,0},{24,8},{1,17},{9,25},{17,1},{25,9},{2,18},{10... | collective-permute-start | bytes 1572872 | tf_op jit(solution)/shard_map/ppermute | solution.py:610
  254.4 19.6 %collective-permute-start.46 = (bf16[256,1024]{1,0:T(8,128)(2,1)}, bf16[256,1024]{1,0:T(8,128)(2,1)}, u32[]{:S(2)}, u32[]{:S(2)}) collective-permute-start(bf16[256,1024]{1,0:T(8,128)(2,1)} %get-tuple-element.188), channel_id=1, source_target_pairs={{0,8},{8,0},{16,24},{24,16},{1,9},{9,1},{17,25},{25,17},{2,10},{10... | collective-permute-start | bytes 1572872 | tf_op jit(solution)/shard_map/ppermute | solution.py:610
  256.3 14.8 %collective-permute-start.75 = (bf16[9,2,16,1024]{3,2,1,0:T(8,128)(2,1)S(1)}, bf16[9,2,16,1024]{3,2,1,0:T(8,128)(2,1)S(1)}, u32[]{:S(2)}, u32[]{:S(2)}) collective-permute-start(bf16[9,2,16,1024]{3,2,1,0:T(8,128)(2,1)S(1)} %shard_map.274.refs_0_), channel_id=1, source_target_pairs={{0,2},{2,4},{4,6},{6,7},{7,5},{5,3},{3,1},{1,0},{8,10},{10,12},{12... | collective-permute-start | bytes 1769480 | tf_op jit(solution)/shard_map/ppermute | solution.py:603
  257.4 14.6 %collective-permute-start.76 = (bf16[9,2,16,1024]{3,2,1,0:T(8,128)(2,1)S(1)}, bf16[9,2,16,1024]{3,2,1,0:T(8,128)(2,1)S(1)}, u32[]{:S(2)}, u32[]{:S(2)}) collective-permute-start(bf16[9,2,16,1024]{3,2,1,0:T(8,128)(2,1)S(1)} %shard_map.274.refs_0_), channel_id=1, source_target_pairs={{2,0},{4,2},{6,4},{7,6},{5,7},{3,5},{1,3},{0,1},{10,8},{12,10},{14... | collective-permute-start | bytes 1769480 | tf_op jit(solution)/shard_map/ppermute | solution.py:607
  271.1 26.7 %collective-permute-start.77 = (bf16[9,2,16,1024]{3,2,1,0:T(8,128)(2,1)S(1)}, bf16[9,2,16,1024]{3,2,1,0:T(8,128)(2,1)S(1)}, u32[]{:S(2)}, u32[]{:S(2)}) collective-permute-start(bf16[9,2,16,1024]{3,2,1,0:T(8,128)(2,1)S(1)} %collective-permute-done.75.refs_1_), channel_id=1, source_target_pairs={{0,2},{2,4},{4,6},{6,7},{7,5},{5,3},{3,1},{1,0},{8,10},{10,12},{12... | collective-permute-start | bytes 1769480 | tf_op jit(solution)/shard_map/ppermute | solution.py:603
  272.1 26.5 %collective-permute-start.78 = (bf16[9,2,16,1024]{3,2,1,0:T(8,128)(2,1)S(1)}, bf16[9,2,16,1024]{3,2,1,0:T(8,128)(2,1)S(1)}, u32[]{:S(2)}, u32[]{:S(2)}) collective-permute-start(bf16[9,2,16,1024]{3,2,1,0:T(8,128)(2,1)S(1)} %collective-permute-done.76.refs_2_), channel_id=1, source_target_pairs={{2,0},{4,2},{6,4},{7,6},{5,7},{3,5},{1,3},{0,1},{10,8},{12,10},{14... | collective-permute-start | bytes 1769480 | tf_op jit(solution)/shard_map/ppermute | solution.py:607
  273.1 20.3 %collective-permute-start.67 = (bf16[4,2,16,1536]{3,2,1,0:T(8,128)(2,1)S(1)}, bf16[4,2,16,1536]{3,2,1,0:T(8,128)(2,1)S(1)}, u32[]{:S(2)}, u32[]{:S(2)}) collective-permute-start(bf16[4,2,16,1536]{3,2,1,0:T(8,128)(2,1)S(1)} %shard_map.279.refs_0_), channel_id=1, source_target_pairs={{0,2},{2,4},{4,6},{6,7},{7,5},{5,3},{3,1},{1,0},{8,10},{10,12},{12... | collective-permute-start | bytes 1179656 | tf_op jit(solution)/shard_map/ppermute | solution.py:603
  274.1 20.1 %collective-permute-start.68 = (bf16[4,2,16,1536]{3,2,1,0:T(8,128)(2,1)S(1)}, bf16[4,2,16,1536]{3,2,1,0:T(8,128)(2,1)S(1)}, u32[]{:S(2)}, u32[]{:S(2)}) collective-permute-start(bf16[4,2,16,1536]{3,2,1,0:T(8,128)(2,1)S(1)} %shard_map.279.refs_0_), channel_id=1, source_target_pairs={{2,0},{4,2},{6,4},{7,6},{5,7},{3,5},{1,3},{0,1},{10,8},{12,10},{14... | collective-permute-start | bytes 1179656 | tf_op jit(solution)/shard_map/ppermute | solution.py:607
  276.4 23.4 %collective-permute-start.47 = (bf16[256,1024]{1,0:T(8,128)(2,1)S(1)}, bf16[256,1024]{1,0:T(8,128)(2,1)S(1)}, u32[]{:S(2)}, u32[]{:S(2)}) collective-permute-start(bf16[256,1024]{1,0:T(8,128)(2,1)S(1)} %slice_add_fusion.1), channel_id=1, source_target_pairs={{0,16},{8,24},{16,0},{24,8},{1,17},{9,25},{17,1},{25,9},{2,18},{10... | collective-permute-start | bytes 1572872 | tf_op jit(solution)/shard_map/ppermute | solution.py:610
  297.8 20.3 %collective-permute-start.79 = (bf16[9,2,16,1024]{3,2,1,0:T(8,128)(2,1)S(1)}, bf16[9,2,16,1024]{3,2,1,0:T(8,128)(2,1)S(1)}, u32[]{:S(2)}, u32[]{:S(2)}) collective-permute-start(bf16[9,2,16,1024]{3,2,1,0:T(8,128)(2,1)S(1)} %collective-permute-done.77.refs_3_), channel_id=1, source_target_pairs={{0,2},{2,4},{4,6},{6,7},{7,5},{5,3},{3,1},{1,0},{8,10},{10,12},{12... | collective-permute-start | bytes 1769480 | tf_op jit(solution)/shard_map/ppermute | solution.py:603
  298.5 20.4 %collective-permute-start.80 = (bf16[9,2,16,1024]{3,2,1,0:T(8,128)(2,1)S(1)}, bf16[9,2,16,1024]{3,2,1,0:T(8,128)(2,1)S(1)}, u32[]{:S(2)}, u32[]{:S(2)}) collective-permute-start(bf16[9,2,16,1024]{3,2,1,0:T(8,128)(2,1)S(1)} %collective-permute-done.78.refs_4_), channel_id=1, source_target_pairs={{2,0},{4,2},{6,4},{7,6},{5,7},{3,5},{1,3},{0,1},{10,8},{12,10},{14... | collective-permute-start | bytes 1769480 | tf_op jit(solution)/shard_map/ppermute | solution.py:607
  305.5 21.1 %collective-permute-start.71 = (bf16[4,2,16,1536]{3,2,1,0:T(8,128)(2,1)S(1)}, bf16[4,2,16,1536]{3,2,1,0:T(8,128)(2,1)S(1)}, u32[]{:S(2)}, u32[]{:S(2)}) collective-permute-start(bf16[4,2,16,1536]{3,2,1,0:T(8,128)(2,1)S(1)} %collective-permute-done.69.refs_3_), channel_id=1, source_target_pairs={{0,2},{2,4},{4,6},{6,7},{7,5},{5,3},{3,1},{1,0},{8,10},{10,12},{12... | collective-permute-start | bytes 1179656 | tf_op jit(solution)/shard_map/ppermute | solution.py:603
  306.3 21.1 %collective-permute-start.72 = (bf16[4,2,16,1536]{3,2,1,0:T(8,128)(2,1)S(1)}, bf16[4,2,16,1536]{3,2,1,0:T(8,128)(2,1)S(1)}, u32[]{:S(2)}, u32[]{:S(2)}) collective-permute-start(bf16[4,2,16,1536]{3,2,1,0:T(8,128)(2,1)S(1)} %collective-permute-done.70.refs_4_), channel_id=1, source_target_pairs={{2,0},{4,2},{6,4},{7,6},{5,7},{3,5},{1,3},{0,1},{10,8},{12,10},{14... | collective-permute-start | bytes 1179656 | tf_op jit(solution)/shard_map/ppermute | solution.py:607
  (125 other events, 976.2 us)

commit v6 on v5

--- a/solution.py
+++ b/solution.py
@@ -75,7 +75,7 @@
     cos_, sin_ = cosine[...], sine[...]
     for index in range(q_heads + k_heads):
         part = full[:, index * head : (index + 1) * head]
-        lin[:, index * head : (index + 1) * head] = part
+        lin[:, index * head : (index + 1) * head] = part.astype(bf16)
         which = 0 if index < q_heads else 1
         unit = part * inverse_root(part) * gains[which : which + 1, :]
         rot[:, index * head : (index + 1) * head] = (unit * cos_ + half_turn(unit) * sin_).astype(
@@ -117,7 +117,7 @@
         out_specs=[row_block(block, n) for n in (width, qk, qk, kv)],
         out_shape=[
             jax.ShapeDtypeStruct((total, width), bf16),
-            jax.ShapeDtypeStruct((total, qk), f32),
+            jax.ShapeDtypeStruct((total, qk), bf16),
             jax.ShapeDtypeStruct((total, qk), bf16),
             jax.ShapeDtypeStruct((total, kv), bf16),
         ],
@@ -381,7 +381,7 @@
         )
         turned = ref[:, spot * head : (spot + 1) * head]
         grad = turned * cos_ - half_turn(turned) * sin_
-        rows = lin[:, index * head : (index + 1) * head]
+        rows = lin[:, index * head : (index + 1) * head].astype(f32)
         scale = inverse_root(rows)
         sums[which] = sums[which] + jnp.sum(grad * rows * scale, axis=0, keepdims=True)
         result[:, spot * head : (spot + 1) * head] = norm_back(

time: 346 us -> 347 us (level)
    unnamed x153 -> x155, local copies, waits for them, and re-layouts: 19.9 us -> 21.2 us
  transfers between devices with their start and end apart: 83 -> 83, of which waited for: 36 -> 36; matrix products, arithmetic and copies ran while one was open for 11% -> 11% of each run, Pallas kernels for 15% -> 14%
where the time goes in v6:
time: 347 us; the launch traced here: 341 us
  waiting for transfers between devices  137 us (39%)
  Pallas kernels  76.3 us (22%)
  starting transfers between devices  65.5 us (19%)
  local copies, waits for them, and re-layouts  30.3 us (9%)
  other arithmetic  17.1 us (5%)
  matrix products  13 us (4%)
    ppermute x16, waiting for transfers between devices, up(): lax.ppermute(item, 'rep', [(ring[i], ring[(i + 1) % 8]) for i in range(8)])  68.6 us
    ppermute x44, waiting for transfers between devices, swap(): return lax.ppermute(item, 'shard', [(i, i ^ mask) for i in range(4)])  29.9 us
    ppermute x7, waiting for transfers between devices, cross_rep(): return lax.ppermute(item, 'rep', [(i, i ^ mask) for i in range(8)])  29.7 us
    ppermute x44, starting transfers between devices, swap(): return lax.ppermute(item, 'shard', [(i, i ^ mask) for i in range(4)])  22.7 us
    unnamed x155, local copies, waits for them, and re-layouts  21.2 us
    pallas_call x1, Pallas kernels, feed(): pl.pallas_call(functools.partial(feed_kernel, count, len(before)), grid=(...  17.8 us
    ppermute x16, starting transfers between devices, up(): lax.ppermute(item, 'rep', [(ring[i], ring[(i + 1) % 8]) for i in range(8)])  16.8 us
    ppermute x16, starting transfers between devices, down(): lax.ppermute(item, 'rep', [(ring[(i + 1) % 8], ring[i]) for i in range(8)])  16.4 us
  transfers between devices with their start and end apart: 83, of which 36 were waited for; matrix products, arithmetic and copies ran while one was open for 11% of the time, Pallas kernels for 14%

profile of v6, /device:TPU:0, one launch (start us, length us, event | category | flops | bytes accessed | tf_op | source)
XLA Modules:
  0.0 341.4 jit_solution(12853833470588023139)
XLA Ops:
  6.6 3.0 collective-permute-start.1
  28.7 8.9 %collective-permute-done.6.refs_4_ = bf16[2,128,1024]{2,1,0:T(8,128)(2,1)S(1)} collective-permute-done((bf16[2,128,1024]{2,1,0:T(8,128)(2,1)S(1)}, bf16[2,128,1024]{2,1,0:T(8,128)(2,1)S(1)}, u32[]{:S(2)}, u32[]{:S(2)}) %collective-permute-start.6) | collective-permute-done | bytes 524320 | tf_op jit(solution)/shard_map/ppermute | solution.py:613
  40.1 4.4 %collective-permute-done.11.refs_2_ = bf16[2,256,256]{2,1,0:T(8,128)(2,1)S(1)} collective-permute-done((bf16[2,256,256]{2,1,0:T(8,128)(2,1)S(1)}, bf16[2,256,256]{2,1,0:T(8,128)(2,1)S(1)}, u32[]{:S(2)}, u32[]{:S(2)}) %collective-permute-start.11) | collective-permute-done | bytes 262176 | tf_op jit(solution)/shard_map/ppermute | solution.py:610
  56.8 5.7 %shard_map.257 = (bf16[1024,1024]{1,0:T(8,128)(2,1)S(1)}, bf16[1024,768]{1,0:T(8,128)(2,1)S(1)}, bf16[1024,768]{1,0:T(8,128)(2,1)S(1)}, bf16[1024,256]{1,0:T(8,128)(2,1)S(1)}) custom-call(f32[1,1024]{1,0:T(1,128)S(1)} %bitcast.146, bf16[1024,1024]{1,0:T(8,128)(2,1)S(1)} %shard_map.256.weight, f32[1024,128]{1,0:T(8,128)S(1)} %get-tuple-element.215.cosine, ...), custom_call_target="tpu_custom_call" | custom-call | flops 2147483648 | bytes 14680064 | tf_op jit(solution)/shard_map/pallas_call | solution.py:106
  65.2 4.4 %shard_map.259 = (f32[1024,512]{1,0:T(8,128)S(1)}, bf16[1024,512]{1,0:T(8,128)(2,1)S(1)}, f32[1024,512]{1,0:T(8,128)S(1)}) custom-call(s32[1]{0:T(128)} %bitcast.1.order, bf16[1024,768]{1,0:T(8,128)(2,1)S(1)} %get-tuple-element.104.query.key, bf16[1024,768]{1,0:T(8,128)(2,1)S(1)} %get-tuple-element.104.query.key, ...), custom_call_target="tpu_custom_call" | custom-call | flops 2147483648 | bytes 6291456 | tf_op jit(solution)/shard_map/pallas_call | solution.py:179
  77.2 5.1 %collective-permute-done.22 = bf16[2,64,1536]{2,1,0:T(8,128)(2,1)S(1)} collective-permute-done((bf16[2,64,1536]{2,1,0:T(8,128)(2,1)}, bf16[2,64,1536]{2,1,0:T(8,128)(2,1)S(1)}, u32[]{:S(2)}, u32[]{:S(2)}) %collective-permute-start.22) | collective-permute-done | bytes 393248 | tf_op jit(solution)/shard_map/ppermute | solution.py:613
  84.0 3.9 %collective-permute-done.20 = bf16[256,1024]{1,0:T(8,128)(2,1)S(1)} collective-permute-done((bf16[256,1024]{1,0:T(8,128)(2,1)S(1)}, bf16[256,1024]{1,0:T(8,128)(2,1)S(1)}, u32[]{:S(2)}, u32[]{:S(2)}) %collective-permute-start.20) | collective-permute-done | bytes 524320 | tf_op jit(solution)/shard_map/ppermute | solution.py:610
  90.0 11.1 %collective-permute-done.23.refs_3_ = bf16[4,64,1536]{2,1,0:T(8,128)(2,1)S(1)} collective-permute-done((bf16[4,64,1536]{2,1,0:T(8,128)(2,1)S(1)}, bf16[4,64,1536]{2,1,0:T(8,128)(2,1)S(1)}, u32[]{:S(2)}, u32[]{:S(2)}) %collective-permute-start.23) | collective-permute-done | bytes 786464 | tf_op jit(solution)/shard_map/ppermute | solution.py:613
  106.8 17.8 %shard_map.262 = (bf16[1024,768]{1,0:T(8,128)(2,1)}, bf16[1024,768]{1,0:T(8,128)(2,1)}, bf16[1024,768]{1,0:T(8,128)(2,1)}, bf16[1024,1024]{1,0:T(8,128)(2,1)}, b...) custom-call(bf16[1024,1536]{1,0:T(8,128)(2,1)} %copy-done.10, ...), custom_call_target="tpu_custom_call" | custom-call | flops 9663676416 | bytes 21495808 | tf_op jit(solution)/shard_map/pallas_call | solution.py:321
  129.1 4.1 %convolution_convert_fusion.1 = bf16[1024,768]{1,0:T(8,128)(2,1)S(1)} fusion(bf16[1024,1024]{1,0:T(8,128)(2,1)} %get-tuple-element.116, bf16[1024,768]{1,0:T(8,128)(2,1)} %get-tuple-element.120), kind=kOutput, calls=%fused_computation.7 | convolution fusion | flops 1611399168 | bytes 5242880 | tf_op jit(solution)/shard_map/dot_general | solution.py:29
  138.4 3.1 collective-permute-done.32
  147.4 6.0 %collective-permute-done.35.refs_6_ = bf16[9,1,16,1024]{3,2,1,0:T(8,128)(2,1)S(1)} collective-permute-done((bf16[9,1,16,1024]{3,2,1,0:T(8,128)(2,1)}, bf16[9,1,16,1024]{3,2,1,0:T(8,128)(2,1)S(1)}, u32[]{:S(2)}, u32[]{:S(2)}) %collective-permute-start.35) | collective-permute-done | bytes 294944 | tf_op jit(solution)/shard_map/ppermute | solution.py:603
  156.2 2.6 shard_map.264
  162.4 3.7 %shard_map.265 = (bf16[1024,512]{1,0:T(8,128)(2,1)S(1)}, bf16[1024,1024]{1,0:T(8,128)(2,1)S(1)}) custom-call(bf16[512,1024]{1,0:T(8,128)(2,1)S(1)} %copy-done.23, bf16[256,1024]{1,0:T(8,128)(2,1)} %get-tuple-element.183.refs_0_, bf16[256,1024]{1,0:T(8,128)(2,1)} %collective-permute-done.33.refs_1_, bf16[256,1024]{1,0:T(8,128)(2,1)} %collective-permute-done.34.refs_2_, ...), custom_call_target="tpu_custom_call" | custom-call | flops 1073741824 | bytes 7340032 | tf_op jit(solution)/shard_map/pallas_call | solution.py:354
  166.1 8.8 %collective-permute-done.41.refs_6_ = bf16[9,2,16,1024]{3,2,1,0:T(8,128)(2,1)} collective-permute-done((bf16[9,2,16,1024]{3,2,1,0:T(8,128)(2,1)}, bf16[9,2,16,1024]{3,2,1,0:T(8,128)(2,1)}, u32[]{:S(2)}, u32[]{:S(2)}) %collective-permute-start.41) | collective-permute-done | bytes 589856 | tf_op jit(solution)/shard_map/ppermute | solution.py:603
  182.8 10.5 %shard_map.267 = (f32[1024,512]{1,0:T(8,128)S(1)}, f32[1024,256]{1,0:T(8,128)S(1)}, f32[1024,256]{1,0:T(8,128)S(1)}) custom-call(s32[1]{0:T(128)} %bitcast.1.order, bf16[1024,768]{1,0:T(8,128)(2,1)S(1)} %copy-done.46, bf16[1024,768]{1,0:T(8,128)(2,1)S(1)} %copy-done.46, bf16[1024,256]{1,0:T(8,128)(2,1)S(1)} %copy-done.52, ...), custom_call_target="tpu_custom_call" | custom-call | flops 5368709120 | bytes 10485760 | tf_op jit(solution)/shard_map/pallas_call | solution.py:252
  197.4 9.5 %shard_map.269 = (bf16[1024,512]{1,0:T(8,128)(2,1)S(1)}, bf16[1024,512]{1,0:T(8,128)(2,1)S(1)}, bf16[1024,1024]{1,0:T(8,128)(2,1)S(1)}, f32[1,1024]{1,0:T(1,128)S(1)}, f32[2,128]{1,0:T(2,128)S(1)}) custom-call(f32[1024,512]{1,0:T(8,128)S(1)} %get-tuple-element.142.query_grad, f32[1024,256]{1,0:T(8,128)S(1)} %get-tuple-element.143.key_grad, ...), custom_call_target="tpu_custom_call" | custom-call | flops 2147483648 | bytes 18874368 | tf_op jit(solution)/shard_map/pallas_call | solution.py:413
  212.6 2.7 collective-permute-done.53.refs_6_
  215.3 4.0 %collective-permute-done.57.refs_7_ = bf16[6,1,16,1024]{3,2,1,0:T(8,128)(2,1)S(1)} collective-permute-done((bf16[6,1,16,1024]{3,2,1,0:T(8,128)(2,1)S(1)}, bf16[6,1,16,1024]{3,2,1,0:T(8,128)(2,1)S(1)}, u32[]{:S(2)}, u32[]{:S(2)}) %collective-permute-start.57) | collective-permute-done | bytes 196640 | tf_op jit(solution)/shard_map/ppermute | solution.py:607
  222.7 5.3 %collective-permute-done.59.refs_2_ = bf16[2,2,16,1536]{3,2,1,0:T(8,128)(2,1)S(1)} collective-permute-done((bf16[2,2,16,1536]{3,2,1,0:T(8,128)(2,1)S(1)}, bf16[2,2,16,1536]{3,2,1,0:T(8,128)(2,1)S(1)}, u32[]{:S(2)}, u32[]{:S(2)}) %collective-permute-start.59) | collective-permute-done | bytes 196640 | tf_op jit(solution)/shard_map/ppermute | solution.py:610
  228.1 2.6 collective-permute-done.58.refs_6_
  234.6 6.7 %collective-permute-done.61.refs_6_ = bf16[6,2,16,1024]{3,2,1,0:T(8,128)(2,1)S(1)} collective-permute-done((bf16[6,2,16,1024]{3,2,1,0:T(8,128)(2,1)S(1)}, bf16[6,2,16,1024]{3,2,1,0:T(8,128)(2,1)S(1)}, u32[]{:S(2)}, u32[]{:S(2)}) %collective-permute-start.61) | collective-permute-done | bytes 393248 | tf_op jit(solution)/shard_map/ppermute | solution.py:603
  245.6 2.8 collective-permute-done.49
  261.5 4.9 %collective-permute-done.66.refs_2_ = bf16[2,2,16,1536]{3,2,1,0:T(8,128)(2,1)S(1)} collective-permute-done((bf16[2,2,16,1536]{3,2,1,0:T(8,128)(2,1)S(1)}, bf16[2,2,16,1536]{3,2,1,0:T(8,128)(2,1)S(1)}, u32[]{:S(2)}, u32[]{:S(2)}) %collective-permute-start.66) | collective-permute-done | bytes 196640 | tf_op jit(solution)/shard_map/ppermute | solution.py:610
  266.5 5.0 %collective-permute-done.75.refs_1_ = bf16[9,2,16,1024]{3,2,1,0:T(8,128)(2,1)S(1)} collective-permute-done((bf16[9,2,16,1024]{3,2,1,0:T(8,128)(2,1)S(1)}, bf16[9,2,16,1024]{3,2,1,0:T(8,128)(2,1)S(1)}, u32[]{:S(2)}, u32[]{:S(2)}) %collective-permute-start.75) | collective-permute-done | bytes 589856 | tf_op jit(solution)/shard_map/ppermute | solution.py:603
  278.6 15.2 %collective-permute-done.67.refs_1_ = bf16[4,2,16,1536]{3,2,1,0:T(8,128)(2,1)S(1)} collective-permute-done((bf16[4,2,16,1536]{3,2,1,0:T(8,128)(2,1)S(1)}, bf16[4,2,16,1536]{3,2,1,0:T(8,128)(2,1)S(1)}, u32[]{:S(2)}, u32[]{:S(2)}) %collective-permute-start.67) | collective-permute-done | bytes 393248 | tf_op jit(solution)/shard_map/ppermute | solution.py:603
  301.7 4.2 %collective-permute-done.69.refs_3_ = bf16[4,2,16,1536]{3,2,1,0:T(8,128)(2,1)S(1)} collective-permute-done((bf16[4,2,16,1536]{3,2,1,0:T(8,128)(2,1)S(1)}, bf16[4,2,16,1536]{3,2,1,0:T(8,128)(2,1)S(1)}, u32[]{:S(2)}, u32[]{:S(2)}) %collective-permute-start.69) | collective-permute-done | bytes 393248 | tf_op jit(solution)/shard_map/ppermute | solution.py:603
  307.9 10.6 %collective-permute-done.79.refs_5_ = bf16[9,2,16,1024]{3,2,1,0:T(8,128)(2,1)S(1)} collective-permute-done((bf16[9,2,16,1024]{3,2,1,0:T(8,128)(2,1)S(1)}, bf16[9,2,16,1024]{3,2,1,0:T(8,128)(2,1)S(1)}, u32[]{:S(2)}, u32[]{:S(2)}) %collective-permute-start.79) | collective-permute-done | bytes 589856 | tf_op jit(solution)/shard_map/ppermute | solution.py:603
  320.7 6.2 %collective-permute-done.71.refs_5_ = bf16[4,2,16,1536]{3,2,1,0:T(8,128)(2,1)S(1)} collective-permute-done((bf16[4,2,16,1536]{3,2,1,0:T(8,128)(2,1)S(1)}, bf16[4,2,16,1536]{3,2,1,0:T(8,128)(2,1)S(1)}, u32[]{:S(2)}, u32[]{:S(2)}) %collective-permute-start.71) | collective-permute-done | bytes 393248 | tf_op jit(solution)/shard_map/ppermute | solution.py:603
  329.1 2.5 fusion.4
  332.4 4.9 %shard_map.281 = (f32[256,3072]{1,0:T(8,128)}, f32[256,3072]{1,0:T(8,128)}, f32[768,1024]{1,0:T(8,128)}) custom-call(s32[4]{0:T(128)S(1)} %pad_add_fusion.scalars, bf16[9,2,16,1024]{3,2,1,0:T(8,128)(2,1)S(1)} %shard_map.274.refs_0_, bf16[9,2,16,1024]{3,2,1,0:T(8,128)(2,1)S(1)} %collective-permute-done.75.refs_1_, ...), custom_call_target="tpu_custom_call" | custom-call | bytes 14155776 | tf_op jit(solution)/shard_map/pallas_call | solution.py:461
  337.4 3.9 %shard_map.280 = (f32[256,2048]{1,0:T(8,128)}, f32[256,1024]{1,0:T(8,128)}, f32[256,1024]{1,0:T(8,128)}, f32[2048,256]{1,0:T(8,128)}) custom-call(s32[4]{0:T(128)S(1)} %pad_add_fusion.scalars, bf16[4,2,16,1536]{3,2,1,0:T(8,128)(2,1)S(1)} %shard_map.279.refs_0_, bf16[4,2,16,1536]{3,2,1,0:T(8,128)(2,1)S(1)} %collective-permute-done.67.refs_1_, ...), custom_call_target="tpu_custom_call" | custom-call | bytes 9437184 | tf_op jit(solution)/shard_map/pallas_call | solution.py:461
  (398 shorter events, 145.2 us)
Async XLA Ops:
  9.6 14.3 %collective-permute-start.4 = (bf16[2,128,1024]{2,1,0:T(8,128)(2,1)S(1)}, bf16[2,128,1024]{2,1,0:T(8,128)(2,1)S(1)}, u32[]{:S(2)}, u32[]{:S(2)}) collective-permute-start(bf16[2,128,1024]{2,1,0:T(8,128)(2,1)S(1)} %get-tuple-element.95), channel_id=1, source_target_pairs={{0,16},{8,24},{16,0},{24,8},{1,17},{9,25},{17,1},{25,9},{2,18},{10... | collective-permute-start | bytes 1572872 | tf_op jit(solution)/shard_map/ppermute | solution.py:610
  9.8 36.8 %collective-permute-start.3 = (bf16[256,1024]{1,0:T(8,128)(2,1)}, bf16[256,1024]{1,0:T(8,128)(2,1)}, u32[]{:S(2)}, u32[]{:S(2)}) collective-permute-start(bf16[256,1024]{1,0:T(8,128)(2,1)} %get-tuple-element.98), channel_id=1, source_target_pairs={{0,8},{8,0},{16,24},{24,16},{1,9},{9,1},{17,25},{25,17},{2,10},{10... | collective-permute-start | bytes 1572872 | tf_op jit(solution)/shard_map/ppermute | solution.py:610
  23.9 13.7 %collective-permute-start.9 = (bf16[256,1024]{1,0:T(8,128)(2,1)S(1)}, bf16[256,1024]{1,0:T(8,128)(2,1)S(1)}, u32[]{:S(2)}, u32[]{:S(2)}) collective-permute-start(bf16[256,1024]{1,0:T(8,128)(2,1)S(1)} %bitcast.134), channel_id=1, source_target_pairs={{0,16},{8,24},{16,0},{24,8},{1,17},{9,25},{17,1},{25,9},{2,18},{10... | collective-permute-start | bytes 1572872 | tf_op jit(solution)/shard_map/ppermute | solution.py:610
  28.7 18.4 %collective-permute-start.5 = (bf16[128,1024]{1,0:T(8,128)(2,1)}, bf16[128,1024]{1,0:T(8,128)(2,1)S(1)}, u32[]{:S(2)}, u32[]{:S(2)}) collective-permute-start(bf16[128,1024]{1,0:T(8,128)(2,1)} %slice_bitcast_fusion.1), channel_id=1, source_target_pairs={{0,8},{8,0},{16,24},{24,16},{1,9},{9,1},{17,25},{25,17},{2,10},{10... | collective-permute-start | bytes 786440 | tf_op jit(solution)/shard_map/ppermute | solution.py:610
  73.5 14.4 %collective-permute-start.20 = (bf16[256,1024]{1,0:T(8,128)(2,1)S(1)}, bf16[256,1024]{1,0:T(8,128)(2,1)S(1)}, u32[]{:S(2)}, u32[]{:S(2)}) collective-permute-start(bf16[256,1024]{1,0:T(8,128)(2,1)S(1)} %slice_add_fusion), channel_id=1, source_target_pairs={{0,16},{8,24},{16,0},{24,8},{1,17},{9,25},{17,1},{25,9},{2,18},{10... | collective-permute-start | bytes 1572872 | tf_op jit(solution)/shard_map/ppermute | solution.py:610
  75.0 26.9 %collective-permute-start.21 = (bf16[256,1536]{1,0:T(8,128)(2,1)S(1)}, bf16[256,1536]{1,0:T(8,128)(2,1)S(1)}, u32[]{:S(2)}, u32[]{:S(2)}) collective-permute-start(bf16[256,1536]{1,0:T(8,128)(2,1)S(1)} %copy-done.42), channel_id=1, source_target_pairs={{0,8},{8,0},{16,24},{24,16},{1,9},{9,1},{17,25},{25,17},{2,10},{10... | collective-permute-start | bytes 2359304 | tf_op jit(solution)/shard_map/ppermute | solution.py:610
  82.3 18.7 %collective-permute-start.23 = (bf16[4,64,1536]{2,1,0:T(8,128)(2,1)S(1)}, bf16[4,64,1536]{2,1,0:T(8,128)(2,1)S(1)}, u32[]{:S(2)}, u32[]{:S(2)}) collective-permute-start(bf16[4,64,1536]{2,1,0:T(8,128)(2,1)S(1)} %constant_dynamic-update-slice_fusion.refs_2_), channel_id=1, source_target_pairs={{0,2},{1,3},{2,0},{3,1},{4,6},{5,7},{6,4},{7,5},{8,10},{9,11},{10,... | collective-permute-start | bytes 2359304 | tf_op jit(solution)/shard_map/ppermute | solution.py:613
  88.5 13.9 %collective-permute-start.26 = (bf16[256,1024]{1,0:T(8,128)(2,1)S(1)}, bf16[256,1024]{1,0:T(8,128)(2,1)S(1)}, u32[]{:S(2)}, u32[]{:S(2)}) collective-permute-start(bf16[256,1024]{1,0:T(8,128)(2,1)S(1)} %multiply_convert_fusion.refs_0_), channel_id=1, source_target_pairs={{0,16},{8,24},{16,0},{24,8},{1,17},{9,25},{17,1},{25,9},{2,18},{10... | collective-permute-start | bytes 1572872 | tf_op jit(solution)/shard_map/ppermute | solution.py:610
  125.5 16.0 %collective-permute-start.30 = (bf16[256,1024]{1,0:T(8,128)(2,1)}, bf16[256,1024]{1,0:T(8,128)(2,1)S(1)}, u32[]{:S(2)}, u32[]{:S(2)}) collective-permute-start(bf16[256,1024]{1,0:T(8,128)(2,1)} %get-tuple-element.113), channel_id=1, source_target_pairs={{0,8},{8,0},{16,24},{24,16},{1,9},{9,1},{17,25},{25,17},{2,10},{10... | collective-permute-start | bytes 1572872 | tf_op jit(solution)/shard_map/ppermute | solution.py:610
  127.5 14.0 %collective-permute-start.32 = (bf16[256,1024]{1,0:T(8,128)(2,1)S(1)}, bf16[256,1024]{1,0:T(8,128)(2,1)S(1)}, u32[]{:S(2)}, u32[]{:S(2)}) collective-permute-start(bf16[256,1024]{1,0:T(8,128)(2,1)S(1)} %add.249), channel_id=1, source_target_pairs={{0,16},{8,24},{16,0},{24,8},{1,17},{9,25},{17,1},{25,9},{2,18},{10... | collective-permute-start | bytes 1572872 | tf_op jit(solution)/shard_map/ppermute | solution.py:610
  143.8 15.1 %collective-permute-start.34 = (bf16[256,1024]{1,0:T(8,128)(2,1)}, bf16[256,1024]{1,0:T(8,128)(2,1)}, u32[]{:S(2)}, u32[]{:S(2)}) collective-permute-start(bf16[256,1024]{1,0:T(8,128)(2,1)} %get-tuple-element.183.refs_0_), channel_id=1, source_target_pairs={{0,16},{8,24},{16,0},{24,8},{1,17},{9,25},{17,1},{25,9},{2,18},{10... | collective-permute-start | bytes 1572872 | tf_op jit(solution)/shard_map/ppermute | solution.py:610
  147.4 13.7 %collective-permute-start.33 = (bf16[256,1024]{1,0:T(8,128)(2,1)}, bf16[256,1024]{1,0:T(8,128)(2,1)}, u32[]{:S(2)}, u32[]{:S(2)}) collective-permute-start(bf16[256,1024]{1,0:T(8,128)(2,1)} %get-tuple-element.183.refs_0_), channel_id=1, source_target_pairs={{0,8},{8,0},{16,24},{24,16},{1,9},{9,1},{17,25},{25,17},{2,10},{10... | collective-permute-start | bytes 1572872 | tf_op jit(solution)/shard_map/ppermute | solution.py:610
  158.9 16.1 %collective-permute-start.41 = (bf16[9,2,16,1024]{3,2,1,0:T(8,128)(2,1)}, bf16[9,2,16,1024]{3,2,1,0:T(8,128)(2,1)}, u32[]{:S(2)}, u32[]{:S(2)}) collective-permute-start(bf16[9,2,16,1024]{3,2,1,0:T(8,128)(2,1)} %get-tuple-element.128), channel_id=1, source_target_pairs={{0,2},{2,4},{4,6},{6,7},{7,5},{5,3},{3,1},{1,0},{8,10},{10,12},{12... | collective-permute-start | bytes 1769480 | tf_op jit(solution)/shard_map/ppermute | solution.py:603
  160.4 15.8 %collective-permute-start.42 = (bf16[9,2,16,1024]{3,2,1,0:T(8,128)(2,1)}, bf16[9,2,16,1024]{3,2,1,0:T(8,128)(2,1)}, u32[]{:S(2)}, u32[]{:S(2)}) collective-permute-start(bf16[9,2,16,1024]{3,2,1,0:T(8,128)(2,1)} %get-tuple-element.133), channel_id=1, source_target_pairs={{2,0},{4,2},{6,4},{7,6},{5,7},{3,5},{1,3},{0,1},{10,8},{12,10},{14... | collective-permute-start | bytes 1769480 | tf_op jit(solution)/shard_map/ppermute | solution.py:607
  178.5 14.8 %collective-permute-start.43 = (bf16[9,2,16,1024]{3,2,1,0:T(8,128)(2,1)S(1)}, bf16[9,2,16,1024]{3,2,1,0:T(8,128)(2,1)S(1)}, u32[]{:S(2)}, u32[]{:S(2)}) collective-permute-start(bf16[9,2,16,1024]{3,2,1,0:T(8,128)(2,1)S(1)} %get-tuple-element.134), channel_id=1, source_target_pairs={{0,2},{2,4},{4,6},{6,7},{7,5},{5,3},{3,1},{1,0},{8,10},{10,12},{12... | collective-permute-start | bytes 1769480 | tf_op jit(solution)/shard_map/ppermute | solution.py:603
  180.1 14.4 %collective-permute-start.44 = (bf16[9,2,16,1024]{3,2,1,0:T(8,128)(2,1)S(1)}, bf16[9,2,16,1024]{3,2,1,0:T(8,128)(2,1)S(1)}, u32[]{:S(2)}, u32[]{:S(2)}) collective-permute-start(bf16[9,2,16,1024]{3,2,1,0:T(8,128)(2,1)S(1)} %get-tuple-element.140), channel_id=1, source_target_pairs={{2,0},{4,2},{6,4},{7,6},{5,7},{3,5},{1,3},{0,1},{10,8},{12,10},{14... | collective-permute-start | bytes 1769480 | tf_op jit(solution)/shard_map/ppermute | solution.py:607
  195.3 15.8 %collective-permute-start.54 = (bf16[9,2,16,1024]{3,2,1,0:T(8,128)(2,1)S(1)}, bf16[9,2,16,1024]{3,2,1,0:T(8,128)(2,1)S(1)}, u32[]{:S(2)}, u32[]{:S(2)}) collective-permute-start(bf16[9,2,16,1024]{3,2,1,0:T(8,128)(2,1)S(1)} %get-tuple-element.141), channel_id=1, source_target_pairs={{0,2},{2,4},{4,6},{6,7},{7,5},{5,3},{3,1},{1,0},{8,10},{10,12},{12... | collective-permute-start | bytes 1769480 | tf_op jit(solution)/shard_map/ppermute | solution.py:603
  196.9 14.3 %collective-permute-start.55 = (bf16[9,2,16,1024]{3,2,1,0:T(8,128)(2,1)S(1)}, bf16[9,2,16,1024]{3,2,1,0:T(8,128)(2,1)S(1)}, u32[]{:S(2)}, u32[]{:S(2)}) collective-permute-start(bf16[9,2,16,1024]{3,2,1,0:T(8,128)(2,1)S(1)} %get-tuple-element.154), channel_id=1, source_target_pairs={{2,0},{4,2},{6,4},{7,6},{5,7},{3,5},{1,3},{0,1},{10,8},{12,10},{14... | collective-permute-start | bytes 1769480 | tf_op jit(solution)/shard_map/ppermute | solution.py:607
  234.1 15.8 %collective-permute-start.39 = (bf16[256,1024]{1,0:T(8,128)(2,1)S(1)}, bf16[256,1024]{1,0:T(8,128)(2,1)S(1)}, u32[]{:S(2)}, u32[]{:S(2)}) collective-permute-start(bf16[256,1024]{1,0:T(8,128)(2,1)S(1)} %get-tuple-element.190), channel_id=1, source_target_pairs={{0,8},{8,0},{16,24},{24,16},{1,9},{9,1},{17,25},{25,17},{2,10},{10... | collective-permute-start | bytes 1572872 | tf_op jit(solution)/shard_map/ppermute | solution.py:610
  250.8 22.8 %collective-permute-start.40 = (bf16[256,1024]{1,0:T(8,128)(2,1)}, bf16[256,1024]{1,0:T(8,128)(2,1)}, u32[]{:S(2)}, u32[]{:S(2)}) collective-permute-start(bf16[256,1024]{1,0:T(8,128)(2,1)} %slice_add_fusion.2), channel_id=1, source_target_pairs={{0,16},{8,24},{16,0},{24,8},{1,17},{9,25},{17,1},{25,9},{2,18},{10... | collective-permute-start | bytes 1572872 | tf_op jit(solution)/shard_map/ppermute | solution.py:610
  254.8 19.7 %collective-permute-start.46 = (bf16[256,1024]{1,0:T(8,128)(2,1)}, bf16[256,1024]{1,0:T(8,128)(2,1)}, u32[]{:S(2)}, u32[]{:S(2)}) collective-permute-start(bf16[256,1024]{1,0:T(8,128)(2,1)} %get-tuple-element.188), channel_id=1, source_target_pairs={{0,8},{8,0},{16,24},{24,16},{1,9},{9,1},{17,25},{25,17},{2,10},{10... | collective-permute-start | bytes 1572872 | tf_op jit(solution)/shard_map/ppermute | solution.py:610
  256.7 14.8 %collective-permute-start.75 = (bf16[9,2,16,1024]{3,2,1,0:T(8,128)(2,1)S(1)}, bf16[9,2,16,1024]{3,2,1,0:T(8,128)(2,1)S(1)}, u32[]{:S(2)}, u32[]{:S(2)}) collective-permute-start(bf16[9,2,16,1024]{3,2,1,0:T(8,128)(2,1)S(1)} %shard_map.274.refs_0_), channel_id=1, source_target_pairs={{0,2},{2,4},{4,6},{6,7},{7,5},{5,3},{3,1},{1,0},{8,10},{10,12},{12... | collective-permute-start | bytes 1769480 | tf_op jit(solution)/shard_map/ppermute | solution.py:603
  257.9 14.6 %collective-permute-start.76 = (bf16[9,2,16,1024]{3,2,1,0:T(8,128)(2,1)S(1)}, bf16[9,2,16,1024]{3,2,1,0:T(8,128)(2,1)S(1)}, u32[]{:S(2)}, u32[]{:S(2)}) collective-permute-start(bf16[9,2,16,1024]{3,2,1,0:T(8,128)(2,1)S(1)} %shard_map.274.refs_0_), channel_id=1, source_target_pairs={{2,0},{4,2},{6,4},{7,6},{5,7},{3,5},{1,3},{0,1},{10,8},{12,10},{14... | collective-permute-start | bytes 1769480 | tf_op jit(solution)/shard_map/ppermute | solution.py:607
  271.5 26.7 %collective-permute-start.77 = (bf16[9,2,16,1024]{3,2,1,0:T(8,128)(2,1)S(1)}, bf16[9,2,16,1024]{3,2,1,0:T(8,128)(2,1)S(1)}, u32[]{:S(2)}, u32[]{:S(2)}) collective-permute-start(bf16[9,2,16,1024]{3,2,1,0:T(8,128)(2,1)S(1)} %collective-permute-done.75.refs_1_), channel_id=1, source_target_pairs={{0,2},{2,4},{4,6},{6,7},{7,5},{5,3},{3,1},{1,0},{8,10},{10,12},{12... | collective-permute-start | bytes 1769480 | tf_op jit(solution)/shard_map/ppermute | solution.py:603
  272.5 26.5 %collective-permute-start.78 = (bf16[9,2,16,1024]{3,2,1,0:T(8,128)(2,1)S(1)}, bf16[9,2,16,1024]{3,2,1,0:T(8,128)(2,1)S(1)}, u32[]{:S(2)}, u32[]{:S(2)}) collective-permute-start(bf16[9,2,16,1024]{3,2,1,0:T(8,128)(2,1)S(1)} %collective-permute-done.76.refs_2_), channel_id=1, source_target_pairs={{2,0},{4,2},{6,4},{7,6},{5,7},{3,5},{1,3},{0,1},{10,8},{12,10},{14... | collective-permute-start | bytes 1769480 | tf_op jit(solution)/shard_map/ppermute | solution.py:607
  273.5 20.3 %collective-permute-start.67 = (bf16[4,2,16,1536]{3,2,1,0:T(8,128)(2,1)S(1)}, bf16[4,2,16,1536]{3,2,1,0:T(8,128)(2,1)S(1)}, u32[]{:S(2)}, u32[]{:S(2)}) collective-permute-start(bf16[4,2,16,1536]{3,2,1,0:T(8,128)(2,1)S(1)} %shard_map.279.refs_0_), channel_id=1, source_target_pairs={{0,2},{2,4},{4,6},{6,7},{7,5},{5,3},{3,1},{1,0},{8,10},{10,12},{12... | collective-permute-start | bytes 1179656 | tf_op jit(solution)/shard_map/ppermute | solution.py:603
  274.5 20.1 %collective-permute-start.68 = (bf16[4,2,16,1536]{3,2,1,0:T(8,128)(2,1)S(1)}, bf16[4,2,16,1536]{3,2,1,0:T(8,128)(2,1)S(1)}, u32[]{:S(2)}, u32[]{:S(2)}) collective-permute-start(bf16[4,2,16,1536]{3,2,1,0:T(8,128)(2,1)S(1)} %shard_map.279.refs_0_), channel_id=1, source_target_pairs={{2,0},{4,2},{6,4},{7,6},{5,7},{3,5},{1,3},{0,1},{10,8},{12,10},{14... | collective-permute-start | bytes 1179656 | tf_op jit(solution)/shard_map/ppermute | solution.py:607
  276.8 23.4 %collective-permute-start.47 = (bf16[256,1024]{1,0:T(8,128)(2,1)S(1)}, bf16[256,1024]{1,0:T(8,128)(2,1)S(1)}, u32[]{:S(2)}, u32[]{:S(2)}) collective-permute-start(bf16[256,1024]{1,0:T(8,128)(2,1)S(1)} %slice_add_fusion.1), channel_id=1, source_target_pairs={{0,16},{8,24},{16,0},{24,8},{1,17},{9,25},{17,1},{25,9},{2,18},{10... | collective-permute-start | bytes 1572872 | tf_op jit(solution)/shard_map/ppermute | solution.py:610
  298.2 20.3 %collective-permute-start.79 = (bf16[9,2,16,1024]{3,2,1,0:T(8,128)(2,1)S(1)}, bf16[9,2,16,1024]{3,2,1,0:T(8,128)(2,1)S(1)}, u32[]{:S(2)}, u32[]{:S(2)}) collective-permute-start(bf16[9,2,16,1024]{3,2,1,0:T(8,128)(2,1)S(1)} %collective-permute-done.77.refs_3_), channel_id=1, source_target_pairs={{0,2},{2,4},{4,6},{6,7},{7,5},{5,3},{3,1},{1,0},{8,10},{10,12},{12... | collective-permute-start | bytes 1769480 | tf_op jit(solution)/shard_map/ppermute | solution.py:603
  299.0 20.4 %collective-permute-start.80 = (bf16[9,2,16,1024]{3,2,1,0:T(8,128)(2,1)S(1)}, bf16[9,2,16,1024]{3,2,1,0:T(8,128)(2,1)S(1)}, u32[]{:S(2)}, u32[]{:S(2)}) collective-permute-start(bf16[9,2,16,1024]{3,2,1,0:T(8,128)(2,1)S(1)} %collective-permute-done.78.refs_4_), channel_id=1, source_target_pairs={{2,0},{4,2},{6,4},{7,6},{5,7},{3,5},{1,3},{0,1},{10,8},{12,10},{14... | collective-permute-start | bytes 1769480 | tf_op jit(solution)/shard_map/ppermute | solution.py:607
  305.9 21.1 %collective-permute-start.71 = (bf16[4,2,16,1536]{3,2,1,0:T(8,128)(2,1)S(1)}, bf16[4,2,16,1536]{3,2,1,0:T(8,128)(2,1)S(1)}, u32[]{:S(2)}, u32[]{:S(2)}) collective-permute-start(bf16[4,2,16,1536]{3,2,1,0:T(8,128)(2,1)S(1)} %collective-permute-done.69.refs_3_), channel_id=1, source_target_pairs={{0,2},{2,4},{4,6},{6,7},{7,5},{5,3},{3,1},{1,0},{8,10},{10,12},{12... | collective-permute-start | bytes 1179656 | tf_op jit(solution)/shard_map/ppermute | solution.py:603
  306.7 21.1 %collective-permute-start.72 = (bf16[4,2,16,1536]{3,2,1,0:T(8,128)(2,1)S(1)}, bf16[4,2,16,1536]{3,2,1,0:T(8,128)(2,1)S(1)}, u32[]{:S(2)}, u32[]{:S(2)}) collective-permute-start(bf16[4,2,16,1536]{3,2,1,0:T(8,128)(2,1)S(1)} %collective-permute-done.70.refs_4_), channel_id=1, source_target_pairs={{2,0},{4,2},{6,4},{7,6},{5,7},{3,5},{1,3},{0,1},{10,8},{12,10},{14... | collective-permute-start | bytes 1179656 | tf_op jit(solution)/shard_map/ppermute | solution.py:607
  (126 other events, 979.5 us)
